TPU v7x, 256 devices: a whole 4x4x8 slice. The times are simulated.
256 devices in a mesh: island: 8 (over z_lo, core), fsdp: 32 (over z_hi, y, x).
Axes of the slice: x: 4, y: 4, z: 8 (z_hi: 2, z_lo: 4; z = z_hi * 4 + z_lo), core: 2. Of those that a mesh axis runs over, the one named last changes fastest.
Arguments:
- activations: bfloat16 [8, 32768, 5120], P('island', 'fsdp'), may hold values from -6 to 6
- upstream: bfloat16 [8, 32768, 384], P('island', 'fsdp'), may hold values from -0.0625 to 0.0625
- drift: float32 [8, 384, 5120], P('island', 'fsdp'), may hold values from -0.75 to 0.75
- first_moment: float32 [8, 384, 5120], P('island', 'fsdp'), may hold values from -4 to 4
- second_moment: float32 [8, 384, 5120], P('island', 'fsdp'), may hold values from 0.01 to 1
- outer_base: float32 [384, 5120], P('fsdp'), may hold values from -0.3 to 0.3
- outer_momentum: float32 [384, 5120], P('fsdp'), may hold values from -0.75 to 0.75
- scale_exponents: int32 [384, 40], P('fsdp'), may hold values from -12 to -5
Outputs:
- first_new: float32 [8, 384, 5120], P('island', 'fsdp')
- second_new: float32 [8, 384, 5120], P('island', 'fsdp')
- momentum_new: float32 [384, 5120], P('fsdp', 'island')
- base_new: float32 [384, 5120], P('fsdp', 'island')
- fragment: bfloat16 [384, 5120], replicated
All inputs are finite; a program needn't handle non-finite values.
Results may differ from a plain program's by a relative error of at most 0.015.
Values may be sent and summed in bfloat16 or wider, within the bound.
No kernel may reach another device: no remote copies, remote signals or barrier semaphores. Data moves between devices by JAX's collectives and lax.ppermute only.
A program may use at most 64 MiB of HBM per device.

v0:
```python
import jax
import jax.numpy as jnp
from jax import lax
from jax.sharding import PartitionSpec as P

INNER_RATE = 0.02
OUTER_RATE = 0.7
BETA_FIRST = 0.9
BETA_SECOND = 0.95
CORRECT_FIRST = 1.0 - 0.9**10
CORRECT_SECOND = 1.0 - 0.95**10
WEIGHT_DECAY = 0.1
EPSILON = 1e-08
NESTEROV_MU = 0.9


def outer_step(summed, unscale, momentum_old, base_old, islands):
    pseudo = summed * unscale / islands
    momentum_next = NESTEROV_MU * momentum_old + pseudo
    base_next = base_old - OUTER_RATE * (pseudo + NESTEROV_MU * momentum_next)
    return (momentum_next, base_next)


def local(
    activations,
    upstream,
    drift,
    first_moment,
    second_moment,
    outer_base,
    outer_momentum,
    scale_exponents,
):
    features = activations[0]
    upstream_rows = upstream[0]
    width = outer_base.shape[1]
    whole_term = lax.dot_general(
        upstream_rows, features, (((0,), (0,)), ((), ())), preferred_element_type=jnp.float32
    )
    gradient = lax.psum_scatter(
        whole_term.astype(jnp.bfloat16), "fsdp", scatter_dimension=0, tiled=True
    ).astype(jnp.float32)
    params = outer_base + drift[0]
    first_new = BETA_FIRST * first_moment[0] + (1.0 - BETA_FIRST) * gradient
    second_new = BETA_SECOND * second_moment[0] + (1.0 - BETA_SECOND) * gradient * gradient
    update = (
        first_new / CORRECT_FIRST / (jnp.sqrt(second_new / CORRECT_SECOND) + EPSILON)
        + WEIGHT_DECAY * params
    )
    inner = params - INNER_RATE * update
    delta = outer_base - inner
    block_size = width // scale_exponents.shape[1]
    exponent_f = jnp.repeat(scale_exponents, block_size, axis=1).astype(jnp.float32)
    scaling = jnp.exp2(-exponent_f)
    unscale = jnp.exp2(exponent_f)
    coded = jnp.clip(delta * scaling, -127.0, 127.0)
    islands = lax.axis_size("island")
    share_width = width // islands
    island_pos = lax.axis_index("island")
    summed = lax.psum(coded.astype(jnp.bfloat16), "island").astype(jnp.float32)
    momentum_next, base_next = outer_step(summed, unscale, outer_momentum, outer_base, islands)
    fragment = lax.all_gather(base_next.astype(jnp.bfloat16), "fsdp", axis=0, tiled=True)
    momentum_out = lax.dynamic_slice_in_dim(momentum_next, island_pos * share_width, share_width, 1)
    base_out = lax.dynamic_slice_in_dim(base_next, island_pos * share_width, share_width, 1)
    return (first_new[None], second_new[None], momentum_out, base_out, fragment)


def solution(mesh):
    in_specs = (
        P("island", "fsdp", None),
        P("island", "fsdp", None),
        P("island", "fsdp", None),
        P("island", "fsdp", None),
        P("island", "fsdp", None),
        P("fsdp", None),
        P("fsdp", None),
        P("fsdp", None),
    )
    out_specs = (
        P("island", "fsdp", None),
        P("island", "fsdp", None),
        P("fsdp", "island"),
        P("fsdp", "island"),
        P(),
    )
    return jax.shard_map(local, mesh=mesh, in_specs=in_specs, out_specs=out_specs, check_vma=False)
```

profile of v0, /device:TPU:1, one launch (start us, length us, event | category | flops | bytes accessed | tf_op | source)
XLA Modules:
  0.0 458.5 jit_solution(17435760016340023965)
XLA Ops:
  7.2 0.0 copy-start
  7.2 0.0 copy-start.8
  7.2 0.0 all-reduce.4.cloned.1.call-start
  7.2 1.1 copy-done
  8.3 9.8 %fusion.3 = bf16[384,5120]{1,0:T(8,128)(2,1)} fusion(bf16[1,1024,5120]{2,1,0:T(8,128)(2,1)} %param.8, bf16[1,1024,384]{2,1,0:T(8,128)(2,1)S(1)} %copy-done), kind=kOutput, calls=%fused_computation.2 | convolution fusion | flops 4028497920 | bytes 15204352 | tf_op jit(solution)/shard_map/dot_general | solution.py:37
  18.1 0.0 copy-start.9
  18.1 0.0 copy-start.1
  18.1 167.6 %fusion = bf16[16,5120]{1,0:T(8,128)(2,1)S(1)} fusion(bf16[384,5120]{1,0:T(8,128)(2,1)} %fusion.3), kind=kCustom, calls=%all-reduce-scatter | all-reduce-scatter fusion | flops 2621441 | bytes 4097024
  185.7 1.3 collective-permute-start.6
  187.0 1.3 collective-permute-start.5
  188.4 1.3 collective-permute-start.7
  189.7 1.3 collective-permute-start.4
  191.0 7.8 %collective-permute-start.3 = (bf16[16,5120]{1,0:T(8,128)(2,1)S(1)}, bf16[16,5120]{1,0:T(8,128)(2,1)S(1)}, u32[]{:S(2)}, u32[]{:S(2)}) collective-permute-start(bf16[16,5120]{1,0:T(8,128)(2,1)S(1)} %fusion), channel_id=1, source_target_pairs={{0,4},{1,5},{2,6},{3,7},{4,8},{5,9},{6,10},{7,11},{8,12},{9,13},{1... | collective-permute-start | bytes 491528
  198.8 0.0 collective-permute-done.7
  198.9 0.0 copy-start.3
  198.9 4.2 collective-permute-start.2
  203.1 0.0 collective-permute-done.6
  203.1 2.8 collective-permute-start.1
  206.0 0.0 collective-permute-done.5
  206.0 0.0 copy-start.2
  206.0 8.9 %collective-permute-start = (bf16[16,5120]{1,0:T(8,128)(2,1)S(1)}, bf16[16,5120]{1,0:T(8,128)(2,1)}, u32[]{:S(2)}, u32[]{:S(2)}) collective-permute-start(bf16[16,5120]{1,0:T(8,128)(2,1)S(1)} %fusion), channel_id=1, source_target_pairs={{0,1},{1,2},{2,3},{3,4},{4,5},{5,6},{6,7},{7,8},{8,9},{9,10},{10,1... | collective-permute-start | bytes 491528
  214.9 0.0 copy-done.8
  214.9 0.0 copy-done.3
  214.9 0.0 copy-done.2
  214.9 0.1 broadcast_in_dim.13
  215.0 0.1 copy.26
  215.1 0.0 copy-done.9
  215.1 0.6 dynamic-slice.4
  216.4 0.0 collective-permute-done.4
  216.4 0.0 copy-start.4
  216.4 0.0 collective-permute-done.3
  216.4 0.0 copy-start.5
  216.4 0.0 collective-permute-done.2
  216.4 0.0 copy-start.6
  216.4 0.0 collective-permute-done.1
  216.4 0.6 copy-done.4
  217.0 0.0 copy-done.5
  217.1 0.1 copy-done.6
  217.2 0.0 copy-start.7
  217.2 0.7 copy-done.7
  217.8 0.0 collective-permute-done
  217.8 13.1 %concatenate = bf16[140,5120]{1,0:T(8,128)(2,1)S(1)} concatenate(bf16[12,5120]{1,0:T(8,128)(2,1)} %copy-done.3, bf16[16,5120]{1,0:T(8,128)(2,1)S(1)} %collective-permute-done.6, bf16[16,5120]{1,0:T(8,128)(2,1)} %copy-done.2, bf16[16,5120]{1,0:T(8,128)(2,1)} %copy-done.4, bf16[16,5120]{1,0:T(8,128)(2,1)} %copy-done.5, bf16[16,5120]{1,0:T(8,128)(2,1)} %copy-done.6, ...), dimensions={0} | concatenate | bytes 2867200
  230.9 0.0 copy-done.1
  230.9 2.2 clamp_convert_fusion
  233.1 0.0 all-reduce.4.cloned.1.call-update
  233.1 0.0 all-gather.3.cloned.1.call-start
  233.2 0.1 broadcast_in_dim.14
  233.4 0.1 copy.27
  233.4 84.1 %all-reduce.4.cloned.1.call-done = bf16[12,5120]{1,0:T(8,128)(2,1)} async-done(((bf16[12,5120]{1,0:T(8,128)(2,1)}), bf16[12,5120]{1,0:T(8,128)(2,1)}) %all-reduce.4.cloned.1.call-update) | async-done | bytes 122896 | tf_op jit(solution)/shard_map/psum | solution.py:60
  317.6 1.9 convert_bitcast_fusion
  319.5 0.0 all-gather.3.cloned.1.call-update
  319.5 0.9 copy.23
  320.4 0.9 copy.24
  321.4 0.6 constant_dynamic-slice_fusion
  322.0 122.7 %all-gather.3.cloned.1.call-done = bf16[32,12,5120]{2,1,0:T(8,128)(2,1)} async-done(((bf16[1,12,5120]{2,1,0:T(8,128)(2,1)}), bf16[32,12,5120]{2,1,0:T(8,128)(2,1)}) %all-gather.3.cloned.1.call-update) | async-done | bytes 3932176 | tf_op jit(solution)/shard_map/all_gather | solution.py:62
  444.7 7.0 %reshape.24 = bf16[384,5120]{1,0:T(8,128)(2,1)} reshape(bf16[32,12,5120]{2,1,0:T(8,128)(2,1)} %all-gather.3.cloned.1.call-done) | data formatting | bytes 7864320
  (4 shorter events, 0.1 us)
Async XLA Ops:
  7.2 1.1 copy-start
  7.2 207.7 %copy-start.8 = (s32[12,40]{1,0:T(8,128)S(1)}, s32[12,40]{1,0:T(8,128)}, u32[]{:S(2)}) copy-start(s32[12,40]{1,0:T(8,128)} %param.15) | copy-start | bytes 5764
  7.2 310.4 %all-reduce.4.cloned.1.call-start = ((), (), s32[]{:S(2)}) async-start(), calls=%async_computation | async-start | bytes 327680 | tf_op jit(solution)/shard_map/psum | solution.py:60
  18.1 197.0 %copy-start.9 = (u32[256]{0:T(256)S(1)}, u32[256]{0:T(256)}, u32[]{:S(2)}) copy-start(u32[256]{0:T(256)} %constant.51) | copy-start | bytes 3076
  18.1 212.8 %copy-start.1 = (f32[1,12,5120]{2,0,1:T(1,128)S(1)}, f32[1,12,5120]{2,0,1:T(1,128)}, u32[]{:S(2)}) copy-start(f32[1,12,5120]{2,0,1:T(1,128)} %param.10) | copy-start | bytes 737284
  185.7 17.4 %collective-permute-start.6 = (bf16[16,5120]{1,0:T(8,128)(2,1)S(1)}, bf16[16,5120]{1,0:T(8,128)(2,1)S(1)}, u32[]{:S(2)}, u32[]{:S(2)}) collective-permute-start(bf16[16,5120]{1,0:T(8,128)(2,1)S(1)} %fusion), channel_id=1, source_target_pairs={{0,7},{1,8},{2,9},{3,10},{4,11},{5,12},{6,13},{7,14},{8,15},{9,16}... | collective-permute-start | bytes 491528
  187.0 18.9 %collective-permute-start.5 = (bf16[16,5120]{1,0:T(8,128)(2,1)S(1)}, bf16[16,5120]{1,0:T(8,128)(2,1)S(1)}, u32[]{:S(2)}, u32[]{:S(2)}) collective-permute-start(bf16[16,5120]{1,0:T(8,128)(2,1)S(1)} %fusion), channel_id=1, source_target_pairs={{0,6},{1,7},{2,8},{3,9},{4,10},{5,11},{6,12},{7,13},{8,14},{9,15},... | collective-permute-start | bytes 491528
  188.4 10.4 %collective-permute-start.7 = (bf16[12,5120]{1,0:T(8,128)(2,1)S(1)}, bf16[12,5120]{1,0:T(8,128)(2,1)S(1)}, u32[]{:S(2)}, u32[]{:S(2)}) collective-permute-start(bf16[12,5120]{1,0:T(8,128)(2,1)S(1)} %slice), channel_id=1, source_target_pairs={{0,8},{1,9},{2,10},{3,11},{4,12},{5,13},{6,14},{7,15},{8,16},{9,17... | collective-permute-start | bytes 368648
  189.7 26.7 %collective-permute-start.4 = (bf16[16,5120]{1,0:T(8,128)(2,1)S(1)}, bf16[16,5120]{1,0:T(8,128)(2,1)S(1)}, u32[]{:S(2)}, u32[]{:S(2)}) collective-permute-start(bf16[16,5120]{1,0:T(8,128)(2,1)S(1)} %fusion), channel_id=1, source_target_pairs={{0,5},{1,6},{2,7},{3,8},{4,9},{5,10},{6,11},{7,12},{8,13},{9,14},{... | collective-permute-start | bytes 491528
  191.0 25.4 %collective-permute-start.3 = (bf16[16,5120]{1,0:T(8,128)(2,1)S(1)}, bf16[16,5120]{1,0:T(8,128)(2,1)S(1)}, u32[]{:S(2)}, u32[]{:S(2)}) collective-permute-start(bf16[16,5120]{1,0:T(8,128)(2,1)S(1)} %fusion), channel_id=1, source_target_pairs={{0,4},{1,5},{2,6},{3,7},{4,8},{5,9},{6,10},{7,11},{8,12},{9,13},{1... | collective-permute-start | bytes 491528
  198.9 16.0 %copy-start.3 = (bf16[12,5120]{1,0:T(8,128)(2,1)}, bf16[12,5120]{1,0:T(8,128)(2,1)S(1)}, u32[]{:S(2)}) copy-start(bf16[12,5120]{1,0:T(8,128)(2,1)S(1)} %collective-permute-done.7) | copy-start | bytes 368644
  198.9 17.6 %collective-permute-start.2 = (bf16[16,5120]{1,0:T(8,128)(2,1)S(1)}, bf16[16,5120]{1,0:T(8,128)(2,1)S(1)}, u32[]{:S(2)}, u32[]{:S(2)}) collective-permute-start(bf16[16,5120]{1,0:T(8,128)(2,1)S(1)} %fusion), channel_id=1, source_target_pairs={{0,3},{1,4},{2,5},{3,6},{4,7},{5,8},{6,9},{7,10},{8,11},{9,12},{10... | collective-permute-start | bytes 491528
  203.1 13.3 %collective-permute-start.1 = (bf16[16,5120]{1,0:T(8,128)(2,1)S(1)}, bf16[16,5120]{1,0:T(8,128)(2,1)S(1)}, u32[]{:S(2)}, u32[]{:S(2)}) collective-permute-start(bf16[16,5120]{1,0:T(8,128)(2,1)S(1)} %fusion), channel_id=1, source_target_pairs={{0,2},{1,3},{2,4},{3,5},{4,6},{5,7},{6,8},{7,9},{8,10},{9,11},{10,... | collective-permute-start | bytes 491528
  206.0 8.9 %copy-start.2 = (bf16[16,5120]{1,0:T(8,128)(2,1)}, bf16[16,5120]{1,0:T(8,128)(2,1)S(1)}, u32[]{:S(2)}) copy-start(bf16[16,5120]{1,0:T(8,128)(2,1)S(1)} %collective-permute-done.5) | copy-start | bytes 491524
  206.0 11.8 %collective-permute-start = (bf16[16,5120]{1,0:T(8,128)(2,1)S(1)}, bf16[16,5120]{1,0:T(8,128)(2,1)}, u32[]{:S(2)}, u32[]{:S(2)}) collective-permute-start(bf16[16,5120]{1,0:T(8,128)(2,1)S(1)} %fusion), channel_id=1, source_target_pairs={{0,1},{1,2},{2,3},{3,4},{4,5},{5,6},{6,7},{7,8},{8,9},{9,10},{10,1... | collective-permute-start | bytes 491528
  216.4 0.7 copy-start.4
  216.4 0.7 copy-start.5
  216.4 0.7 copy-start.6
  217.2 0.7 copy-start.7
  233.1 211.5 %all-gather.3.cloned.1.call-start = ((), (), s32[]{:S(2)}) async-start(), calls=%async_computation.1 | async-start | bytes 5406720 | tf_op jit(solution)/shard_map/all_gather | solution.py:62
Sparse Core Ops, SparseCore 0:
  233.3 84.2 all-reduce.3
  322.1 122.5 all-gather.2
where the time goes:
time: 460 us; the launch traced here: 459 us
  waiting for transfers between devices  207 us (45%)
  blocking collectives  168 us (37%)
  starting transfers between devices  29 us (6%)
  local copies, waits for them, and re-layouts  26.1 us (6%)
  between operations  15 us (3%)
  matrix products  9.8 us (2%)
    unnamed x1, blocking collectives  168 us
    all_gather x1, waiting for transfers between devices, local(): lax.all_gather(base_next.astype(jnp.bfloat16), 'fsdp', axis=0, tiled=True)  123 us
    psum x1, waiting for transfers between devices, local(): summed = lax.psum(coded.astype(jnp.bfloat16), 'island').astype(jnp.float32)  84.1 us
    unnamed x8, starting transfers between devices  29 us
    unnamed x30, local copies, waits for them, and re-layouts  25.3 us
    dot_general x1, matrix products, local(): lax.dot_general(upstream_rows, features, (((0,), (0,)), ((), ())), prefer...  9.8 us
  transfers between devices with their start and end apart: 10, of which 2 were waited for; matrix products, arithmetic and copies ran while one was open for 1% of the time, Pallas kernels for 0%

commit v1 on v0

v1 whole, which is shorter than its diff:
```python
import functools

import jax
import jax.numpy as jnp
import numpy as np
from jax import lax
from jax.experimental import pallas as pl
from jax.experimental.pallas import tpu as pltpu
from jax.sharding import PartitionSpec as P

INNER_RATE = 0.02
OUTER_RATE = 0.7
BETA_FIRST = 0.9
BETA_SECOND = 0.95
CORRECT_FIRST = 1.0 - 0.9**10
CORRECT_SECOND = 1.0 - 0.95**10
WEIGHT_DECAY = 0.1
EPSILON = 1e-08
NESTEROV_MU = 0.9

N_ISLAND = 8
N_FSDP = 32
N_ZLO = 4
RING = 4
OWN = 12
ROWS = 384
QUARTER = ROWS // 4
PAIR = 2 * OWN
BLOCK = 128
MIB = 1 << 20
BF16 = jnp.bfloat16
F32 = jnp.float32
AXES = ("island", "fsdp")


def device_pairs(target):
    pairs = []
    for zlo in range(N_ZLO):
        for core in range(2):
            for zhi in range(2):
                for y in range(RING):
                    for x in range(RING):
                        here = (zlo, core, zhi, y, x)
                        pairs.append((device_id(*here), device_id(*target(*here))))
    return pairs


def device_id(zlo, core, zhi, y, x):
    return (zlo * 2 + core) * N_FSDP + (zhi * RING + y) * RING + x


def along_a(step):
    def target(zlo, core, zhi, y, x):
        if core == 0:
            return (zlo, core, zhi, y, (x + step) % RING)
        return (zlo, core, zhi, (y + step) % RING, x)

    return device_pairs(target)


def along_b(step):
    def target(zlo, core, zhi, y, x):
        if core == 0:
            return (zlo, core, zhi, (y + step) % RING, x)
        return (zlo, core, zhi, y, (x + step) % RING)

    return device_pairs(target)


OTHER_ZHI = device_pairs(lambda zlo, core, zhi, y, x: (zlo, core, 1 - zhi, y, x))
OTHER_CORE = device_pairs(lambda zlo, core, zhi, y, x: (zlo, 1 - core, zhi, y, x))


def other_zlo(k):
    return device_pairs(lambda zlo, core, zhi, y, x: (zlo ^ k, core, zhi, y, x))


def send(value, pairs):
    return lax.ppermute(value, AXES, pairs)


def fragment_row(position, core, zhi, y, x):
    position = position.astype(F32)
    ja = jnp.floor((position + 0.5) / QUARTER)
    rest = position - QUARTER * ja
    jb = jnp.floor((rest + 0.5) / PAIR)
    rest = rest - PAIR * jb
    jz = jnp.floor((rest + 0.5) / OWN)
    r = rest - OWN * jz
    first = jnp.where(core == 0, ja, jb)
    second = jnp.where(core == 0, jb, ja)
    col = x.astype(F32) + first
    col = jnp.where(col >= RING, col - RING, col)
    line = y.astype(F32) + second
    line = jnp.where(line >= RING, line - RING, line)
    half = jnp.where(zhi == 0, jz, 1.0 - jz)
    return ((half * RING + line) * RING + col) * OWN + r


def product_kernel(pos, up_ref, act_ref, *rest):
    outs, up_rows = rest[:4], rest[4]

    @pl.when(pl.program_id(0) == 0)
    def _():
        _, core, zhi, y, x = (pos[i] for i in range(5))
        wanted = fragment_row(lax.broadcasted_iota(jnp.int32, (ROWS, 1), 0), core, zhi, y, x)
        column = lax.broadcasted_iota(jnp.int32, (ROWS, ROWS), 1).astype(F32)
        pick = jnp.where(column == wanted, 1.0, 0.0).astype(BF16)
        up_rows[...] = lax.dot_general(
            pick, up_ref[...], (((1,), (1,)), ((), ())), preferred_element_type=F32
        ).astype(BF16)

    total = jnp.dot(up_rows[...], act_ref[...], preferred_element_type=F32).astype(BF16)
    for j in range(4):
        outs[j][...] = total[j * QUARTER : (j + 1) * QUARTER]


def product(pos, upstream, activations, first_col, width, tile):
    tokens = activations.shape[1]
    skip = first_col // tile
    return pl.pallas_call(
        product_kernel,
        grid_spec=pltpu.PrefetchScalarGridSpec(
            num_scalar_prefetch=1,
            grid=(width // tile,),
            in_specs=[
                pl.BlockSpec((None, tokens, ROWS), lambda t, p: (0, 0, 0)),
                pl.BlockSpec((None, tokens, tile), lambda t, p: (0, 0, t + skip)),
            ],
            out_specs=[pl.BlockSpec((QUARTER, tile), lambda t, p: (0, t))] * 4,
            scratch_shapes=[pltpu.VMEM((ROWS, tokens), BF16)],
        ),
        out_shape=[jax.ShapeDtypeStruct((QUARTER, width), BF16)] * 4,
        compiler_params=pltpu.CompilerParams(vmem_limit_bytes=32 * MIB),
        cost_estimate=pl.CostEstimate(
            flops=2 * ROWS * tokens * width,
            bytes_accessed=2 * tokens * (width + ROWS) + 2 * ROWS * width,
            transcendentals=0,
        ),
        name="product",
    )(pos, upstream, activations)


def add_first_kernel(own, one, two, three, *outs):
    total = (own[...].astype(F32) + one[...].astype(F32)) + (
        two[...].astype(F32) + three[...].astype(F32)
    )
    for j in range(4):
        outs[j][...] = total[j * PAIR : (j + 1) * PAIR].astype(BF16)


def add_first(parts, tile):
    width = parts[0].shape[1]
    return pl.pallas_call(
        add_first_kernel,
        grid=(width // tile,),
        in_specs=[pl.BlockSpec((QUARTER, tile), lambda t: (0, t))] * 4,
        out_specs=[pl.BlockSpec((PAIR, tile), lambda t: (0, t))] * 4,
        out_shape=[jax.ShapeDtypeStruct((PAIR, width), BF16)] * 4,
        compiler_params=pltpu.CompilerParams(vmem_limit_bytes=32 * MIB),
        name="add_first",
    )(*parts)


def add_second_kernel(own, one, two, three, keep, away):
    total = (own[...].astype(F32) + one[...].astype(F32)) + (
        two[...].astype(F32) + three[...].astype(F32)
    )
    keep[...] = total[:OWN]
    blank = jnp.zeros((16 - OWN, total.shape[1]), F32)
    away[...] = jnp.concatenate([total[OWN:], blank], axis=0).astype(BF16)


def add_second(parts):
    width = parts[0].shape[1]
    return pl.pallas_call(
        add_second_kernel,
        out_shape=[
            jax.ShapeDtypeStruct((OWN, width), F32),
            jax.ShapeDtypeStruct((16, width), BF16),
        ],
        compiler_params=pltpu.CompilerParams(vmem_limit_bytes=32 * MIB),
        name="add_second",
    )(*parts)


def inner_kernel(pos, keep, arrived, drift, first, second, base, exponents, first_out, second_out, own, away, unscale_out):
    core = pos[1]
    width = keep.shape[1]
    share = width // N_ISLAND
    exponent = exponents[...].astype(F32)
    scaling_all = jnp.exp2(-exponent)
    unscale_all = jnp.exp2(exponent)
    per_share = share // BLOCK
    blank = jnp.zeros((16 - OWN, share), F32)
    for i in range(N_ISLAND):
        cols = slice(i * share, (i + 1) * share)
        gradient = keep[:, cols] + arrived[:OWN, cols].astype(F32)
        base_now = base[:, cols]
        params = base_now + drift[:, cols]
        first_new = BETA_FIRST * first[:, cols] + (1.0 - BETA_FIRST) * gradient
        second_new = BETA_SECOND * second[:, cols] + (1.0 - BETA_SECOND) * gradient * gradient
        first_out[:, cols] = first_new
        second_out[:, cols] = second_new
        update = (
            first_new / CORRECT_FIRST / (jnp.sqrt(second_new / CORRECT_SECOND) + EPSILON)
            + WEIGHT_DECAY * params
        )
        inner = params - INNER_RATE * update
        delta = base_now - inner
        blocks = range(i * per_share, (i + 1) * per_share)
        scaling = jnp.concatenate(
            [jnp.broadcast_to(scaling_all[:, b : b + 1], (OWN, BLOCK)) for b in blocks], axis=1
        )
        unscale = jnp.concatenate(
            [jnp.broadcast_to(unscale_all[:, b : b + 1], (OWN, BLOCK)) for b in blocks], axis=1
        )
        coded = jnp.clip(delta * scaling, -127.0, 127.0)
        coded = jnp.concatenate([coded, blank], axis=0).astype(BF16)
        place = slice((i // 2) * share, (i // 2 + 1) * share)

        @pl.when(core == i % 2)
        def _():
            own[:, place] = coded
            unscale_out[:, place] = unscale

        @pl.when(core != i % 2)
        def _():
            away[:, place] = coded


def inner_step(pos, keep, arrived, drift, first, second, base, exponents):
    width = keep.shape[1]
    rows = pl.BlockSpec((None, OWN, width), lambda t, p: (0, 0, 0))

    def whole(a):
        return pl.BlockSpec(a.shape, lambda t, p: (0, 0))

    outs = [
        jax.ShapeDtypeStruct((1, OWN, width), F32),
        jax.ShapeDtypeStruct((1, OWN, width), F32),
        jax.ShapeDtypeStruct((16, width // 2), BF16),
        jax.ShapeDtypeStruct((16, width // 2), BF16),
        jax.ShapeDtypeStruct((OWN, width // 2), F32),
    ]
    return pl.pallas_call(
        inner_kernel,
        grid_spec=pltpu.PrefetchScalarGridSpec(
            num_scalar_prefetch=1,
            grid=(1,),
            in_specs=[whole(keep), whole(arrived), rows, rows, rows, whole(base), whole(exponents)],
            out_specs=[rows, rows] + [whole(o) for o in outs[2:]],
        ),
        out_shape=outs,
        compiler_params=pltpu.CompilerParams(vmem_limit_bytes=32 * MIB),
        name="inner_step",
    )(pos, keep, arrived, drift, first, second, base, exponents)


def add_cores_kernel(own, arrived, out):
    out[...] = (own[...].astype(F32) + arrived[...].astype(F32)).astype(BF16)


def add_cores(own, arrived):
    return pl.pallas_call(
        add_cores_kernel,
        out_shape=jax.ShapeDtypeStruct(own.shape, BF16),
        name="add_cores",
    )(own, arrived)


def outer_kernel(pos, own, one, two, three, unscale, momentum, base, momentum_out, base_out, fragment):
    zlo, core = pos[0], pos[1]
    share = own.shape[1] // N_ZLO
    blank = jnp.zeros((16 - OWN, share), F32)
    for k in range(N_ZLO):
        place = slice(k * share, (k + 1) * share)
        cols = pl.ds(pl.multiple_of((2 * k + core) * share, BLOCK), share)
        summed = (own[:OWN, place].astype(F32) + one[:OWN, place].astype(F32)) + (
            two[:OWN, place].astype(F32) + three[:OWN, place].astype(F32)
        )
        pseudo = summed * unscale[:, place] / N_ISLAND
        momentum_next = NESTEROV_MU * momentum[:, cols] + pseudo
        base_next = base[:, cols] - OUTER_RATE * (pseudo + NESTEROV_MU * momentum_next)
        fragment[:, place] = jnp.concatenate([base_next, blank], axis=0).astype(BF16)

        @pl.when(zlo == k)
        def _():
            momentum_out[...] = momentum_next
            base_out[...] = base_next


def outer_step(pos, parts, unscale, momentum, base):
    width = base.shape[1]
    args = (*parts, unscale, momentum, base)

    def whole(a):
        return pl.BlockSpec(a.shape, lambda t, p: (0, 0))

    outs = [
        jax.ShapeDtypeStruct((OWN, width // N_ISLAND), F32),
        jax.ShapeDtypeStruct((OWN, width // N_ISLAND), F32),
        jax.ShapeDtypeStruct((16, width // 2), BF16),
    ]
    return pl.pallas_call(
        outer_kernel,
        grid_spec=pltpu.PrefetchScalarGridSpec(
            num_scalar_prefetch=1,
            grid=(1,),
            in_specs=[whole(a) for a in args],
            out_specs=[whole(o) for o in outs],
        ),
        out_shape=outs,
        compiler_params=pltpu.CompilerParams(vmem_limit_bytes=32 * MIB),
        name="outer_step",
    )(pos, *args)


def join_pair_kernel(own, arrived, out):
    out[...] = jnp.concatenate(
        [own[:OWN].astype(F32), arrived[:OWN].astype(F32)], axis=0
    ).astype(BF16)


def join_pair(own, arrived):
    return pl.pallas_call(
        join_pair_kernel,
        out_shape=jax.ShapeDtypeStruct((PAIR, own.shape[1]), BF16),
        name="join_pair",
    )(own, arrived)


def join_four_kernel(*refs):
    out = refs[4]
    out[...] = jnp.concatenate([r[...].astype(F32) for r in refs[:4]], axis=0).astype(BF16)


def join_four(parts):
    return pl.pallas_call(
        join_four_kernel,
        out_shape=jax.ShapeDtypeStruct((QUARTER, parts[0].shape[1]), BF16),
        name="join_four",
    )(*parts)


def place_kernel(pos, *refs):
    mine, theirs, out, order = refs[:4], refs[4:8], refs[8], refs[9]
    which = pl.program_id(1)

    @pl.when((pl.program_id(0) == 0) & (which == 0))
    def _():
        _, core, zhi, y, x = (pos[i] for i in range(5))
        position = lax.broadcasted_iota(jnp.int32, (1, ROWS), 1)
        row = lax.broadcasted_iota(jnp.int32, (ROWS, ROWS), 0).astype(F32)
        for w in range(2):
            wanted = fragment_row(position, core if w == 0 else 1 - core, zhi, y, x)
            order[w] = jnp.where(row == wanted, 1.0, 0.0).astype(BF16)

    for w, parts in enumerate((mine, theirs)):

        @pl.when(which == w)
        def _():
            rows = jnp.concatenate([p[...] for p in parts], axis=0)
            out[...] = jnp.dot(order[w], rows, preferred_element_type=F32).astype(BF16)


def place(pos, mine, theirs):
    half = mine[0].shape[1]
    share = half // N_ZLO
    part = pl.BlockSpec((QUARTER, share), lambda k, w, p: (0, k))
    return pl.pallas_call(
        place_kernel,
        grid_spec=pltpu.PrefetchScalarGridSpec(
            num_scalar_prefetch=1,
            grid=(N_ZLO, 2),
            in_specs=[part] * 8,
            out_specs=pl.BlockSpec(
                (ROWS, share), lambda k, w, p: (0, 2 * k + jnp.where(w == 0, p[1], 1 - p[1]))
            ),
            scratch_shapes=[pltpu.VMEM((2, ROWS, ROWS), BF16)],
        ),
        out_shape=jax.ShapeDtypeStruct((ROWS, 2 * half), BF16),
        compiler_params=pltpu.CompilerParams(vmem_limit_bytes=32 * MIB),
        name="place",
    )(pos, *mine, *theirs)


def local(activations, upstream, drift, first_moment, second_moment, outer_base, outer_momentum, scale_exponents):
    island = lax.axis_index("island")
    fsdp = lax.axis_index("fsdp")
    pos = jnp.stack([island // 2, island % 2, fsdp // 16, (fsdp // RING) % RING, fsdp % RING]).astype(jnp.int32)
    width = outer_base.shape[1]

    chunks = product(pos, upstream, activations, 0, width, 512)
    arrived = [send(chunks[j], along_a(j)) for j in (2, 1, 3)]
    chunks = add_first([chunks[0], *arrived], 1024)
    arrived = [send(chunks[j], along_b(j)) for j in (2, 1, 3)]
    keep, away = add_second([chunks[0], *arrived])
    arrived = send(away, OTHER_ZHI)

    first_new, second_new, own, away, unscale = inner_step(
        pos, keep, arrived, drift, first_moment, second_moment, outer_base, scale_exponents
    )
    coded = add_cores(own, send(away, OTHER_CORE))
    parts = [coded] + [send(coded, other_zlo(k)) for k in (1, 2, 3)]
    momentum_out, base_out, piece = outer_step(pos, parts, unscale, outer_momentum, outer_base)

    piece = join_pair(piece, send(piece, OTHER_ZHI))
    piece = join_four([piece] + [send(piece, along_b(-j)) for j in (1, 2, 3)])
    mine = [piece] + [send(piece, along_a(-j)) for j in (1, 2, 3)]
    theirs = [send(m, OTHER_CORE) for m in mine]
    fragment = place(pos, mine, theirs)
    return (first_new, second_new, momentum_out, base_out, fragment)


def solution(mesh):
    in_specs = (
        P("island", "fsdp", None),
        P("island", "fsdp", None),
        P("island", "fsdp", None),
        P("island", "fsdp", None),
        P("island", "fsdp", None),
        P("fsdp", None),
        P("fsdp", None),
        P("fsdp", None),
    )
    out_specs = (
        P("island", "fsdp", None),
        P("island", "fsdp", None),
        P("fsdp", "island"),
        P("fsdp", "island"),
        P(),
    )
    return jax.shard_map(local, mesh=mesh, in_specs=in_specs, out_specs=out_specs, check_vma=False)
```

time: 460 us -> 134 us (0.29)
  blocking collectives: 168 us -> 0 us
  waiting for transfers between devices: 207 us -> 45.1 us
  Pallas kernels: 0 us -> 23.5 us
  starting transfers between devices: 29 us -> 51.8 us
  between operations: 15 us -> 0.82 us
  local copies, waits for them, and re-layouts: 26.1 us -> 12 us
  matrix products: 9.8 us -> 0 us
    unnamed x1 -> x0, blocking collectives: 168 us -> none
    all_gather x1 -> x0, waiting for transfers between devices: 123 us -> none  [local(): lax.all_gather(base_next.astype(jnp.bfloat16), 'fsdp', axis=0, tiled=True)]
    psum x1 -> x0, waiting for transfers between devices: 84.1 us -> none  [local(): summed = lax.psum(coded.astype(jnp.bfloat16), 'island').astype(jnp.float32)]
    ppermute x0 -> x22, starting transfers between devices: none -> 51.8 us  [send(): return lax.ppermute(value, AXES, pairs)]
    ppermute x0 -> x22, waiting for transfers between devices: none -> 45.1 us  [send(): return lax.ppermute(value, AXES, pairs)]
    unnamed x8 -> x0, starting transfers between devices: 29 us -> none
    pallas_call x0 -> x9, Pallas kernels: none -> 23.5 us  [the longest x1 8.1 us: product(): pl.pallas_call(product_kernel, grid_spec=pltpu.PrefetchScalarGridSpec(num...]
    unnamed x30 -> x39, local copies, waits for them, and re-layouts: 25.3 us -> 11.9 us
  transfers between devices with their start and end apart: 10 -> 22, of which waited for: 2 -> 17; matrix products, arithmetic and copies ran while one was open for 1% -> 2% of each run, Pallas kernels for 0% -> 0%
where the time goes in v1:
time: 134 us; the launch traced here: 133 us
  starting transfers between devices  51.8 us (39%)
  waiting for transfers between devices  45.1 us (34%)
  Pallas kernels  23.5 us (18%)
  local copies, waits for them, and re-layouts  12 us (9%)
    ppermute x22, starting transfers between devices, send(): return lax.ppermute(value, AXES, pairs)  51.8 us
    ppermute x22, waiting for transfers between devices, send(): return lax.ppermute(value, AXES, pairs)  45.1 us
    unnamed x39, local copies, waits for them, and re-layouts  11.9 us
    pallas_call x1, Pallas kernels, product(): pl.pallas_call(product_kernel, grid_spec=pltpu.PrefetchScalarGridSpec(num...  8.1 us
    pallas_call x1, Pallas kernels, place(): pl.pallas_call(place_kernel, grid_spec=pltpu.PrefetchScalarGridSpec(num_s...  6.6 us
  transfers between devices with their start and end apart: 22, of which 17 were waited for; matrix products, arithmetic and copies ran while one was open for 2% of the time, Pallas kernels for 0%

profile of v1, /device:TPU:1, one launch (start us, length us, event | category | flops | bytes accessed | tf_op | source)
XLA Modules:
  0.0 133.2 jit_solution(8267654309871760184)
XLA Ops:
  0.7 0.1 stack.23.pos
  0.8 4.0 %copy-done.7 = bf16[1,1024,5120]{2,1,0:T(8,128)(2,1)S(1)} copy-done((bf16[1,1024,5120]{2,1,0:T(8,128)(2,1)S(1)}, bf16[1,1024,5120]{2,1,0:T(8,128)(2,1)}, u32[]{:S(2)}) %copy-start.7) | copy-done | bytes 10485784
  4.8 1.1 copy-done.8
  5.9 0.0 copy-start.6
  5.9 0.0 copy-start.3
  5.9 8.1 %product.1 = (bf16[96,5120]{1,0:T(8,128)(2,1)S(1)}, bf16[96,5120]{1,0:T(8,128)(2,1)S(1)}, bf16[96,5120]{1,0:T(8,128)(2,1)S(1)}, bf16[96,5120]{1,0:T(8,128)(2,1)S(1)}) custom-call(s32[5]{0:T(128)S(1)} %stack.23.pos, bf16[1,1024,384]{2,1,0:T(8,128)(2,1)S(1)} %copy-done.8, bf16[1,1024,5120]{2,1,0:T(8,128)(2,1)S(1)} %copy-done.7), custom_call_target="tpu_custom_call" | custom-call | flops 4026531840 | bytes 15204352 | tf_op jit(solution)/shard_map/product/pallas_call | solution.py:121
  14.0 3.8 %collective-permute-start = (bf16[96,5120]{1,0:T(8,128)(2,1)S(1)}, bf16[96,5120]{1,0:T(8,128)(2,1)S(1)}, u32[]{:S(2)}, u32[]{:S(2)}) collective-permute-start(bf16[96,5120]{1,0:T(8,128)(2,1)S(1)} %get-tuple-element.24), channel_id=1, source_target_pairs={{0,2},{1,3},{2,0},{3,1},{4,6},{5,7},{6,4},{7,5},{8,10},{9,11},{10,... | collective-permute-start | bytes 2949128 | tf_op jit(solution)/shard_map/ppermute | solution.py:79
  17.9 0.4 collective-permute-start.1
  18.3 2.3 %collective-permute-start.2 = (bf16[96,5120]{1,0:T(8,128)(2,1)S(1)}, bf16[96,5120]{1,0:T(8,128)(2,1)S(1)}, u32[]{:S(2)}, u32[]{:S(2)}) collective-permute-start(bf16[96,5120]{1,0:T(8,128)(2,1)S(1)} %get-tuple-element.26), channel_id=1, source_target_pairs={{0,3},{1,0},{2,1},{3,2},{4,7},{5,4},{6,5},{7,6},{8,11},{9,8},{10,9... | collective-permute-start | bytes 2949128 | tf_op jit(solution)/shard_map/ppermute | solution.py:79
  20.5 9.1 %collective-permute-done.one = bf16[96,5120]{1,0:T(8,128)(2,1)S(1)} collective-permute-done((bf16[96,5120]{1,0:T(8,128)(2,1)S(1)}, bf16[96,5120]{1,0:T(8,128)(2,1)S(1)}, u32[]{:S(2)}, u32[]{:S(2)}) %collective-permute-start) | collective-permute-done | bytes 983072 | tf_op jit(solution)/shard_map/ppermute | solution.py:79
  29.7 10.5 %collective-permute-done.1.two = bf16[96,5120]{1,0:T(8,128)(2,1)S(1)} collective-permute-done((bf16[96,5120]{1,0:T(8,128)(2,1)S(1)}, bf16[96,5120]{1,0:T(8,128)(2,1)S(1)}, u32[]{:S(2)}, u32[]{:S(2)}) %collective-permute-start.1) | collective-permute-done | bytes 983072 | tf_op jit(solution)/shard_map/ppermute | solution.py:79
  40.2 0.4 collective-permute-done.2.three
  40.6 1.0 add_first.1
  41.6 2.8 %collective-permute-start.3 = (bf16[24,5120]{1,0:T(8,128)(2,1)S(1)}, bf16[24,5120]{1,0:T(8,128)(2,1)S(1)}, u32[]{:S(2)}, u32[]{:S(2)}) collective-permute-start(bf16[24,5120]{1,0:T(8,128)(2,1)S(1)} %get-tuple-element.28), channel_id=1, source_target_pairs={{0,8},{1,9},{2,10},{3,11},{4,12},{5,13},{6,14},{7,15},{8,0},{9,1},... | collective-permute-start | bytes 737288 | tf_op jit(solution)/shard_map/ppermute | solution.py:79
  44.4 0.3 collective-permute-start.4
  44.7 2.4 %collective-permute-start.5 = (bf16[24,5120]{1,0:T(8,128)(2,1)S(1)}, bf16[24,5120]{1,0:T(8,128)(2,1)S(1)}, u32[]{:S(2)}, u32[]{:S(2)}) collective-permute-start(bf16[24,5120]{1,0:T(8,128)(2,1)S(1)} %get-tuple-element.30), channel_id=1, source_target_pairs={{0,12},{1,13},{2,14},{3,15},{4,0},{5,1},{6,2},{7,3},{8,4},{9,5},{1... | collective-permute-start | bytes 737288 | tf_op jit(solution)/shard_map/ppermute | solution.py:79
  47.1 1.1 collective-permute-done.3.one
  48.2 2.9 %collective-permute-done.4.two = bf16[24,5120]{1,0:T(8,128)(2,1)S(1)} collective-permute-done((bf16[24,5120]{1,0:T(8,128)(2,1)S(1)}, bf16[24,5120]{1,0:T(8,128)(2,1)S(1)}, u32[]{:S(2)}, u32[]{:S(2)}) %collective-permute-start.4) | collective-permute-done | bytes 245792 | tf_op jit(solution)/shard_map/ppermute | solution.py:79
  51.1 0.1 collective-permute-done.5.three
  51.2 0.1 add_second.1
  51.4 7.0 %collective-permute-start.6 = (bf16[16,5120]{1,0:T(8,128)(2,1)S(1)}, bf16[16,5120]{1,0:T(8,128)(2,1)S(1)}, u32[]{:S(2)}, u32[]{:S(2)}) collective-permute-start(bf16[16,5120]{1,0:T(8,128)(2,1)S(1)} %get-tuple-element.32), channel_id=1, source_target_pairs={{0,16},{1,17},{2,18},{3,19},{4,20},{5,21},{6,22},{7,23},{8,24},{9,... | collective-permute-start | bytes 491528 | tf_op jit(solution)/shard_map/ppermute | solution.py:79
  58.4 0.1 copy.13.drift
  58.4 0.1 copy.14.first
  58.5 0.1 copy.15.second
  58.6 2.6 %collective-permute-done.6.arrived = bf16[16,5120]{1,0:T(8,128)(2,1)S(1)} collective-permute-done((bf16[16,5120]{1,0:T(8,128)(2,1)S(1)}, bf16[16,5120]{1,0:T(8,128)(2,1)S(1)}, u32[]{:S(2)}, u32[]{:S(2)}) %collective-permute-start.6) | collective-permute-done | bytes 163872 | tf_op jit(solution)/shard_map/ppermute | solution.py:79
  61.2 1.3 inner_step.1
  62.5 0.0 copy-start.4
  62.5 0.6 copy-done.4
  63.2 4.7 %collective-permute-start.7 = (bf16[16,2560]{1,0:T(8,128)(2,1)S(1)}, bf16[16,2560]{1,0:T(8,128)(2,1)S(1)}, u32[]{:S(2)}, u32[]{:S(2)}) collective-permute-start(bf16[16,2560]{1,0:T(8,128)(2,1)S(1)} %get-tuple-element.36), channel_id=1, source_target_pairs={{0,32},{1,33},{2,34},{3,35},{4,36},{5,37},{6,38},{7,39},{8,40},{9,... | collective-permute-start | bytes 245768 | tf_op jit(solution)/shard_map/ppermute | solution.py:79
  67.8 0.9 collective-permute-done.7.arrived
  68.8 0.6 copy-done.15
  69.4 1.6 %add_cores.1.own = bf16[16,2560]{1,0:T(8,128)(2,1)} custom-call(bf16[16,2560]{1,0:T(8,128)(2,1)} %copy-done.4, bf16[16,2560]{1,0:T(8,128)(2,1)} %copy-done.15), custom_call_target="tpu_custom_call" | custom-call | tf_op jit(solution)/shard_map/add_cores/pallas_call | solution.py:265
  71.0 3.1 %collective-permute-start.10 = (bf16[16,2560]{1,0:T(8,128)(2,1)}, bf16[16,2560]{1,0:T(8,128)(2,1)S(1)}, u32[]{:S(2)}, u32[]{:S(2)}) collective-permute-start(bf16[16,2560]{1,0:T(8,128)(2,1)} %add_cores.1.own), channel_id=1, source_target_pairs={{0,192},{1,193},{2,194},{3,195},{4,196},{5,197},{6,198},{7,199},{8... | collective-permute-start | bytes 245768 | tf_op jit(solution)/shard_map/ppermute | solution.py:79
  74.1 0.4 collective-permute-start.8
  74.5 2.1 %collective-permute-done.10.three = bf16[16,2560]{1,0:T(8,128)(2,1)S(1)} collective-permute-done((bf16[16,2560]{1,0:T(8,128)(2,1)}, bf16[16,2560]{1,0:T(8,128)(2,1)S(1)}, u32[]{:S(2)}, u32[]{:S(2)}) %collective-permute-start.10) | collective-permute-done | bytes 81952 | tf_op jit(solution)/shard_map/ppermute | solution.py:79
  76.7 5.0 %collective-permute-done.9.two = bf16[16,2560]{1,0:T(8,128)(2,1)S(1)} collective-permute-done((bf16[16,2560]{1,0:T(8,128)(2,1)}, bf16[16,2560]{1,0:T(8,128)(2,1)S(1)}, u32[]{:S(2)}, u32[]{:S(2)}) %collective-permute-start.9) | collective-permute-done | bytes 81952 | tf_op jit(solution)/shard_map/ppermute | solution.py:79
  81.7 0.9 copy-done.2
  82.6 1.3 outer_step.1
  83.9 5.3 %collective-permute-start.11 = (bf16[16,2560]{1,0:T(8,128)(2,1)S(1)}, bf16[16,2560]{1,0:T(8,128)(2,1)S(1)}, u32[]{:S(2)}, u32[]{:S(2)}) collective-permute-start(bf16[16,2560]{1,0:T(8,128)(2,1)S(1)} %get-tuple-element.40.own), channel_id=1, source_target_pairs={{0,16},{1,17},{2,18},{3,19},{4,20},{5,21},{6,22},{7,23},{8,24},{9,... | collective-permute-start | bytes 245768 | tf_op jit(solution)/shard_map/ppermute | solution.py:79
  89.1 2.0 %collective-permute-done.11.arrived = bf16[16,2560]{1,0:T(8,128)(2,1)S(1)} collective-permute-done((bf16[16,2560]{1,0:T(8,128)(2,1)S(1)}, bf16[16,2560]{1,0:T(8,128)(2,1)S(1)}, u32[]{:S(2)}, u32[]{:S(2)}) %collective-permute-start.11) | collective-permute-done | bytes 81952 | tf_op jit(solution)/shard_map/ppermute | solution.py:79
  91.2 0.6 copy-done.16
  91.8 1.6 %join_pair.1.refs_0_ = bf16[24,2560]{1,0:T(8,128)(2,1)} custom-call(bf16[16,2560]{1,0:T(8,128)(2,1)} %copy-done.5, bf16[16,2560]{1,0:T(8,128)(2,1)} %copy-done.16), custom_call_target="tpu_custom_call" | custom-call | tf_op jit(solution)/shard_map/join_pair/pallas_call | solution.py:326
  93.4 1.1 collective-permute-start.14
  94.5 2.5 %collective-permute-start.13 = (bf16[24,2560]{1,0:T(8,128)(2,1)}, bf16[24,2560]{1,0:T(8,128)(2,1)S(1)}, u32[]{:S(2)}, u32[]{:S(2)}) collective-permute-start(bf16[24,2560]{1,0:T(8,128)(2,1)} %join_pair.1.refs_0_), channel_id=1, source_target_pairs={{0,8},{1,9},{2,10},{3,11},{4,12},{5,13},{6,14},{7,15},{8,0},{9,1},... | collective-permute-start | bytes 368648 | tf_op jit(solution)/shard_map/ppermute | solution.py:79
  97.0 0.3 collective-permute-start.12
  97.3 1.2 collective-permute-done.14.refs_3_
  98.6 2.2 %collective-permute-done.13.refs_2_ = bf16[24,2560]{1,0:T(8,128)(2,1)S(1)} collective-permute-done((bf16[24,2560]{1,0:T(8,128)(2,1)}, bf16[24,2560]{1,0:T(8,128)(2,1)S(1)}, u32[]{:S(2)}, u32[]{:S(2)}) %collective-permute-start.13) | collective-permute-done | bytes 122912 | tf_op jit(solution)/shard_map/ppermute | solution.py:79
  100.8 0.4 collective-permute-done.12.refs_1_
  101.2 0.2 copy-done.13
  101.5 0.6 copy-done.14
  102.1 1.9 %join_four.1.refs_0_ = bf16[96,2560]{1,0:T(8,128)(2,1)} custom-call(bf16[24,2560]{1,0:T(8,128)(2,1)} %join_pair.1.refs_0_, bf16[24,2560]{1,0:T(8,128)(2,1)} %copy-done.14, bf16[24,2560]{1,0:T(8,128)(2,1)} %copy-done.13, bf16[24,2560]{1,0:T(8,128)(2,1)} %copy-done.12), custom_call_target="tpu_custom_call" | custom-call | tf_op jit(solution)/shard_map/join_four/pallas_call | solution.py:339
  104.0 0.7 collective-permute-start.17
  104.7 3.0 %collective-permute-start.16 = (bf16[96,2560]{1,0:T(8,128)(2,1)}, bf16[96,2560]{1,0:T(8,128)(2,1)S(1)}, u32[]{:S(2)}, u32[]{:S(2)}) collective-permute-start(bf16[96,2560]{1,0:T(8,128)(2,1)} %join_four.1.refs_0_), channel_id=1, source_target_pairs={{0,2},{1,3},{2,0},{3,1},{4,6},{5,7},{6,4},{7,5},{8,10},{9,11},{10,... | collective-permute-start | bytes 1474568 | tf_op jit(solution)/shard_map/ppermute | solution.py:79
  107.7 4.0 %collective-permute-start.18 = (bf16[96,2560]{1,0:T(8,128)(2,1)}, bf16[96,2560]{1,0:T(8,128)(2,1)S(1)}, u32[]{:S(2)}, u32[]{:S(2)}) collective-permute-start(bf16[96,2560]{1,0:T(8,128)(2,1)} %join_four.1.refs_0_), channel_id=1, source_target_pairs={{0,32},{1,33},{2,34},{3,35},{4,36},{5,37},{6,38},{7,39},{8,40},{9,... | collective-permute-start | bytes 1474568 | tf_op jit(solution)/shard_map/ppermute | solution.py:79
  111.7 1.7 %collective-permute-done.17.refs_3_ = bf16[96,2560]{1,0:T(8,128)(2,1)S(1)} collective-permute-done((bf16[96,2560]{1,0:T(8,128)(2,1)}, bf16[96,2560]{1,0:T(8,128)(2,1)S(1)}, u32[]{:S(2)}, u32[]{:S(2)}) %collective-permute-start.17) | collective-permute-done | bytes 491552 | tf_op jit(solution)/shard_map/ppermute | solution.py:79
  113.4 3.9 %collective-permute-start.21 = (bf16[96,2560]{1,0:T(8,128)(2,1)S(1)}, bf16[96,2560]{1,0:T(8,128)(2,1)S(1)}, u32[]{:S(2)}, u32[]{:S(2)}) collective-permute-start(bf16[96,2560]{1,0:T(8,128)(2,1)S(1)} %collective-permute-done.17.refs_3_), channel_id=1, source_target_pairs={{0,32},{1,33},{2,34},{3,35},{4,36},{5,37},{6,38},{7,39},{8,40},{9,... | collective-permute-start | bytes 1474568 | tf_op jit(solution)/shard_map/ppermute | solution.py:79
  117.3 2.4 %collective-permute-done.16.refs_2_ = bf16[96,2560]{1,0:T(8,128)(2,1)S(1)} collective-permute-done((bf16[96,2560]{1,0:T(8,128)(2,1)}, bf16[96,2560]{1,0:T(8,128)(2,1)S(1)}, u32[]{:S(2)}, u32[]{:S(2)}) %collective-permute-start.16) | collective-permute-done | bytes 491552 | tf_op jit(solution)/shard_map/ppermute | solution.py:79
  119.7 3.7 %collective-permute-start.20 = (bf16[96,2560]{1,0:T(8,128)(2,1)S(1)}, bf16[96,2560]{1,0:T(8,128)(2,1)S(1)}, u32[]{:S(2)}, u32[]{:S(2)}) collective-permute-start(bf16[96,2560]{1,0:T(8,128)(2,1)S(1)} %collective-permute-done.16.refs_2_), channel_id=1, source_target_pairs={{0,32},{1,33},{2,34},{3,35},{4,36},{5,37},{6,38},{7,39},{8,40},{9,... | collective-permute-start | bytes 1474568 | tf_op jit(solution)/shard_map/ppermute | solution.py:79
  123.4 0.1 collective-permute-start.19
  123.5 0.9 copy.16
  124.4 0.9 copy.17
  125.4 0.2 collective-permute-done.19.refs_5_
  125.6 1.0 copy-done
  126.6 6.6 %place.1 = bf16[384,5120]{1,0:T(8,128)(2,1)} custom-call(s32[5]{0:T(128)S(1)} %stack.23.pos, bf16[96,2560]{1,0:T(8,128)(2,1)S(1)} %copy-done, bf16[96,2560]{1,0:T(8,128)(2,1)S(1)} %collective-permute-done.15.refs_1_, bf16[96,2560]{1,0:T(8,128)(2,1)S(1)} %collective-permute-done.16.refs_2_, bf16[96,2560]{1,0:T(8,128)(2,1)S(1)} %collective-permute-done.17.refs_3_, ...), custom_call_target="tpu_custom_call" | custom-call | tf_op jit(solution)/shard_map/place/pallas_call | solution.py:371
  (29 shorter events, 0.1 us)
Async XLA Ops:
  0.8 4.0 %copy-start.7 = (bf16[1,1024,5120]{2,1,0:T(8,128)(2,1)S(1)}, bf16[1,1024,5120]{2,1,0:T(8,128)(2,1)}, u32[]{:S(2)}) copy-start(bf16[1,1024,5120]{2,1,0:T(8,128)(2,1)} %act_ref.1) | copy-start | bytes 31457284
  4.8 1.1 copy-start.8
  5.9 52.5 %copy-start.9 = (f32[1,12,5120]{2,0,1:T(1,128)S(1)}, f32[1,12,5120]{2,0,1:T(1,128)}, u32[]{:S(2)}) copy-start(f32[1,12,5120]{2,0,1:T(1,128)} %param.10) | copy-start | bytes 737284
  5.9 52.5 %copy-start.10 = (f32[1,12,5120]{2,0,1:T(1,128)S(1)}, f32[1,12,5120]{2,0,1:T(1,128)}, u32[]{:S(2)}) copy-start(f32[1,12,5120]{2,0,1:T(1,128)} %param.11) | copy-start | bytes 737284
  5.9 52.6 %copy-start.11 = (f32[1,12,5120]{2,0,1:T(1,128)S(1)}, f32[1,12,5120]{2,0,1:T(1,128)}, u32[]{:S(2)}) copy-start(f32[1,12,5120]{2,0,1:T(1,128)} %param.12) | copy-start | bytes 737284
  5.9 55.3 %copy-start.1 = (f32[12,5120]{1,0:T(8,128)S(1)}, f32[12,5120]{1,0:T(8,128)}, u32[]{:S(2)}) copy-start(f32[12,5120]{1,0:T(8,128)} %base.3) | copy-start | bytes 737284
  5.9 55.3 %copy-start.6 = (s32[12,40]{1,0:T(8,128)S(1)}, s32[12,40]{1,0:T(8,128)}, u32[]{:S(2)}) copy-start(s32[12,40]{1,0:T(8,128)} %exponents.1) | copy-start | bytes 5764
  5.9 75.8 %copy-start.3 = (f32[12,5120]{1,0:T(8,128)S(1)}, f32[12,5120]{1,0:T(8,128)}, u32[]{:S(2)}) copy-start(f32[12,5120]{1,0:T(8,128)} %momentum.1) | copy-start | bytes 737284
  14.0 15.7 %collective-permute-start = (bf16[96,5120]{1,0:T(8,128)(2,1)S(1)}, bf16[96,5120]{1,0:T(8,128)(2,1)S(1)}, u32[]{:S(2)}, u32[]{:S(2)}) collective-permute-start(bf16[96,5120]{1,0:T(8,128)(2,1)S(1)} %get-tuple-element.24), channel_id=1, source_target_pairs={{0,2},{1,3},{2,0},{3,1},{4,6},{5,7},{6,4},{7,5},{8,10},{9,11},{10,... | collective-permute-start | bytes 2949128 | tf_op jit(solution)/shard_map/ppermute | solution.py:79
  17.9 22.3 %collective-permute-start.1 = (bf16[96,5120]{1,0:T(8,128)(2,1)S(1)}, bf16[96,5120]{1,0:T(8,128)(2,1)S(1)}, u32[]{:S(2)}, u32[]{:S(2)}) collective-permute-start(bf16[96,5120]{1,0:T(8,128)(2,1)S(1)} %get-tuple-element.25), channel_id=1, source_target_pairs={{0,1},{1,2},{2,3},{3,0},{4,5},{5,6},{6,7},{7,4},{8,9},{9,10},{10,1... | collective-permute-start | bytes 2949128 | tf_op jit(solution)/shard_map/ppermute | solution.py:79
  18.3 22.4 %collective-permute-start.2 = (bf16[96,5120]{1,0:T(8,128)(2,1)S(1)}, bf16[96,5120]{1,0:T(8,128)(2,1)S(1)}, u32[]{:S(2)}, u32[]{:S(2)}) collective-permute-start(bf16[96,5120]{1,0:T(8,128)(2,1)S(1)} %get-tuple-element.26), channel_id=1, source_target_pairs={{0,3},{1,0},{2,1},{3,2},{4,7},{5,4},{6,5},{7,6},{8,11},{9,8},{10,9... | collective-permute-start | bytes 2949128 | tf_op jit(solution)/shard_map/ppermute | solution.py:79
  41.6 6.7 %collective-permute-start.3 = (bf16[24,5120]{1,0:T(8,128)(2,1)S(1)}, bf16[24,5120]{1,0:T(8,128)(2,1)S(1)}, u32[]{:S(2)}, u32[]{:S(2)}) collective-permute-start(bf16[24,5120]{1,0:T(8,128)(2,1)S(1)} %get-tuple-element.28), channel_id=1, source_target_pairs={{0,8},{1,9},{2,10},{3,11},{4,12},{5,13},{6,14},{7,15},{8,0},{9,1},... | collective-permute-start | bytes 737288 | tf_op jit(solution)/shard_map/ppermute | solution.py:79
  44.4 6.7 %collective-permute-start.4 = (bf16[24,5120]{1,0:T(8,128)(2,1)S(1)}, bf16[24,5120]{1,0:T(8,128)(2,1)S(1)}, u32[]{:S(2)}, u32[]{:S(2)}) collective-permute-start(bf16[24,5120]{1,0:T(8,128)(2,1)S(1)} %get-tuple-element.29), channel_id=1, source_target_pairs={{0,4},{1,5},{2,6},{3,7},{4,8},{5,9},{6,10},{7,11},{8,12},{9,13},{1... | collective-permute-start | bytes 737288 | tf_op jit(solution)/shard_map/ppermute | solution.py:79
  44.7 6.5 %collective-permute-start.5 = (bf16[24,5120]{1,0:T(8,128)(2,1)S(1)}, bf16[24,5120]{1,0:T(8,128)(2,1)S(1)}, u32[]{:S(2)}, u32[]{:S(2)}) collective-permute-start(bf16[24,5120]{1,0:T(8,128)(2,1)S(1)} %get-tuple-element.30), channel_id=1, source_target_pairs={{0,12},{1,13},{2,14},{3,15},{4,0},{5,1},{6,2},{7,3},{8,4},{9,5},{1... | collective-permute-start | bytes 737288 | tf_op jit(solution)/shard_map/ppermute | solution.py:79
  51.4 9.8 %collective-permute-start.6 = (bf16[16,5120]{1,0:T(8,128)(2,1)S(1)}, bf16[16,5120]{1,0:T(8,128)(2,1)S(1)}, u32[]{:S(2)}, u32[]{:S(2)}) collective-permute-start(bf16[16,5120]{1,0:T(8,128)(2,1)S(1)} %get-tuple-element.32), channel_id=1, source_target_pairs={{0,16},{1,17},{2,18},{3,19},{4,20},{5,21},{6,22},{7,23},{8,24},{9,... | collective-permute-start | bytes 491528 | tf_op jit(solution)/shard_map/ppermute | solution.py:79
  62.5 0.6 copy-start.4
  63.2 5.6 %collective-permute-start.7 = (bf16[16,2560]{1,0:T(8,128)(2,1)S(1)}, bf16[16,2560]{1,0:T(8,128)(2,1)S(1)}, u32[]{:S(2)}, u32[]{:S(2)}) collective-permute-start(bf16[16,2560]{1,0:T(8,128)(2,1)S(1)} %get-tuple-element.36), channel_id=1, source_target_pairs={{0,32},{1,33},{2,34},{3,35},{4,36},{5,37},{6,38},{7,39},{8,40},{9,... | collective-permute-start | bytes 245768 | tf_op jit(solution)/shard_map/ppermute | solution.py:79
  68.7 0.6 copy-start.15
  71.0 5.7 %collective-permute-start.10 = (bf16[16,2560]{1,0:T(8,128)(2,1)}, bf16[16,2560]{1,0:T(8,128)(2,1)S(1)}, u32[]{:S(2)}, u32[]{:S(2)}) collective-permute-start(bf16[16,2560]{1,0:T(8,128)(2,1)} %add_cores.1.own), channel_id=1, source_target_pairs={{0,192},{1,193},{2,194},{3,195},{4,196},{5,197},{6,198},{7,199},{8... | collective-permute-start | bytes 245768 | tf_op jit(solution)/shard_map/ppermute | solution.py:79
  74.1 7.6 %collective-permute-start.9 = (bf16[16,2560]{1,0:T(8,128)(2,1)}, bf16[16,2560]{1,0:T(8,128)(2,1)S(1)}, u32[]{:S(2)}, u32[]{:S(2)}) collective-permute-start(bf16[16,2560]{1,0:T(8,128)(2,1)} %add_cores.1.own), channel_id=1, source_target_pairs={{0,128},{1,129},{2,130},{3,131},{4,132},{5,133},{6,134},{7,135},{8... | collective-permute-start | bytes 245768 | tf_op jit(solution)/shard_map/ppermute | solution.py:79
  74.1 7.6 %collective-permute-start.8 = (bf16[16,2560]{1,0:T(8,128)(2,1)}, bf16[16,2560]{1,0:T(8,128)(2,1)S(1)}, u32[]{:S(2)}, u32[]{:S(2)}) collective-permute-start(bf16[16,2560]{1,0:T(8,128)(2,1)} %add_cores.1.own), channel_id=1, source_target_pairs={{0,64},{1,65},{2,66},{3,67},{4,68},{5,69},{6,70},{7,71},{8,72},{9,... | collective-permute-start | bytes 245768 | tf_op jit(solution)/shard_map/ppermute | solution.py:79
  81.7 0.9 copy-start.2
  83.9 7.3 %copy-start.5 = (bf16[16,2560]{1,0:T(8,128)(2,1)}, bf16[16,2560]{1,0:T(8,128)(2,1)S(1)}, u32[]{:S(2)}) copy-start(bf16[16,2560]{1,0:T(8,128)(2,1)S(1)} %get-tuple-element.40.own) | copy-start | bytes 245764
  83.9 7.3 %collective-permute-start.11 = (bf16[16,2560]{1,0:T(8,128)(2,1)S(1)}, bf16[16,2560]{1,0:T(8,128)(2,1)S(1)}, u32[]{:S(2)}, u32[]{:S(2)}) collective-permute-start(bf16[16,2560]{1,0:T(8,128)(2,1)S(1)} %get-tuple-element.40.own), channel_id=1, source_target_pairs={{0,16},{1,17},{2,18},{3,19},{4,20},{5,21},{6,22},{7,23},{8,24},{9,... | collective-permute-start | bytes 245768 | tf_op jit(solution)/shard_map/ppermute | solution.py:79
  91.2 0.6 copy-start.16
  93.4 5.2 %collective-permute-start.14 = (bf16[24,2560]{1,0:T(8,128)(2,1)}, bf16[24,2560]{1,0:T(8,128)(2,1)S(1)}, u32[]{:S(2)}, u32[]{:S(2)}) collective-permute-start(bf16[24,2560]{1,0:T(8,128)(2,1)} %join_pair.1.refs_0_), channel_id=1, source_target_pairs={{0,4},{1,5},{2,6},{3,7},{4,8},{5,9},{6,10},{7,11},{8,12},{9,13},{1... | collective-permute-start | bytes 368648 | tf_op jit(solution)/shard_map/ppermute | solution.py:79
  94.5 6.3 %collective-permute-start.13 = (bf16[24,2560]{1,0:T(8,128)(2,1)}, bf16[24,2560]{1,0:T(8,128)(2,1)S(1)}, u32[]{:S(2)}, u32[]{:S(2)}) collective-permute-start(bf16[24,2560]{1,0:T(8,128)(2,1)} %join_pair.1.refs_0_), channel_id=1, source_target_pairs={{0,8},{1,9},{2,10},{3,11},{4,12},{5,13},{6,14},{7,15},{8,0},{9,1},... | collective-permute-start | bytes 368648 | tf_op jit(solution)/shard_map/ppermute | solution.py:79
  97.0 4.2 %collective-permute-start.12 = (bf16[24,2560]{1,0:T(8,128)(2,1)}, bf16[24,2560]{1,0:T(8,128)(2,1)S(1)}, u32[]{:S(2)}, u32[]{:S(2)}) collective-permute-start(bf16[24,2560]{1,0:T(8,128)(2,1)} %join_pair.1.refs_0_), channel_id=1, source_target_pairs={{0,12},{1,13},{2,14},{3,15},{4,0},{5,1},{6,2},{7,3},{8,4},{9,5},{1... | collective-permute-start | bytes 368648 | tf_op jit(solution)/shard_map/ppermute | solution.py:79
  98.6 2.7 %copy-start.12 = (bf16[24,2560]{1,0:T(8,128)(2,1)}, bf16[24,2560]{1,0:T(8,128)(2,1)S(1)}, u32[]{:S(2)}) copy-start(bf16[24,2560]{1,0:T(8,128)(2,1)S(1)} %collective-permute-done.14.refs_3_) | copy-start | bytes 368644
  100.8 0.6 copy-start.13
  101.5 0.6 copy-start.14
  104.0 9.4 %collective-permute-start.17 = (bf16[96,2560]{1,0:T(8,128)(2,1)}, bf16[96,2560]{1,0:T(8,128)(2,1)S(1)}, u32[]{:S(2)}, u32[]{:S(2)}) collective-permute-start(bf16[96,2560]{1,0:T(8,128)(2,1)} %join_four.1.refs_0_), channel_id=1, source_target_pairs={{0,1},{1,2},{2,3},{3,0},{4,5},{5,6},{6,7},{7,4},{8,9},{9,10},{10,1... | collective-permute-start | bytes 1474568 | tf_op jit(solution)/shard_map/ppermute | solution.py:79
  104.7 15.0 %collective-permute-start.16 = (bf16[96,2560]{1,0:T(8,128)(2,1)}, bf16[96,2560]{1,0:T(8,128)(2,1)S(1)}, u32[]{:S(2)}, u32[]{:S(2)}) collective-permute-start(bf16[96,2560]{1,0:T(8,128)(2,1)} %join_four.1.refs_0_), channel_id=1, source_target_pairs={{0,2},{1,3},{2,0},{3,1},{4,6},{5,7},{6,4},{7,5},{8,10},{9,11},{10,... | collective-permute-start | bytes 1474568 | tf_op jit(solution)/shard_map/ppermute | solution.py:79
  107.7 15.7 %collective-permute-start.15 = (bf16[96,2560]{1,0:T(8,128)(2,1)}, bf16[96,2560]{1,0:T(8,128)(2,1)S(1)}, u32[]{:S(2)}, u32[]{:S(2)}) collective-permute-start(bf16[96,2560]{1,0:T(8,128)(2,1)} %join_four.1.refs_0_), channel_id=1, source_target_pairs={{0,3},{1,0},{2,1},{3,2},{4,7},{5,4},{6,5},{7,6},{8,11},{9,8},{10,9... | collective-permute-start | bytes 1474568 | tf_op jit(solution)/shard_map/ppermute | solution.py:79
  107.7 17.7 %collective-permute-start.18 = (bf16[96,2560]{1,0:T(8,128)(2,1)}, bf16[96,2560]{1,0:T(8,128)(2,1)S(1)}, u32[]{:S(2)}, u32[]{:S(2)}) collective-permute-start(bf16[96,2560]{1,0:T(8,128)(2,1)} %join_four.1.refs_0_), channel_id=1, source_target_pairs={{0,32},{1,33},{2,34},{3,35},{4,36},{5,37},{6,38},{7,39},{8,40},{9,... | collective-permute-start | bytes 1474568 | tf_op jit(solution)/shard_map/ppermute | solution.py:79
  113.4 12.0 %collective-permute-start.21 = (bf16[96,2560]{1,0:T(8,128)(2,1)S(1)}, bf16[96,2560]{1,0:T(8,128)(2,1)S(1)}, u32[]{:S(2)}, u32[]{:S(2)}) collective-permute-start(bf16[96,2560]{1,0:T(8,128)(2,1)S(1)} %collective-permute-done.17.refs_3_), channel_id=1, source_target_pairs={{0,32},{1,33},{2,34},{3,35},{4,36},{5,37},{6,38},{7,39},{8,40},{9,... | collective-permute-start | bytes 1474568 | tf_op jit(solution)/shard_map/ppermute | solution.py:79
  119.7 5.7 %collective-permute-start.20 = (bf16[96,2560]{1,0:T(8,128)(2,1)S(1)}, bf16[96,2560]{1,0:T(8,128)(2,1)S(1)}, u32[]{:S(2)}, u32[]{:S(2)}) collective-permute-start(bf16[96,2560]{1,0:T(8,128)(2,1)S(1)} %collective-permute-done.16.refs_2_), channel_id=1, source_target_pairs={{0,32},{1,33},{2,34},{3,35},{4,36},{5,37},{6,38},{7,39},{8,40},{9,... | collective-permute-start | bytes 1474568 | tf_op jit(solution)/shard_map/ppermute | solution.py:79
  123.4 2.2 %collective-permute-start.19 = (bf16[96,2560]{1,0:T(8,128)(2,1)S(1)}, bf16[96,2560]{1,0:T(8,128)(2,1)S(1)}, u32[]{:S(2)}, u32[]{:S(2)}) collective-permute-start(bf16[96,2560]{1,0:T(8,128)(2,1)S(1)} %collective-permute-done.15.refs_1_), channel_id=1, source_target_pairs={{0,32},{1,33},{2,34},{3,35},{4,36},{5,37},{6,38},{7,39},{8,40},{9,... | collective-permute-start | bytes 1474568 | tf_op jit(solution)/shard_map/ppermute | solution.py:79
  125.6 1.0 copy-start

commit v2 on v0

v2 whole, which is shorter than its diff:
```python
import functools

import jax
import jax.numpy as jnp
import numpy as np
from jax import lax
from jax.experimental import pallas as pl
from jax.experimental.pallas import tpu as pltpu
from jax.sharding import PartitionSpec as P

INNER_RATE = 0.02
OUTER_RATE = 0.7
BETA_FIRST = 0.9
BETA_SECOND = 0.95
CORRECT_FIRST = 1.0 - 0.9**10
CORRECT_SECOND = 1.0 - 0.95**10
WEIGHT_DECAY = 0.1
EPSILON = 1e-08
NESTEROV_MU = 0.9

N_ISLAND = 8
N_FSDP = 32
N_ZLO = 4
RING = 4
OWN = 12
ROWS = 384
QUARTER = ROWS // 4
PAIR = 2 * OWN
BLOCK = 128
MIB = 1 << 20
BF16 = jnp.bfloat16
F32 = jnp.float32
TILE = 1280
AXES = ("island", "fsdp")
SCALARS = pl.BlockSpec(memory_space=pltpu.SMEM)
IN_VMEM = pl.BlockSpec(memory_space=pltpu.VMEM)
IN_HBM = pl.BlockSpec(memory_space=pltpu.HBM)
SMALL = pltpu.CompilerParams(vmem_limit_bytes=16 * MIB)


def device_pairs(target):
    pairs = []
    for zlo in range(N_ZLO):
        for core in range(2):
            for zhi in range(2):
                for y in range(RING):
                    for x in range(RING):
                        here = (zlo, core, zhi, y, x)
                        pairs.append((device_id(*here), device_id(*target(*here))))
    return pairs


def device_id(zlo, core, zhi, y, x):
    return (zlo * 2 + core) * N_FSDP + (zhi * RING + y) * RING + x


def along_a(step):
    def target(zlo, core, zhi, y, x):
        if core == 0:
            return (zlo, core, zhi, y, (x + step) % RING)
        return (zlo, core, zhi, (y + step) % RING, x)

    return device_pairs(target)


def along_b(step):
    def target(zlo, core, zhi, y, x):
        if core == 0:
            return (zlo, core, zhi, (y + step) % RING, x)
        return (zlo, core, zhi, y, (x + step) % RING)

    return device_pairs(target)


OTHER_ZHI = device_pairs(lambda zlo, core, zhi, y, x: (zlo, core, 1 - zhi, y, x))
NEAR_OTHER_ZHI = device_pairs(lambda zlo, core, zhi, y, x: (zlo ^ 2, core, 1 - zhi, y, x))
OTHER_CORE = device_pairs(lambda zlo, core, zhi, y, x: (zlo, 1 - core, zhi, y, x))


def other_zlo(k):
    return device_pairs(lambda zlo, core, zhi, y, x: (zlo ^ k, core, zhi, y, x))


def send(value, pairs):
    return lax.ppermute(value, AXES, pairs)


def coordinates(pos):
    device = pos[0]
    bit = lambda low, count: lax.bitwise_and(lax.shift_right_logical(device, jnp.int32(low)), jnp.int32(count - 1))
    return bit(6, N_ZLO), bit(5, 2), bit(4, 2), bit(2, RING), bit(0, RING)


def fragment_row(position, core, zhi, y, x):
    position = position.astype(F32)
    ja = jnp.floor((position + 0.5) / QUARTER)
    rest = position - QUARTER * ja
    jb = jnp.floor((rest + 0.5) / PAIR)
    rest = rest - PAIR * jb
    jz = jnp.floor((rest + 0.5) / OWN)
    r = rest - OWN * jz
    first = jnp.where(core == 0, ja, jb)
    second = jnp.where(core == 0, jb, ja)
    col = x.astype(F32) + first
    col = jnp.where(col >= RING, col - RING, col)
    line = y.astype(F32) + second
    line = jnp.where(line >= RING, line - RING, line)
    half = jnp.where(zhi == 0, jz, 1.0 - jz)
    return ((half * RING + line) * RING + col) * OWN + r


def order_kernel(pos, up_ref, *outs):
    _, core, zhi, y, x = coordinates(pos)
    wanted = fragment_row(lax.broadcasted_iota(jnp.int32, (ROWS, 1), 0), core, zhi, y, x)
    column = lax.broadcasted_iota(jnp.int32, (ROWS, ROWS), 1).astype(F32)
    pick = jnp.where(column == wanted, 1.0, 0.0).astype(BF16)
    up_rows = lax.dot_general(
        pick, up_ref[0], (((1,), (1,)), ((), ())), preferred_element_type=F32
    ).astype(BF16)
    outs[0][...] = up_rows[:QUARTER]
    outs[1][:QUARTER] = up_rows[QUARTER : 2 * QUARTER]
    outs[1][QUARTER:] = up_rows[3 * QUARTER :]
    outs[2][...] = up_rows[2 * QUARTER : 3 * QUARTER]


def order_rows(pos, upstream):
    tokens = upstream.shape[1]
    return pl.pallas_call(
        order_kernel,
        in_specs=[SCALARS, IN_VMEM],
        out_specs=[IN_VMEM] * 3,
        out_shape=[jax.ShapeDtypeStruct((n * QUARTER, tokens), BF16) for n in (1, 2, 1)],
        compiler_params=SMALL,
        name="order_rows",
    )(pos, upstream)


def product_kernel(up_rows, act_ref, *outs):
    width = act_ref.shape[2]
    chunks = up_rows.shape[0] // QUARTER
    pieces = len(outs) // chunks
    per_out = width // pieces
    for first in range(0, width, TILE):
        total = jnp.dot(
            up_rows[...], act_ref[0, :, first : first + TILE], preferred_element_type=F32
        ).astype(BF16)
        piece, place = divmod(first, per_out)
        for c in range(chunks):
            outs[c * pieces + piece][:, place : place + TILE] = total[c * QUARTER : (c + 1) * QUARTER]


def product(up_rows, activations, pieces):
    rows, tokens = up_rows.shape
    width = activations.shape[2]
    count = rows // QUARTER * pieces
    return pl.pallas_call(
        product_kernel,
        in_specs=[IN_VMEM, IN_VMEM],
        out_specs=[IN_VMEM] * count,
        out_shape=[jax.ShapeDtypeStruct((QUARTER, width // pieces), BF16)] * count,
        compiler_params=SMALL,
        cost_estimate=pl.CostEstimate(
            flops=2 * rows * tokens * width,
            bytes_accessed=2 * tokens * (width + rows) + 2 * rows * width,
            transcendentals=0,
        ),
        name="product",
    )(up_rows, activations)


def add_first_kernel(own, left_one, left_two, right_one, right_two, *outs):
    half = left_one.shape[1]
    for h, (one, two) in enumerate(((left_one, left_two), (right_one, right_two))):
        cols = slice(h * half, (h + 1) * half)
        total = own[:, cols].astype(F32) + (one[...].astype(F32) + two[...].astype(F32))
        for j in range(4):
            outs[j][:, cols] = total[j * PAIR : (j + 1) * PAIR].astype(BF16)


def add_first(parts):
    return pl.pallas_call(
        add_first_kernel,
        out_shape=[jax.ShapeDtypeStruct((PAIR, parts[0].shape[1]), BF16)] * 4,
        compiler_params=SMALL,
        name="add_first",
    )(*parts)


def packed(rows):
    half = rows.shape[1] // 2
    return jnp.concatenate([rows[:, :half], rows[:, half:]], axis=0).astype(BF16)


def add_second_kernel(own, one, two, three, keep, away):
    total = (own[...].astype(F32) + one[...].astype(F32)) + (
        two[...].astype(F32) + three[...].astype(F32)
    )
    keep[...] = total[:OWN]
    away[...] = packed(total[OWN:])


def add_second(parts):
    width = parts[0].shape[1]
    return pl.pallas_call(
        add_second_kernel,
        out_shape=[
            jax.ShapeDtypeStruct((OWN, width), F32),
            jax.ShapeDtypeStruct((PAIR, width // 2), BF16),
        ],
        compiler_params=SMALL,
        name="add_second",
    )(*parts)


def inner_kernel(pos, keep, arrived, drift, first, second, base, exponents, first_out, second_out, own, away, unscale_out):
    _, core, _, _, _ = coordinates(pos)
    width = keep.shape[1]
    share = width // N_ISLAND
    per_share = share // BLOCK
    exponent = exponents[...].astype(F32)
    scaling_all = jnp.exp2(-exponent)
    unscale_all = jnp.exp2(exponent)

    def spread(values, i):
        return jnp.concatenate(
            [
                jnp.broadcast_to(values[:, b : b + 1], (OWN, BLOCK))
                for b in range(i * per_share, (i + 1) * per_share)
            ],
            axis=1,
        )

    def coded_share(i, received):
        cols = slice(i * share, (i + 1) * share)
        gradient = keep[:, cols] + received
        base_now = base[:, cols]
        params = base_now + drift[0, :, cols]
        first_new = BETA_FIRST * first[0, :, cols] + (1.0 - BETA_FIRST) * gradient
        second_new = BETA_SECOND * second[0, :, cols] + (1.0 - BETA_SECOND) * gradient * gradient
        first_out[0, :, cols] = first_new
        second_out[0, :, cols] = second_new
        update = (
            first_new / CORRECT_FIRST / (jnp.sqrt(second_new / CORRECT_SECOND) + EPSILON)
            + WEIGHT_DECAY * params
        )
        inner = params - INNER_RATE * update
        return jnp.clip((base_now - inner) * spread(scaling_all, i), -127.0, 127.0)

    for i in range(N_ISLAND // 2):
        received = arrived[:, i * share : (i + 1) * share].astype(F32)
        upper = coded_share(i, received[:OWN])
        lower = coded_share(i + N_ISLAND // 2, received[OWN:])
        coded = jnp.concatenate([upper, lower], axis=0).astype(BF16)
        place = slice((i // 2) * share, (i // 2 + 1) * share)
        place_lower = slice((i // 2 + 2) * share, (i // 2 + 3) * share)

        @pl.when(core == i % 2)
        def _():
            own[:, place] = coded
            unscale_out[:, place] = spread(unscale_all, i)
            unscale_out[:, place_lower] = spread(unscale_all, i + N_ISLAND // 2)

        @pl.when(core != i % 2)
        def _():
            away[:, place] = coded


def inner_step(pos, keep, arrived, drift, first, second, base, exponents):
    width = keep.shape[1]
    return pl.pallas_call(
        inner_kernel,
        in_specs=[SCALARS] + [IN_VMEM] * 7,
        out_specs=[IN_VMEM] * 5,
        out_shape=[
            jax.ShapeDtypeStruct(first.shape, F32),
            jax.ShapeDtypeStruct(second.shape, F32),
            jax.ShapeDtypeStruct((PAIR, width // 4), BF16),
            jax.ShapeDtypeStruct((PAIR, width // 4), BF16),
            jax.ShapeDtypeStruct((OWN, width // 2), F32),
        ],
        compiler_params=SMALL,
        name="inner_step",
    )(pos, keep, arrived, drift, first, second, base, exponents)


def add_two_kernel(own, arrived, out):
    out[...] = (own[...].astype(F32) + arrived[...].astype(F32)).astype(BF16)


def add_two(own, arrived):
    return pl.pallas_call(
        add_two_kernel,
        out_shape=jax.ShapeDtypeStruct(own.shape, BF16),
        compiler_params=SMALL,
        name="add_two",
    )(own, arrived)


def outer_kernel(pos, own, one, two, three, unscale, momentum, base, momentum_out, base_out, fragment):
    zlo, core, _, _, _ = coordinates(pos)
    share = own.shape[1] // 2

    def outer_share(k, summed):
        cols = pl.ds(pl.multiple_of((2 * k + core) * share, BLOCK), share)
        pseudo = summed * unscale[:, k * share : (k + 1) * share] / N_ISLAND
        momentum_next = NESTEROV_MU * momentum[:, cols] + pseudo
        base_next = base[:, cols] - OUTER_RATE * (pseudo + NESTEROV_MU * momentum_next)

        @pl.when(zlo == k)
        def _():
            momentum_out[...] = momentum_next
            base_out[...] = base_next

        return base_next

    for k in range(N_ZLO // 2):
        place = slice(k * share, (k + 1) * share)
        summed = (own[:, place].astype(F32) + one[:, place].astype(F32)) + (
            two[:, place].astype(F32) + three[:, place].astype(F32)
        )
        upper = outer_share(k, summed[:OWN])
        lower = outer_share(k + 2, summed[OWN:])
        fragment[:, place] = jnp.concatenate([upper, lower], axis=0).astype(BF16)


def outer_step(pos, parts, unscale, momentum, base):
    width = base.shape[1]
    return pl.pallas_call(
        outer_kernel,
        in_specs=[SCALARS] + [IN_VMEM] * 7,
        out_specs=[IN_VMEM] * 3,
        out_shape=[
            jax.ShapeDtypeStruct((OWN, width // N_ISLAND), F32),
            jax.ShapeDtypeStruct((OWN, width // N_ISLAND), F32),
            jax.ShapeDtypeStruct((PAIR, width // 4), BF16),
        ],
        compiler_params=SMALL,
        name="outer_step",
    )(pos, *parts, unscale, momentum, base)


def join_kernel(*refs):
    *parts, out = refs
    out[...] = jnp.concatenate([p[...].astype(F32) for p in parts], axis=0).astype(BF16)


def join(parts):
    rows, width = parts[0].shape
    return pl.pallas_call(
        join_kernel,
        out_shape=jax.ShapeDtypeStruct((len(parts) * rows, width), BF16),
        compiler_params=SMALL,
        name="join",
    )(*parts)


def place_kernel(w, pos, *refs):
    parts = refs[:4]
    out, held, sent = refs[-3:]
    _, core, zhi, y, x = coordinates(pos)
    whose = core if w == 0 else 1 - core
    line_rows = RING * OWN
    share = parts[0].shape[1] // 2

    def fill(a_is_x, x_here, k, b):
        source = pl.ds(pl.multiple_of(k * share + b * BLOCK, BLOCK), BLOCK)
        rows = [p[:, source].astype(F32) for p in parts]
        for jz in range(2):
            half = zhi if jz == 0 else 1 - zhi
            for h in range(2):
                target = pl.ds(pl.multiple_of((2 * h + k) * share + b * BLOCK, BLOCK), BLOCK)
                for q in range(RING):
                    pieces = []
                    for x_there in range(RING):
                        jx = (x_there - x_here) % RING
                        ja, jb = (jx, q) if a_is_x else (q, jx)
                        first = (jb * 2 + jz) * PAIR + h * OWN
                        pieces.append(rows[ja][first : first + OWN])
                    line = half * RING + lax.rem(y + q, RING)
                    start = pl.multiple_of(line * line_rows, 16)
                    held[pl.ds(start, line_rows), target] = jnp.concatenate(pieces, axis=0).astype(BF16)

    copies = []
    for k in range(2):
        for a_is_x in (True, False):
            for x_here in range(RING):

                @pl.when(((whose == 0) == a_is_x) & (x == x_here))
                def _():
                    @pl.loop(0, share // BLOCK)
                    def _(b):
                        fill(a_is_x, x_here, k, b)

        for zlo in (k, 2 + k):
            cols = pl.ds(pl.multiple_of((2 * zlo + whose) * share, BLOCK), share)
            copies.append(
                pltpu.make_async_copy(
                    held.at[:, pl.ds(zlo * share, share)], out.at[:, cols], sent.at[len(copies)]
                )
            )
            copies[-1].start()
    for copy in copies:
        copy.wait()


def place(w, pos, parts, fragment=None):
    width = 4 * parts[0].shape[1]
    again = () if fragment is None else (fragment,)
    return pl.pallas_call(
        functools.partial(place_kernel, w),
        in_specs=[SCALARS] + [IN_VMEM] * 4 + [IN_HBM] * len(again),
        out_specs=IN_HBM,
        out_shape=jax.ShapeDtypeStruct((ROWS, width), BF16),
        scratch_shapes=[pltpu.VMEM((ROWS, width // 2), BF16), pltpu.SemaphoreType.DMA((4,))],
        input_output_aliases={5: 0} if again else {},
        compiler_params=SMALL,
        name="place",
    )(pos, *parts, *again)


def local(activations, upstream, drift, first_moment, second_moment, outer_base, outer_momentum, scale_exponents):
    pos = lax.axis_index(AXES).astype(jnp.int32).reshape(1)

    up_own, up_sides, up_far = order_rows(pos, upstream)
    far_left, far_right = product(up_far, activations, 2)
    via_left = send(far_left, along_a(1))
    via_right = send(far_right, along_a(-1))
    next_left, next_right, last_left, last_right = product(up_sides, activations, 2)
    right_one = send(next_right, along_a(1))
    left_two = send(last_left, along_a(-1))
    (own,) = product(up_own, activations, 1)
    left_one = send(add_two(next_left, via_left), along_a(1))
    right_two = send(add_two(last_right, via_right), along_a(-1))
    chunks = add_first([own, left_one, left_two, right_one, right_two])
    keep, away = add_second([chunks[0]] + [send(chunks[j], along_b(j)) for j in (2, 1, 3)])
    arrived = send(away, OTHER_ZHI)

    first_new, second_new, own, away, unscale = inner_step(
        pos, keep, arrived, drift, first_moment, second_moment, outer_base, scale_exponents
    )
    coded = add_two(own, send(away, OTHER_CORE))
    parts = [send(coded, other_zlo(k)) for k in (1, 2, 3)]
    flat = (first_new.size // BLOCK, BLOCK)
    first_flat, second_flat, *parts = lax.optimization_barrier(
        (first_new.reshape(flat), second_new.reshape(flat), *parts)
    )
    momentum_out, base_out, piece = outer_step(pos, [coded, *parts], unscale, outer_momentum, outer_base)

    piece = join([piece, send(piece, NEAR_OTHER_ZHI)])
    line = {j: send(piece, along_b(-j)) for j in (2, 1, 3)}
    piece = join([piece, line[1], line[2], line[3]])
    plane = {j: send(piece, along_a(-j)) for j in (2, 1, 3)}
    mine = [piece, plane[1], plane[2], plane[3]]
    theirs = [send(m, OTHER_CORE) for m in mine]
    fragment = place(1, pos, theirs, place(0, pos, mine))
    return (
        first_flat.reshape(first_new.shape),
        second_flat.reshape(second_new.shape),
        momentum_out,
        base_out,
        fragment,
    )


def solution(mesh):
    in_specs = (
        P("island", "fsdp", None),
        P("island", "fsdp", None),
        P("island", "fsdp", None),
        P("island", "fsdp", None),
        P("island", "fsdp", None),
        P("fsdp", None),
        P("fsdp", None),
        P("fsdp", None),
    )
    out_specs = (
        P("island", "fsdp", None),
        P("island", "fsdp", None),
        P("fsdp", "island"),
        P("fsdp", "island"),
        P(),
    )
    return jax.shard_map(local, mesh=mesh, in_specs=in_specs, out_specs=out_specs, check_vma=False)
```

time: 460 us -> 102 us (0.22)
  waiting for transfers between devices: 207 us -> 29.1 us
  blocking collectives: 168 us -> 0 us
  starting transfers between devices: 29 us -> 53.3 us
  local copies, waits for them, and re-layouts: 26.1 us -> 6.77 us
  between operations: 15 us -> 1.03 us
  Pallas kernels: 0 us -> 11.8 us
  matrix products: 9.8 us -> 0 us
    unnamed x1 -> x0, blocking collectives: 168 us -> none
    all_gather x1 -> x0, waiting for transfers between devices: 123 us -> none  [local(): lax.all_gather(base_next.astype(jnp.bfloat16), 'fsdp', axis=0, tiled=True)]
    psum x1 -> x0, waiting for transfers between devices: 84.1 us -> none  [local(): summed = lax.psum(coded.astype(jnp.bfloat16), 'island').astype(jnp.float32)]
    ppermute x0 -> x25, starting transfers between devices: none -> 53.3 us  [send(): return lax.ppermute(value, AXES, pairs)]
    ppermute x0 -> x25, waiting for transfers between devices: none -> 29.1 us  [send(): return lax.ppermute(value, AXES, pairs)]
    unnamed x8 -> x0, starting transfers between devices: 29 us -> none
    unnamed x30 -> x21, local copies, waits for them, and re-layouts: 25.3 us -> 5.3 us
    pallas_call x0 -> x15, Pallas kernels: none -> 11.8 us  [the longest x3 5.78 us: product(): pl.pallas_call(product_kernel, in_specs=[IN_VMEM, IN_VMEM], out_specs=[IN...]
  transfers between devices with their start and end apart: 10 -> 25, of which waited for: 2 -> 17; matrix products, arithmetic and copies ran while one was open for 1% -> 2% of each run, Pallas kernels for 0% -> 6%
where the time goes in v2:
time: 102 us
  starting transfers between devices  53.3 us (52%)
  waiting for transfers between devices  29.1 us (29%)
  Pallas kernels  11.8 us (12%)
  local copies, waits for them, and re-layouts  6.77 us (7%)
  between operations  1.03 us (1%)
    ppermute x25, starting transfers between devices, send(): return lax.ppermute(value, AXES, pairs)  53.3 us
    ppermute x25, waiting for transfers between devices, send(): return lax.ppermute(value, AXES, pairs)  29.1 us
    pallas_call x3, Pallas kernels, product(): pl.pallas_call(product_kernel, in_specs=[IN_VMEM, IN_VMEM], out_specs=[IN...  5.78 us
    unnamed x21, local copies, waits for them, and re-layouts  5.3 us
    pallas_call x2, Pallas kernels, place(): pl.pallas_call(functools.partial(place_kernel, w), in_specs=[SCALARS] + [...  3.19 us
  transfers between devices with their start and end apart: 25, of which 17 were waited for; matrix products, arithmetic and copies ran while one was open for 2% of the time, Pallas kernels for 6%

profile of v2, /device:TPU:1, one launch (start us, length us, event | category | flops | bytes accessed | tf_op | source)
XLA Modules:
  0.0 102.0 jit_solution(5278076100648501518)
XLA Ops:
  0.6 1.1 %copy-done.3 = bf16[1,1024,384]{2,1,0:T(8,128)(2,1)S(1)} copy-done((bf16[1,1024,384]{2,1,0:T(8,128)(2,1)S(1)}, bf16[1,1024,384]{2,1,0:T(8,128)(2,1)}, u32[]{:S(2)}) %copy-start.3) | copy-done | bytes 786456
  1.8 0.7 order_rows.1
  2.5 0.0 copy-start
  2.5 4.0 %copy-done = bf16[1,1024,5120]{2,1,0:T(8,128)(2,1)S(1)} copy-done((bf16[1,1024,5120]{2,1,0:T(8,128)(2,1)S(1)}, bf16[1,1024,5120]{2,1,0:T(8,128)(2,1)}, u32[]{:S(2)}) %copy-start) | copy-done | bytes 10485784
  6.5 1.8 %product.5 = (bf16[96,2560]{1,0:T(8,128)(2,1)S(1)}, bf16[96,2560]{1,0:T(8,128)(2,1)S(1)}) custom-call(bf16[96,1024]{1,0:T(8,128)(2,1)S(1)} %get-tuple-element.36.up_rows, bf16[1,1024,5120]{2,1,0:T(8,128)(2,1)S(1)} %copy-done), custom_call_target="tpu_custom_call" | custom-call | flops 1006632960 | bytes 11665408 | tf_op jit(solution)/shard_map/product/pallas_call | solution.py:156
  8.3 2.2 %collective-permute-start = (bf16[96,2560]{1,0:T(8,128)(2,1)S(1)}, bf16[96,2560]{1,0:T(8,128)(2,1)S(1)}, u32[]{:S(2)}, u32[]{:S(2)}) collective-permute-start(bf16[96,2560]{1,0:T(8,128)(2,1)S(1)} %get-tuple-element.37), channel_id=1, source_target_pairs={{0,1},{1,2},{2,3},{3,0},{4,5},{5,6},{6,7},{7,4},{8,9},{9,10},{10,1... | collective-permute-start | bytes 1474568 | tf_op jit(solution)/shard_map/ppermute | solution.py:85
  10.5 1.5 %collective-permute-start.4 = (bf16[96,2560]{1,0:T(8,128)(2,1)S(1)}, bf16[96,2560]{1,0:T(8,128)(2,1)S(1)}, u32[]{:S(2)}, u32[]{:S(2)}) collective-permute-start(bf16[96,2560]{1,0:T(8,128)(2,1)S(1)} %get-tuple-element.41), channel_id=1, source_target_pairs={{0,3},{1,0},{2,1},{3,2},{4,7},{5,4},{6,5},{7,6},{8,11},{9,8},{10,9... | collective-permute-start | bytes 1474568 | tf_op jit(solution)/shard_map/ppermute | solution.py:85
  12.0 2.2 %product.4 = (bf16[96,2560]{1,0:T(8,128)(2,1)S(1)}, bf16[96,2560]{1,0:T(8,128)(2,1)S(1)}, bf16[96,2560]{1,0:T(8,128)(2,1)S(1)}, bf16[96,2560]{1,0:T(8,128)(2,1)S(1)}) custom-call(bf16[192,1024]{1,0:T(8,128)(2,1)S(1)} %get-tuple-element.34.up_rows, bf16[1,1024,5120]{2,1,0:T(8,128)(2,1)S(1)} %copy-done.1), custom_call_target="tpu_custom_call" | custom-call | flops 2013265920 | bytes 12845056 | tf_op jit(solution)/shard_map/product/pallas_call | solution.py:156
  14.2 2.1 %collective-permute-start.2 = (bf16[96,2560]{1,0:T(8,128)(2,1)S(1)}, bf16[96,2560]{1,0:T(8,128)(2,1)S(1)}, u32[]{:S(2)}, u32[]{:S(2)}) collective-permute-start(bf16[96,2560]{1,0:T(8,128)(2,1)S(1)} %get-tuple-element.38), channel_id=1, source_target_pairs={{0,3},{1,0},{2,1},{3,2},{4,7},{5,4},{6,5},{7,6},{8,11},{9,8},{10,9... | collective-permute-start | bytes 1474568 | tf_op jit(solution)/shard_map/ppermute | solution.py:85
  16.3 2.1 %collective-permute-done.arrived = bf16[96,2560]{1,0:T(8,128)(2,1)S(1)} collective-permute-done((bf16[96,2560]{1,0:T(8,128)(2,1)S(1)}, bf16[96,2560]{1,0:T(8,128)(2,1)S(1)}, u32[]{:S(2)}, u32[]{:S(2)}) %collective-permute-start) | collective-permute-done | bytes 491552 | tf_op jit(solution)/shard_map/ppermute | solution.py:85
  18.4 0.1 add_two.3
  18.6 0.1 collective-permute-start.1
  18.7 0.1 add_two.4
  18.8 2.7 %collective-permute-start.5 = (bf16[96,2560]{1,0:T(8,128)(2,1)S(1)}, bf16[96,2560]{1,0:T(8,128)(2,1)S(1)}, u32[]{:S(2)}, u32[]{:S(2)}) collective-permute-start(bf16[96,2560]{1,0:T(8,128)(2,1)S(1)} %add_two.4), channel_id=1, source_target_pairs={{0,3},{1,0},{2,1},{3,2},{4,7},{5,4},{6,5},{7,6},{8,11},{9,8},{10,9... | collective-permute-start | bytes 1474568 | tf_op jit(solution)/shard_map/ppermute | solution.py:85
  21.5 1.8 %product.3.own = bf16[96,5120]{1,0:T(8,128)(2,1)S(1)} custom-call(bf16[96,1024]{1,0:T(8,128)(2,1)S(1)} %get-tuple-element.33.up_rows, bf16[1,1024,5120]{2,1,0:T(8,128)(2,1)S(1)} %copy-done.1), custom_call_target="tpu_custom_call" | custom-call | flops 1006632960 | bytes 11665408 | tf_op jit(solution)/shard_map/product/pallas_call | solution.py:156
  23.3 0.0 copy-start.6
  23.3 0.0 copy-start.7
  23.3 0.0 copy-start.8
  23.3 0.0 copy-start.2
  23.4 0.0 copy-start.4
  23.4 0.4 collective-permute-done.2.left_two
  23.7 1.8 %collective-permute-done.3.right_one = bf16[96,2560]{1,0:T(8,128)(2,1)S(1)} collective-permute-done((bf16[96,2560]{1,0:T(8,128)(2,1)S(1)}, bf16[96,2560]{1,0:T(8,128)(2,1)S(1)}, u32[]{:S(2)}, u32[]{:S(2)}) %collective-permute-start.3) | collective-permute-done | bytes 491552 | tf_op jit(solution)/shard_map/ppermute | solution.py:85
  25.5 5.3 %collective-permute-done.1.left_one = bf16[96,2560]{1,0:T(8,128)(2,1)S(1)} collective-permute-done((bf16[96,2560]{1,0:T(8,128)(2,1)S(1)}, bf16[96,2560]{1,0:T(8,128)(2,1)S(1)}, u32[]{:S(2)}, u32[]{:S(2)}) %collective-permute-start.1) | collective-permute-done | bytes 491552 | tf_op jit(solution)/shard_map/ppermute | solution.py:85
  30.8 0.4 add_first.1
  31.1 2.5 %collective-permute-start.6 = (bf16[24,5120]{1,0:T(8,128)(2,1)S(1)}, bf16[24,5120]{1,0:T(8,128)(2,1)S(1)}, u32[]{:S(2)}, u32[]{:S(2)}) collective-permute-start(bf16[24,5120]{1,0:T(8,128)(2,1)S(1)} %get-tuple-element.43), channel_id=1, source_target_pairs={{0,8},{1,9},{2,10},{3,11},{4,12},{5,13},{6,14},{7,15},{8,0},{9,1},... | collective-permute-start | bytes 737288 | tf_op jit(solution)/shard_map/ppermute | solution.py:85
  33.7 0.6 collective-permute-start.7
  34.3 2.1 %collective-permute-start.8 = (bf16[24,5120]{1,0:T(8,128)(2,1)S(1)}, bf16[24,5120]{1,0:T(8,128)(2,1)S(1)}, u32[]{:S(2)}, u32[]{:S(2)}) collective-permute-start(bf16[24,5120]{1,0:T(8,128)(2,1)S(1)} %get-tuple-element.45), channel_id=1, source_target_pairs={{0,12},{1,13},{2,14},{3,15},{4,0},{5,1},{6,2},{7,3},{8,4},{9,5},{1... | collective-permute-start | bytes 737288 | tf_op jit(solution)/shard_map/ppermute | solution.py:85
  36.3 1.7 %collective-permute-done.6.one = bf16[24,5120]{1,0:T(8,128)(2,1)S(1)} collective-permute-done((bf16[24,5120]{1,0:T(8,128)(2,1)S(1)}, bf16[24,5120]{1,0:T(8,128)(2,1)S(1)}, u32[]{:S(2)}, u32[]{:S(2)}) %collective-permute-start.6) | collective-permute-done | bytes 245792 | tf_op jit(solution)/shard_map/ppermute | solution.py:85
  38.1 2.6 %collective-permute-done.7.two = bf16[24,5120]{1,0:T(8,128)(2,1)S(1)} collective-permute-done((bf16[24,5120]{1,0:T(8,128)(2,1)S(1)}, bf16[24,5120]{1,0:T(8,128)(2,1)S(1)}, u32[]{:S(2)}, u32[]{:S(2)}) %collective-permute-start.7) | collective-permute-done | bytes 245792 | tf_op jit(solution)/shard_map/ppermute | solution.py:85
  40.7 0.1 collective-permute-done.8.three
  40.8 0.1 add_second.1
  40.9 6.9 %collective-permute-start.9 = (bf16[24,2560]{1,0:T(8,128)(2,1)S(1)}, bf16[24,2560]{1,0:T(8,128)(2,1)S(1)}, u32[]{:S(2)}, u32[]{:S(2)}) collective-permute-start(bf16[24,2560]{1,0:T(8,128)(2,1)S(1)} %get-tuple-element.47), channel_id=1, source_target_pairs={{0,16},{1,17},{2,18},{3,19},{4,20},{5,21},{6,22},{7,23},{8,24},{9,... | collective-permute-start | bytes 368648 | tf_op jit(solution)/shard_map/ppermute | solution.py:85
  47.8 0.1 copy.22.drift
  47.9 0.1 copy.23.first
  48.0 0.1 copy.24.second
  48.0 2.2 %collective-permute-done.9.arrived = bf16[24,2560]{1,0:T(8,128)(2,1)S(1)} collective-permute-done((bf16[24,2560]{1,0:T(8,128)(2,1)S(1)}, bf16[24,2560]{1,0:T(8,128)(2,1)S(1)}, u32[]{:S(2)}, u32[]{:S(2)}) %collective-permute-start.9) | collective-permute-done | bytes 122912 | tf_op jit(solution)/shard_map/ppermute | solution.py:85
  50.2 0.6 inner_step.1
  50.8 4.0 %collective-permute-start.10 = (bf16[24,1280]{1,0:T(8,128)(2,1)S(1)}, bf16[24,1280]{1,0:T(8,128)(2,1)S(1)}, u32[]{:S(2)}, u32[]{:S(2)}) collective-permute-start(bf16[24,1280]{1,0:T(8,128)(2,1)S(1)} %get-tuple-element.51), channel_id=1, source_target_pairs={{0,32},{1,33},{2,34},{3,35},{4,36},{5,37},{6,38},{7,39},{8,40},{9,... | collective-permute-start | bytes 184328 | tf_op jit(solution)/shard_map/ppermute | solution.py:85
  54.8 0.9 collective-permute-done.10.arrived
  55.8 3.7 %collective-permute-start.13 = (bf16[24,1280]{1,0:T(8,128)(2,1)S(1)}, bf16[24,1280]{1,0:T(8,128)(2,1)S(1)}, u32[]{:S(2)}, u32[]{:S(2)}) collective-permute-start(bf16[24,1280]{1,0:T(8,128)(2,1)S(1)} %add_two.5.own), channel_id=1, source_target_pairs={{0,192},{1,193},{2,194},{3,195},{4,196},{5,197},{6,198},{7,199},{8... | collective-permute-start | bytes 184328 | tf_op jit(solution)/shard_map/ppermute | solution.py:85
  59.5 0.4 collective-permute-start.11
  59.8 0.7 reshape.26
  60.6 0.7 reshape.27
  61.3 0.2 collective-permute-done.13.three
  61.5 3.1 %collective-permute-done.12.two = bf16[24,1280]{1,0:T(8,128)(2,1)S(1)} collective-permute-done((bf16[24,1280]{1,0:T(8,128)(2,1)S(1)}, bf16[24,1280]{1,0:T(8,128)(2,1)S(1)}, u32[]{:S(2)}, u32[]{:S(2)}) %collective-permute-start.12) | collective-permute-done | bytes 61472 | tf_op jit(solution)/shard_map/ppermute | solution.py:85
  64.7 0.7 outer_step.1
  65.4 3.1 %collective-permute-start.14 = (bf16[24,1280]{1,0:T(8,128)(2,1)S(1)}, bf16[24,1280]{1,0:T(8,128)(2,1)S(1)}, u32[]{:S(2)}, u32[]{:S(2)}) collective-permute-start(bf16[24,1280]{1,0:T(8,128)(2,1)S(1)} %get-tuple-element.60.refs_0_), channel_id=1, source_target_pairs={{0,144},{1,145},{2,146},{3,147},{4,148},{5,149},{6,150},{7,151},{8... | collective-permute-start | bytes 184328 | tf_op jit(solution)/shard_map/ppermute | solution.py:85
  68.6 2.1 %collective-permute-done.14.refs_1_ = bf16[24,1280]{1,0:T(8,128)(2,1)S(1)} collective-permute-done((bf16[24,1280]{1,0:T(8,128)(2,1)S(1)}, bf16[24,1280]{1,0:T(8,128)(2,1)S(1)}, u32[]{:S(2)}, u32[]{:S(2)}) %collective-permute-start.14) | collective-permute-done | bytes 61472 | tf_op jit(solution)/shard_map/ppermute | solution.py:85
  70.6 1.4 %collective-permute-start.17 = (bf16[48,1280]{1,0:T(8,128)(2,1)S(1)}, bf16[48,1280]{1,0:T(8,128)(2,1)S(1)}, u32[]{:S(2)}, u32[]{:S(2)}) collective-permute-start(bf16[48,1280]{1,0:T(8,128)(2,1)S(1)} %join.2.refs_0_), channel_id=1, source_target_pairs={{0,4},{1,5},{2,6},{3,7},{4,8},{5,9},{6,10},{7,11},{8,12},{9,13},{1... | collective-permute-start | bytes 368648 | tf_op jit(solution)/shard_map/ppermute | solution.py:85
  72.0 2.5 %collective-permute-start.16 = (bf16[48,1280]{1,0:T(8,128)(2,1)S(1)}, bf16[48,1280]{1,0:T(8,128)(2,1)S(1)}, u32[]{:S(2)}, u32[]{:S(2)}) collective-permute-start(bf16[48,1280]{1,0:T(8,128)(2,1)S(1)} %join.2.refs_0_), channel_id=1, source_target_pairs={{0,8},{1,9},{2,10},{3,11},{4,12},{5,13},{6,14},{7,15},{8,0},{9,1},... | collective-permute-start | bytes 368648 | tf_op jit(solution)/shard_map/ppermute | solution.py:85
  74.5 0.0 collective-permute-start.15
  74.5 1.1 %collective-permute-done.17.refs_3_ = bf16[48,1280]{1,0:T(8,128)(2,1)S(1)} collective-permute-done((bf16[48,1280]{1,0:T(8,128)(2,1)S(1)}, bf16[48,1280]{1,0:T(8,128)(2,1)S(1)}, u32[]{:S(2)}, u32[]{:S(2)}) %collective-permute-start.17) | collective-permute-done | bytes 122912 | tf_op jit(solution)/shard_map/ppermute | solution.py:85
  75.7 2.4 %collective-permute-done.16.refs_2_ = bf16[48,1280]{1,0:T(8,128)(2,1)S(1)} collective-permute-done((bf16[48,1280]{1,0:T(8,128)(2,1)S(1)}, bf16[48,1280]{1,0:T(8,128)(2,1)S(1)}, u32[]{:S(2)}, u32[]{:S(2)}) %collective-permute-start.16) | collective-permute-done | bytes 122912 | tf_op jit(solution)/shard_map/ppermute | solution.py:85
  78.0 0.3 collective-permute-done.15.refs_1_
  78.4 0.5 collective-permute-start.23
  78.9 3.3 %collective-permute-start.21 = (bf16[192,1280]{1,0:T(8,128)(2,1)S(1)}, bf16[192,1280]{1,0:T(8,128)(2,1)S(1)}, u32[]{:S(2)}, u32[]{:S(2)}) collective-permute-start(bf16[192,1280]{1,0:T(8,128)(2,1)S(1)} %join.3.refs_0_), channel_id=1, source_target_pairs={{0,2},{1,3},{2,0},{3,1},{4,6},{5,7},{6,4},{7,5},{8,10},{9,11},{10,... | collective-permute-start | bytes 1474568 | tf_op jit(solution)/shard_map/ppermute | solution.py:85
  82.2 4.3 %collective-permute-start.18 = (bf16[192,1280]{1,0:T(8,128)(2,1)S(1)}, bf16[192,1280]{1,0:T(8,128)(2,1)S(1)}, u32[]{:S(2)}, u32[]{:S(2)}) collective-permute-start(bf16[192,1280]{1,0:T(8,128)(2,1)S(1)} %join.3.refs_0_), channel_id=1, source_target_pairs={{0,32},{1,33},{2,34},{3,35},{4,36},{5,37},{6,38},{7,39},{8,40},{9,... | collective-permute-start | bytes 1474568 | tf_op jit(solution)/shard_map/ppermute | solution.py:85
  86.5 1.1 %collective-permute-done.23.refs_3_ = bf16[192,1280]{1,0:T(8,128)(2,1)S(1)} collective-permute-done((bf16[192,1280]{1,0:T(8,128)(2,1)S(1)}, bf16[192,1280]{1,0:T(8,128)(2,1)S(1)}, u32[]{:S(2)}, u32[]{:S(2)}) %collective-permute-start.23) | collective-permute-done | bytes 491552 | tf_op jit(solution)/shard_map/ppermute | solution.py:85
  87.7 4.7 %collective-permute-start.24 = (bf16[192,1280]{1,0:T(8,128)(2,1)S(1)}, bf16[192,1280]{1,0:T(8,128)(2,1)S(1)}, u32[]{:S(2)}, u32[]{:S(2)}) collective-permute-start(bf16[192,1280]{1,0:T(8,128)(2,1)S(1)} %collective-permute-done.23.refs_3_), channel_id=1, source_target_pairs={{0,32},{1,33},{2,34},{3,35},{4,36},{5,37},{6,38},{7,39},{8,40},{9,... | collective-permute-start | bytes 1474568 | tf_op jit(solution)/shard_map/ppermute | solution.py:85
  92.4 1.6 %collective-permute-done.21.refs_2_ = bf16[192,1280]{1,0:T(8,128)(2,1)S(1)} collective-permute-done((bf16[192,1280]{1,0:T(8,128)(2,1)S(1)}, bf16[192,1280]{1,0:T(8,128)(2,1)S(1)}, u32[]{:S(2)}, u32[]{:S(2)}) %collective-permute-start.21) | collective-permute-done | bytes 491552 | tf_op jit(solution)/shard_map/ppermute | solution.py:85
  94.0 3.7 %collective-permute-start.22 = (bf16[192,1280]{1,0:T(8,128)(2,1)S(1)}, bf16[192,1280]{1,0:T(8,128)(2,1)S(1)}, u32[]{:S(2)}, u32[]{:S(2)}) collective-permute-start(bf16[192,1280]{1,0:T(8,128)(2,1)S(1)} %collective-permute-done.21.refs_2_), channel_id=1, source_target_pairs={{0,32},{1,33},{2,34},{3,35},{4,36},{5,37},{6,38},{7,39},{8,40},{9,... | collective-permute-start | bytes 1474568 | tf_op jit(solution)/shard_map/ppermute | solution.py:85
  97.7 0.9 collective-permute-start.20
  98.6 1.6 %place.2.refs_4_ = bf16[384,5120]{1,0:T(8,128)(2,1)} custom-call(s32[1]{0:T(128)} %bitcast.pos, bf16[192,1280]{1,0:T(8,128)(2,1)S(1)} %join.3.refs_0_, bf16[192,1280]{1,0:T(8,128)(2,1)S(1)} %collective-permute-done.19.refs_1_, bf16[192,1280]{1,0:T(8,128)(2,1)S(1)} %collective-permute-done.21.refs_2_, bf16[192,1280]{1,0:T(8,128)(2,1)S(1)} %collective-permute-done.23.refs_3_), custom_call_target="tpu_custom_call" | custom-call | tf_op jit(solution)/shard_map/place/pallas_call | solution.py:409
  100.2 1.6 %place.3 = bf16[384,5120]{1,0:T(8,128)(2,1)} custom-call(s32[1]{0:T(128)} %bitcast.pos, bf16[192,1280]{1,0:T(8,128)(2,1)S(1)} %collective-permute-done.18.refs_0_, bf16[192,1280]{1,0:T(8,128)(2,1)S(1)} %collective-permute-done.20.refs_1_, bf16[192,1280]{1,0:T(8,128)(2,1)S(1)} %collective-permute-done.22.refs_2_, ...), custom_call_target="tpu_custom_call", output_to_operand_aliasing={{}: (5, {})} | custom-call | tf_op jit(solution)/shard_map/place/pallas_call | solution.py:409
  (24 shorter events, 0.1 us)
Async XLA Ops:
  0.6 1.1 %copy-start.3 = (bf16[1,1024,384]{2,1,0:T(8,128)(2,1)S(1)}, bf16[1,1024,384]{2,1,0:T(8,128)(2,1)}, u32[]{:S(2)}) copy-start(bf16[1,1024,384]{2,1,0:T(8,128)(2,1)} %up_ref.1) | copy-start | bytes 2359300
  2.5 4.0 %copy-start = (bf16[1,1024,5120]{2,1,0:T(8,128)(2,1)S(1)}, bf16[1,1024,5120]{2,1,0:T(8,128)(2,1)}, u32[]{:S(2)}) copy-start(bf16[1,1024,5120]{2,1,0:T(8,128)(2,1)} %act_ref.5) | copy-start | bytes 31457284
  6.5 5.5 %copy-start.1 = (bf16[1,1024,5120]{2,1,0:T(8,128)(2,1)S(1)}, bf16[1,1024,5120]{2,1,0:T(8,128)(2,1)}, u32[]{:S(2)}) copy-start(bf16[1,1024,5120]{2,1,0:T(8,128)(2,1)} %act_ref.5) | copy-start | bytes 31457284
  8.3 10.2 %collective-permute-start = (bf16[96,2560]{1,0:T(8,128)(2,1)S(1)}, bf16[96,2560]{1,0:T(8,128)(2,1)S(1)}, u32[]{:S(2)}, u32[]{:S(2)}) collective-permute-start(bf16[96,2560]{1,0:T(8,128)(2,1)S(1)} %get-tuple-element.37), channel_id=1, source_target_pairs={{0,1},{1,2},{2,3},{3,0},{4,5},{5,6},{6,7},{7,4},{8,9},{9,10},{10,1... | collective-permute-start | bytes 1474568 | tf_op jit(solution)/shard_map/ppermute | solution.py:85
  10.5 8.2 %collective-permute-start.4 = (bf16[96,2560]{1,0:T(8,128)(2,1)S(1)}, bf16[96,2560]{1,0:T(8,128)(2,1)S(1)}, u32[]{:S(2)}, u32[]{:S(2)}) collective-permute-start(bf16[96,2560]{1,0:T(8,128)(2,1)S(1)} %get-tuple-element.41), channel_id=1, source_target_pairs={{0,3},{1,0},{2,1},{3,2},{4,7},{5,4},{6,5},{7,6},{8,11},{9,8},{10,9... | collective-permute-start | bytes 1474568 | tf_op jit(solution)/shard_map/ppermute | solution.py:85
  14.2 9.5 %collective-permute-start.2 = (bf16[96,2560]{1,0:T(8,128)(2,1)S(1)}, bf16[96,2560]{1,0:T(8,128)(2,1)S(1)}, u32[]{:S(2)}, u32[]{:S(2)}) collective-permute-start(bf16[96,2560]{1,0:T(8,128)(2,1)S(1)} %get-tuple-element.38), channel_id=1, source_target_pairs={{0,3},{1,0},{2,1},{3,2},{4,7},{5,4},{6,5},{7,6},{8,11},{9,8},{10,9... | collective-permute-start | bytes 1474568 | tf_op jit(solution)/shard_map/ppermute | solution.py:85
  16.3 9.2 %collective-permute-start.3 = (bf16[96,2560]{1,0:T(8,128)(2,1)S(1)}, bf16[96,2560]{1,0:T(8,128)(2,1)S(1)}, u32[]{:S(2)}, u32[]{:S(2)}) collective-permute-start(bf16[96,2560]{1,0:T(8,128)(2,1)S(1)} %get-tuple-element.39), channel_id=1, source_target_pairs={{0,1},{1,2},{2,3},{3,0},{4,5},{5,6},{6,7},{7,4},{8,9},{9,10},{10,1... | collective-permute-start | bytes 1474568 | tf_op jit(solution)/shard_map/ppermute | solution.py:85
  18.6 12.2 %collective-permute-start.1 = (bf16[96,2560]{1,0:T(8,128)(2,1)S(1)}, bf16[96,2560]{1,0:T(8,128)(2,1)S(1)}, u32[]{:S(2)}, u32[]{:S(2)}) collective-permute-start(bf16[96,2560]{1,0:T(8,128)(2,1)S(1)} %add_two.3), channel_id=1, source_target_pairs={{0,1},{1,2},{2,3},{3,0},{4,5},{5,6},{6,7},{7,4},{8,9},{9,10},{10,1... | collective-permute-start | bytes 1474568 | tf_op jit(solution)/shard_map/ppermute | solution.py:85
  18.8 12.0 %collective-permute-start.5 = (bf16[96,2560]{1,0:T(8,128)(2,1)S(1)}, bf16[96,2560]{1,0:T(8,128)(2,1)S(1)}, u32[]{:S(2)}, u32[]{:S(2)}) collective-permute-start(bf16[96,2560]{1,0:T(8,128)(2,1)S(1)} %add_two.4), channel_id=1, source_target_pairs={{0,3},{1,0},{2,1},{3,2},{4,7},{5,4},{6,5},{7,6},{8,11},{9,8},{10,9... | collective-permute-start | bytes 1474568 | tf_op jit(solution)/shard_map/ppermute | solution.py:85
  23.3 24.5 %copy-start.6 = (f32[1,12,5120]{2,0,1:T(1,128)S(1)}, f32[1,12,5120]{2,0,1:T(1,128)}, u32[]{:S(2)}) copy-start(f32[1,12,5120]{2,0,1:T(1,128)} %param.10) | copy-start | bytes 737284
  23.3 24.6 %copy-start.7 = (f32[1,12,5120]{2,0,1:T(1,128)S(1)}, f32[1,12,5120]{2,0,1:T(1,128)}, u32[]{:S(2)}) copy-start(f32[1,12,5120]{2,0,1:T(1,128)} %param.11) | copy-start | bytes 737284
  23.3 24.6 %copy-start.8 = (f32[1,12,5120]{2,0,1:T(1,128)S(1)}, f32[1,12,5120]{2,0,1:T(1,128)}, u32[]{:S(2)}) copy-start(f32[1,12,5120]{2,0,1:T(1,128)} %param.12) | copy-start | bytes 737284
  23.3 26.9 %copy-start.2 = (f32[12,5120]{1,0:T(8,128)S(1)}, f32[12,5120]{1,0:T(8,128)}, u32[]{:S(2)}) copy-start(f32[12,5120]{1,0:T(8,128)} %base.3) | copy-start | bytes 737284
  23.3 26.9 %copy-start.5 = (s32[12,40]{1,0:T(8,128)S(1)}, s32[12,40]{1,0:T(8,128)}, u32[]{:S(2)}) copy-start(s32[12,40]{1,0:T(8,128)} %exponents.1) | copy-start | bytes 5764
  23.4 41.3 %copy-start.4 = (f32[12,5120]{1,0:T(8,128)S(1)}, f32[12,5120]{1,0:T(8,128)}, u32[]{:S(2)}) copy-start(f32[12,5120]{1,0:T(8,128)} %momentum.1) | copy-start | bytes 737284
  31.1 6.9 %collective-permute-start.6 = (bf16[24,5120]{1,0:T(8,128)(2,1)S(1)}, bf16[24,5120]{1,0:T(8,128)(2,1)S(1)}, u32[]{:S(2)}, u32[]{:S(2)}) collective-permute-start(bf16[24,5120]{1,0:T(8,128)(2,1)S(1)} %get-tuple-element.43), channel_id=1, source_target_pairs={{0,8},{1,9},{2,10},{3,11},{4,12},{5,13},{6,14},{7,15},{8,0},{9,1},... | collective-permute-start | bytes 737288 | tf_op jit(solution)/shard_map/ppermute | solution.py:85
  33.7 7.0 %collective-permute-start.7 = (bf16[24,5120]{1,0:T(8,128)(2,1)S(1)}, bf16[24,5120]{1,0:T(8,128)(2,1)S(1)}, u32[]{:S(2)}, u32[]{:S(2)}) collective-permute-start(bf16[24,5120]{1,0:T(8,128)(2,1)S(1)} %get-tuple-element.44), channel_id=1, source_target_pairs={{0,4},{1,5},{2,6},{3,7},{4,8},{5,9},{6,10},{7,11},{8,12},{9,13},{1... | collective-permute-start | bytes 737288 | tf_op jit(solution)/shard_map/ppermute | solution.py:85
  34.3 6.5 %collective-permute-start.8 = (bf16[24,5120]{1,0:T(8,128)(2,1)S(1)}, bf16[24,5120]{1,0:T(8,128)(2,1)S(1)}, u32[]{:S(2)}, u32[]{:S(2)}) collective-permute-start(bf16[24,5120]{1,0:T(8,128)(2,1)S(1)} %get-tuple-element.45), channel_id=1, source_target_pairs={{0,12},{1,13},{2,14},{3,15},{4,0},{5,1},{6,2},{7,3},{8,4},{9,5},{1... | collective-permute-start | bytes 737288 | tf_op jit(solution)/shard_map/ppermute | solution.py:85
  40.9 9.3 %collective-permute-start.9 = (bf16[24,2560]{1,0:T(8,128)(2,1)S(1)}, bf16[24,2560]{1,0:T(8,128)(2,1)S(1)}, u32[]{:S(2)}, u32[]{:S(2)}) collective-permute-start(bf16[24,2560]{1,0:T(8,128)(2,1)S(1)} %get-tuple-element.47), channel_id=1, source_target_pairs={{0,16},{1,17},{2,18},{3,19},{4,20},{5,21},{6,22},{7,23},{8,24},{9,... | collective-permute-start | bytes 368648 | tf_op jit(solution)/shard_map/ppermute | solution.py:85
  50.8 4.9 %collective-permute-start.10 = (bf16[24,1280]{1,0:T(8,128)(2,1)S(1)}, bf16[24,1280]{1,0:T(8,128)(2,1)S(1)}, u32[]{:S(2)}, u32[]{:S(2)}) collective-permute-start(bf16[24,1280]{1,0:T(8,128)(2,1)S(1)} %get-tuple-element.51), channel_id=1, source_target_pairs={{0,32},{1,33},{2,34},{3,35},{4,36},{5,37},{6,38},{7,39},{8,40},{9,... | collective-permute-start | bytes 184328 | tf_op jit(solution)/shard_map/ppermute | solution.py:85
  55.8 5.8 %collective-permute-start.13 = (bf16[24,1280]{1,0:T(8,128)(2,1)S(1)}, bf16[24,1280]{1,0:T(8,128)(2,1)S(1)}, u32[]{:S(2)}, u32[]{:S(2)}) collective-permute-start(bf16[24,1280]{1,0:T(8,128)(2,1)S(1)} %add_two.5.own), channel_id=1, source_target_pairs={{0,192},{1,193},{2,194},{3,195},{4,196},{5,197},{6,198},{7,199},{8... | collective-permute-start | bytes 184328 | tf_op jit(solution)/shard_map/ppermute | solution.py:85
  59.4 5.2 %collective-permute-start.12 = (bf16[24,1280]{1,0:T(8,128)(2,1)S(1)}, bf16[24,1280]{1,0:T(8,128)(2,1)S(1)}, u32[]{:S(2)}, u32[]{:S(2)}) collective-permute-start(bf16[24,1280]{1,0:T(8,128)(2,1)S(1)} %add_two.5.own), channel_id=1, source_target_pairs={{0,128},{1,129},{2,130},{3,131},{4,132},{5,133},{6,134},{7,135},{8... | collective-permute-start | bytes 184328 | tf_op jit(solution)/shard_map/ppermute | solution.py:85
  59.5 5.2 %collective-permute-start.11 = (bf16[24,1280]{1,0:T(8,128)(2,1)S(1)}, bf16[24,1280]{1,0:T(8,128)(2,1)S(1)}, u32[]{:S(2)}, u32[]{:S(2)}) collective-permute-start(bf16[24,1280]{1,0:T(8,128)(2,1)S(1)} %add_two.5.own), channel_id=1, source_target_pairs={{0,64},{1,65},{2,66},{3,67},{4,68},{5,69},{6,70},{7,71},{8,72},{9,... | collective-permute-start | bytes 184328 | tf_op jit(solution)/shard_map/ppermute | solution.py:85
  65.4 5.2 %collective-permute-start.14 = (bf16[24,1280]{1,0:T(8,128)(2,1)S(1)}, bf16[24,1280]{1,0:T(8,128)(2,1)S(1)}, u32[]{:S(2)}, u32[]{:S(2)}) collective-permute-start(bf16[24,1280]{1,0:T(8,128)(2,1)S(1)} %get-tuple-element.60.refs_0_), channel_id=1, source_target_pairs={{0,144},{1,145},{2,146},{3,147},{4,148},{5,149},{6,150},{7,151},{8... | collective-permute-start | bytes 184328 | tf_op jit(solution)/shard_map/ppermute | solution.py:85
  70.6 5.0 %collective-permute-start.17 = (bf16[48,1280]{1,0:T(8,128)(2,1)S(1)}, bf16[48,1280]{1,0:T(8,128)(2,1)S(1)}, u32[]{:S(2)}, u32[]{:S(2)}) collective-permute-start(bf16[48,1280]{1,0:T(8,128)(2,1)S(1)} %join.2.refs_0_), channel_id=1, source_target_pairs={{0,4},{1,5},{2,6},{3,7},{4,8},{5,9},{6,10},{7,11},{8,12},{9,13},{1... | collective-permute-start | bytes 368648 | tf_op jit(solution)/shard_map/ppermute | solution.py:85
  72.0 6.0 %collective-permute-start.16 = (bf16[48,1280]{1,0:T(8,128)(2,1)S(1)}, bf16[48,1280]{1,0:T(8,128)(2,1)S(1)}, u32[]{:S(2)}, u32[]{:S(2)}) collective-permute-start(bf16[48,1280]{1,0:T(8,128)(2,1)S(1)} %join.2.refs_0_), channel_id=1, source_target_pairs={{0,8},{1,9},{2,10},{3,11},{4,12},{5,13},{6,14},{7,15},{8,0},{9,1},... | collective-permute-start | bytes 368648 | tf_op jit(solution)/shard_map/ppermute | solution.py:85
  74.5 3.9 %collective-permute-start.15 = (bf16[48,1280]{1,0:T(8,128)(2,1)S(1)}, bf16[48,1280]{1,0:T(8,128)(2,1)S(1)}, u32[]{:S(2)}, u32[]{:S(2)}) collective-permute-start(bf16[48,1280]{1,0:T(8,128)(2,1)S(1)} %join.2.refs_0_), channel_id=1, source_target_pairs={{0,12},{1,13},{2,14},{3,15},{4,0},{5,1},{6,2},{7,3},{8,4},{9,5},{1... | collective-permute-start | bytes 368648 | tf_op jit(solution)/shard_map/ppermute | solution.py:85
  78.4 9.3 %collective-permute-start.23 = (bf16[192,1280]{1,0:T(8,128)(2,1)S(1)}, bf16[192,1280]{1,0:T(8,128)(2,1)S(1)}, u32[]{:S(2)}, u32[]{:S(2)}) collective-permute-start(bf16[192,1280]{1,0:T(8,128)(2,1)S(1)} %join.3.refs_0_), channel_id=1, source_target_pairs={{0,1},{1,2},{2,3},{3,0},{4,5},{5,6},{6,7},{7,4},{8,9},{9,10},{10,1... | collective-permute-start | bytes 1474568 | tf_op jit(solution)/shard_map/ppermute | solution.py:85
  78.9 15.1 %collective-permute-start.21 = (bf16[192,1280]{1,0:T(8,128)(2,1)S(1)}, bf16[192,1280]{1,0:T(8,128)(2,1)S(1)}, u32[]{:S(2)}, u32[]{:S(2)}) collective-permute-start(bf16[192,1280]{1,0:T(8,128)(2,1)S(1)} %join.3.refs_0_), channel_id=1, source_target_pairs={{0,2},{1,3},{2,0},{3,1},{4,6},{5,7},{6,4},{7,5},{8,10},{9,11},{10,... | collective-permute-start | bytes 1474568 | tf_op jit(solution)/shard_map/ppermute | solution.py:85
  82.2 15.4 %collective-permute-start.19 = (bf16[192,1280]{1,0:T(8,128)(2,1)S(1)}, bf16[192,1280]{1,0:T(8,128)(2,1)S(1)}, u32[]{:S(2)}, u32[]{:S(2)}) collective-permute-start(bf16[192,1280]{1,0:T(8,128)(2,1)S(1)} %join.3.refs_0_), channel_id=1, source_target_pairs={{0,3},{1,0},{2,1},{3,2},{4,7},{5,4},{6,5},{7,6},{8,11},{9,8},{10,9... | collective-permute-start | bytes 1474568 | tf_op jit(solution)/shard_map/ppermute | solution.py:85
  82.2 17.9 %collective-permute-start.18 = (bf16[192,1280]{1,0:T(8,128)(2,1)S(1)}, bf16[192,1280]{1,0:T(8,128)(2,1)S(1)}, u32[]{:S(2)}, u32[]{:S(2)}) collective-permute-start(bf16[192,1280]{1,0:T(8,128)(2,1)S(1)} %join.3.refs_0_), channel_id=1, source_target_pairs={{0,32},{1,33},{2,34},{3,35},{4,36},{5,37},{6,38},{7,39},{8,40},{9,... | collective-permute-start | bytes 1474568 | tf_op jit(solution)/shard_map/ppermute | solution.py:85
  87.7 12.5 %collective-permute-start.24 = (bf16[192,1280]{1,0:T(8,128)(2,1)S(1)}, bf16[192,1280]{1,0:T(8,128)(2,1)S(1)}, u32[]{:S(2)}, u32[]{:S(2)}) collective-permute-start(bf16[192,1280]{1,0:T(8,128)(2,1)S(1)} %collective-permute-done.23.refs_3_), channel_id=1, source_target_pairs={{0,32},{1,33},{2,34},{3,35},{4,36},{5,37},{6,38},{7,39},{8,40},{9,... | collective-permute-start | bytes 1474568 | tf_op jit(solution)/shard_map/ppermute | solution.py:85
  94.0 6.2 %collective-permute-start.22 = (bf16[192,1280]{1,0:T(8,128)(2,1)S(1)}, bf16[192,1280]{1,0:T(8,128)(2,1)S(1)}, u32[]{:S(2)}, u32[]{:S(2)}) collective-permute-start(bf16[192,1280]{1,0:T(8,128)(2,1)S(1)} %collective-permute-done.21.refs_2_), channel_id=1, source_target_pairs={{0,32},{1,33},{2,34},{3,35},{4,36},{5,37},{6,38},{7,39},{8,40},{9,... | collective-permute-start | bytes 1474568 | tf_op jit(solution)/shard_map/ppermute | solution.py:85
  97.7 2.5 %collective-permute-start.20 = (bf16[192,1280]{1,0:T(8,128)(2,1)S(1)}, bf16[192,1280]{1,0:T(8,128)(2,1)S(1)}, u32[]{:S(2)}, u32[]{:S(2)}) collective-permute-start(bf16[192,1280]{1,0:T(8,128)(2,1)S(1)} %collective-permute-done.19.refs_1_), channel_id=1, source_target_pairs={{0,32},{1,33},{2,34},{3,35},{4,36},{5,37},{6,38},{7,39},{8,40},{9,... | collective-permute-start | bytes 1474568 | tf_op jit(solution)/shard_map/ppermute | solution.py:85

commit v3 on v2

--- a/solution.py
+++ b/solution.py
@@ -31,6 +31,8 @@
 BF16 = jnp.bfloat16
 F32 = jnp.float32
 TILE = 1280
+READ_TILE = 1280
+AHEAD = 2
 AXES = ("island", "fsdp")
 SCALARS = pl.BlockSpec(memory_space=pltpu.SMEM)
 IN_VMEM = pl.BlockSpec(memory_space=pltpu.VMEM)
@@ -57,8 +59,8 @@
 def along_a(step):
     def target(zlo, core, zhi, y, x):
         if core == 0:
-            return (zlo, core, zhi, y, (x + step) % RING)
-        return (zlo, core, zhi, (y + step) % RING, x)
+            return (zlo, core, zhi, y, (x - step) % RING)
+        return (zlo, core, zhi, (y - step) % RING, x)
 
     return device_pairs(target)
 
@@ -66,8 +68,8 @@
 def along_b(step):
     def target(zlo, core, zhi, y, x):
         if core == 0:
-            return (zlo, core, zhi, (y + step) % RING, x)
-        return (zlo, core, zhi, y, (x + step) % RING)
+            return (zlo, core, zhi, (y - step) % RING, x)
+        return (zlo, core, zhi, y, (x - step) % RING)
 
     return device_pairs(target)
 
@@ -101,38 +103,76 @@
     r = rest - OWN * jz
     first = jnp.where(core == 0, ja, jb)
     second = jnp.where(core == 0, jb, ja)
-    col = x.astype(F32) + first
-    col = jnp.where(col >= RING, col - RING, col)
-    line = y.astype(F32) + second
-    line = jnp.where(line >= RING, line - RING, line)
+    col = x.astype(F32) - first
+    col = jnp.where(col < 0, col + RING, col)
+    line = y.astype(F32) - second
+    line = jnp.where(line < 0, line + RING, line)
     half = jnp.where(zhi == 0, jz, 1.0 - jz)
     return ((half * RING + line) * RING + col) * OWN + r
 
 
-def order_kernel(pos, up_ref, *outs):
+def far_kernel(pos, up_ref, act_ref, left, right, up_sides, up_own, act_held, up_held, up_arrived, arrived):
+    up_copy = pltpu.make_async_copy(up_ref.at[0], up_held, up_arrived)
+    up_copy.start()
+    tiles = act_ref.shape[2] // READ_TILE
+    copies = []
+    for t in range(tiles):
+        cols = pl.ds(t * READ_TILE, READ_TILE)
+        copies.append(
+            pltpu.make_async_copy(act_ref.at[0, :, cols], act_held.at[0, :, cols], arrived.at[t])
+        )
+    for copy in copies[:AHEAD]:
+        copy.start()
     _, core, zhi, y, x = coordinates(pos)
     wanted = fragment_row(lax.broadcasted_iota(jnp.int32, (ROWS, 1), 0), core, zhi, y, x)
     column = lax.broadcasted_iota(jnp.int32, (ROWS, ROWS), 1).astype(F32)
     pick = jnp.where(column == wanted, 1.0, 0.0).astype(BF16)
+    up_copy.wait()
     up_rows = lax.dot_general(
-        pick, up_ref[0], (((1,), (1,)), ((), ())), preferred_element_type=F32
+        pick, up_held[...], (((1,), (1,)), ((), ())), preferred_element_type=F32
     ).astype(BF16)
-    outs[0][...] = up_rows[:QUARTER]
-    outs[1][:QUARTER] = up_rows[QUARTER : 2 * QUARTER]
-    outs[1][QUARTER:] = up_rows[3 * QUARTER :]
-    outs[2][...] = up_rows[2 * QUARTER : 3 * QUARTER]
-
-
-def order_rows(pos, upstream):
-    tokens = upstream.shape[1]
-    return pl.pallas_call(
-        order_kernel,
-        in_specs=[SCALARS, IN_VMEM],
-        out_specs=[IN_VMEM] * 3,
-        out_shape=[jax.ShapeDtypeStruct((n * QUARTER, tokens), BF16) for n in (1, 2, 1)],
-        compiler_params=SMALL,
-        name="order_rows",
-    )(pos, upstream)
+    up_own[...] = up_rows[:QUARTER]
+    up_sides[:QUARTER] = up_rows[QUARTER : 2 * QUARTER]
+    up_sides[QUARTER:] = up_rows[3 * QUARTER :]
+    up_far = up_rows[2 * QUARTER : 3 * QUARTER]
+    half = left.shape[1]
+    for t in range(tiles):
+        copies[t].wait()
+        if t + AHEAD < tiles:
+            copies[t + AHEAD].start()
+        first = t * READ_TILE
+        out, place = (left, first) if first < half else (right, first - half)
+        out[:, place : place + READ_TILE] = jnp.dot(
+            up_far, act_held[0, :, first : first + READ_TILE], preferred_element_type=F32
+        ).astype(BF16)
+
+
+def far_product(pos, upstream, activations):
+    _, tokens, width = activations.shape
+    shapes = [
+        (QUARTER, width // 2),
+        (QUARTER, width // 2),
+        (2 * QUARTER, tokens),
+        (QUARTER, tokens),
+        activations.shape,
+    ]
+    return pl.pallas_call(
+        far_kernel,
+        in_specs=[SCALARS, IN_HBM, IN_HBM],
+        out_specs=[IN_VMEM] * 5,
+        out_shape=[jax.ShapeDtypeStruct(shape, BF16) for shape in shapes],
+        scratch_shapes=[
+            pltpu.VMEM((tokens, ROWS), BF16),
+            pltpu.SemaphoreType.DMA,
+            pltpu.SemaphoreType.DMA((width // READ_TILE,)),
+        ],
+        compiler_params=SMALL,
+        name="far_product",
+    )(
+        pos,
+        pltpu.with_memory_space_constraint(upstream, pltpu.HBM),
+        pltpu.with_memory_space_constraint(activations, pltpu.HBM),
+    )
 
 
 def product_kernel(up_rows, act_ref, *outs):
@@ -364,21 +404,22 @@
 
     def fill(a_is_x, x_here, k, b):
         source = pl.ds(pl.multiple_of(k * share + b * BLOCK, BLOCK), BLOCK)
-        rows = [p[:, source].astype(F32) for p in parts]
-        for jz in range(2):
-            half = zhi if jz == 0 else 1 - zhi
-            for h in range(2):
-                target = pl.ds(pl.multiple_of((2 * h + k) * share + b * BLOCK, BLOCK), BLOCK)
-                for q in range(RING):
-                    pieces = []
-                    for x_there in range(RING):
-                        jx = (x_there - x_here) % RING
-                        ja, jb = (jx, q) if a_is_x else (q, jx)
-                        first = (jb * 2 + jz) * PAIR + h * OWN
-                        pieces.append(rows[ja][first : first + OWN])
-                    line = half * RING + lax.rem(y + q, RING)
-                    start = pl.multiple_of(line * line_rows, 16)
-                    held[pl.ds(start, line_rows), target] = jnp.concatenate(pieces, axis=0).astype(BF16)
+        for q in range(RING):
+            rows = []
+            for x_there in range(RING):
+                jx = (x_here - x_there) % RING
+                ja, jb = (jx, q) if a_is_x else (q, jx)
+                rows.append(parts[ja][jb * 2 * PAIR : (jb + 1) * 2 * PAIR, source].astype(F32))
+            for jz in range(2):
+                half = zhi if jz == 0 else 1 - zhi
+                line = half * RING + lax.rem(y + RING - q, RING)
+                start = pl.multiple_of(line * line_rows, 16)
+                for h in range(2):
+                    first = jz * PAIR + h * OWN
+                    target = pl.ds(pl.multiple_of((2 * h + k) * share + b * BLOCK, BLOCK), BLOCK)
+                    held[pl.ds(start, line_rows), target] = jnp.concatenate(
+                        [r[first : first + OWN] for r in rows], axis=0
+                    ).astype(BF16)
 
     copies = []
     for k in range(2):
@@ -421,8 +462,7 @@
 def local(activations, upstream, drift, first_moment, second_moment, outer_base, outer_momentum, scale_exponents):
     pos = lax.axis_index(AXES).astype(jnp.int32).reshape(1)
 
-    up_own, up_sides, up_far = order_rows(pos, upstream)
-    far_left, far_right = product(up_far, activations, 2)
+    far_left, far_right, up_sides, up_own, activations = far_product(pos, upstream, activations)
     via_left = send(far_left, along_a(1))
     via_right = send(far_right, along_a(-1))
     next_left, next_right, last_left, last_right = product(up_sides, activations, 2)

time: 102 us -> 101 us (level)
  local copies, waits for them, and re-layouts: 6.77 us -> 1.66 us
  Pallas kernels: 11.8 us -> 15.1 us
  waiting for transfers between devices: 29.1 us -> 32.3 us
  starting transfers between devices: 53.3 us -> 51.1 us
    pallas_call x1, Pallas kernels: 0.72 us -> 5.84 us  [far_product(): pl.pallas_call(far_kernel, in_specs=[SCALARS, IN_HBM, IN_HBM], out_specs=...]
    unnamed x21 -> x15, local copies, waits for them, and re-layouts: 5.3 us -> 0.2 us
    ppermute x25, waiting for transfers between devices: 29.1 us -> 32.3 us  [send(): return lax.ppermute(value, AXES, pairs)]
    ppermute x25, starting transfers between devices: 53.3 us -> 51.1 us  [send(): return lax.ppermute(value, AXES, pairs)]
    pallas_call x3 -> x2, Pallas kernels: 5.78 us -> 4 us  [product(): pl.pallas_call(product_kernel, in_specs=[IN_VMEM, IN_VMEM], out_specs=[IN...]
  transfers between devices with their start and end apart: 25 -> 25, of which waited for: 17 -> 15; matrix products, arithmetic and copies ran while one was open for 2% -> 2% of each run, Pallas kernels for 6% -> 6%
where the time goes in v3:
time: 101 us
  starting transfers between devices  51.1 us (51%)
  waiting for transfers between devices  32.3 us (32%)
  Pallas kernels  15.1 us (15%)
  local copies, waits for them, and re-layouts  1.66 us (2%)
  between operations  1.01 us (1%)
    ppermute x25, starting transfers between devices, send(): return lax.ppermute(value, AXES, pairs)  51.1 us
    ppermute x25, waiting for transfers between devices, send(): return lax.ppermute(value, AXES, pairs)  32.3 us
    pallas_call x1, Pallas kernels, far_product(): pl.pallas_call(far_kernel, in_specs=[SCALARS, IN_HBM, IN_HBM], out_specs=...  5.84 us
    pallas_call x2, Pallas kernels, product(): pl.pallas_call(product_kernel, in_specs=[IN_VMEM, IN_VMEM], out_specs=[IN...  4 us
    pallas_call x2, Pallas kernels, place(): pl.pallas_call(functools.partial(place_kernel, w), in_specs=[SCALARS] + [...  3.18 us
  transfers between devices with their start and end apart: 25, of which 15 were waited for; matrix products, arithmetic and copies ran while one was open for 2% of the time, Pallas kernels for 6%

profile of v3, /device:TPU:1, one launch (start us, length us, event | category | flops | bytes accessed | tf_op | source)
XLA Modules:
  0.0 101.2 jit_solution(8382609198782981521)
XLA Ops:
  0.6 5.8 %far_product.1 = (bf16[96,2560]{1,0:T(8,128)(2,1)S(1)}, bf16[96,2560]{1,0:T(8,128)(2,1)S(1)}, bf16[192,1024]{1,0:T(8,128)(2,1)S(1)}, bf16[96,1024]{1,0:T(8,128)(2,1)S(1)}, bf16[1,1024,5120]{2,1,0:T(8,128)(2,1)S(1)}) custom-call(s32[1]{0:T(128)} %bitcast.pos, bf16[1,1024,384]{2,1,0:T(8,128)(2,1)} %up_ref.1, bf16[1,1024,5120]{2,1,0:T(8,128)(2,1)} %act_ref.1), custom_call_target="tpu_custom_call" | custom-call | tf_op jit(solution)/shard_map/far_product/pallas_call | solution.py:159
  6.5 2.2 %collective-permute-start.4 = (bf16[96,2560]{1,0:T(8,128)(2,1)S(1)}, bf16[96,2560]{1,0:T(8,128)(2,1)S(1)}, u32[]{:S(2)}, u32[]{:S(2)}) collective-permute-start(bf16[96,2560]{1,0:T(8,128)(2,1)S(1)} %get-tuple-element.41), channel_id=1, source_target_pairs={{0,1},{1,2},{2,3},{3,0},{4,5},{5,6},{6,7},{7,4},{8,9},{9,10},{10,1... | collective-permute-start | bytes 1474568 | tf_op jit(solution)/shard_map/ppermute | solution.py:87
  8.7 1.5 %collective-permute-start = (bf16[96,2560]{1,0:T(8,128)(2,1)S(1)}, bf16[96,2560]{1,0:T(8,128)(2,1)S(1)}, u32[]{:S(2)}, u32[]{:S(2)}) collective-permute-start(bf16[96,2560]{1,0:T(8,128)(2,1)S(1)} %get-tuple-element.37), channel_id=1, source_target_pairs={{0,3},{1,0},{2,1},{3,2},{4,7},{5,4},{6,5},{7,6},{8,11},{9,8},{10,9... | collective-permute-start | bytes 1474568 | tf_op jit(solution)/shard_map/ppermute | solution.py:87
  10.2 2.2 %product.3 = (bf16[96,2560]{1,0:T(8,128)(2,1)S(1)}, bf16[96,2560]{1,0:T(8,128)(2,1)S(1)}, bf16[96,2560]{1,0:T(8,128)(2,1)S(1)}, bf16[96,2560]{1,0:T(8,128)(2,1)S(1)}) custom-call(bf16[192,1024]{1,0:T(8,128)(2,1)S(1)} %get-tuple-element.35.up_rows, bf16[1,1024,5120]{2,1,0:T(8,128)(2,1)S(1)} %get-tuple-element.34.act_ref), custom_call_target="tpu_custom_call" | custom-call | flops 2013265920 | bytes 12845056 | tf_op jit(solution)/shard_map/product/pallas_call | solution.py:196
  12.4 0.0 copy-start.3
  12.5 0.0 copy-start.4
  12.5 0.0 copy-start.5
  12.5 0.0 copy-start
  12.5 0.0 copy-start.2
  12.5 0.1 collective-permute-start.2
  12.6 2.7 %collective-permute-start.3 = (bf16[96,2560]{1,0:T(8,128)(2,1)S(1)}, bf16[96,2560]{1,0:T(8,128)(2,1)S(1)}, u32[]{:S(2)}, u32[]{:S(2)}) collective-permute-start(bf16[96,2560]{1,0:T(8,128)(2,1)S(1)} %get-tuple-element.39), channel_id=1, source_target_pairs={{0,3},{1,0},{2,1},{3,2},{4,7},{5,4},{6,5},{7,6},{8,11},{9,8},{10,9... | collective-permute-start | bytes 1474568 | tf_op jit(solution)/shard_map/ppermute | solution.py:87
  15.3 1.4 %collective-permute-done.4.arrived = bf16[96,2560]{1,0:T(8,128)(2,1)S(1)} collective-permute-done((bf16[96,2560]{1,0:T(8,128)(2,1)S(1)}, bf16[96,2560]{1,0:T(8,128)(2,1)S(1)}, u32[]{:S(2)}, u32[]{:S(2)}) %collective-permute-start.4) | collective-permute-done | bytes 491552 | tf_op jit(solution)/shard_map/ppermute | solution.py:87
  16.7 0.1 add_two.4
  16.8 0.1 collective-permute-start.5
  16.9 0.1 add_two.3
  17.0 0.0 copy-start.1
  17.0 2.7 %collective-permute-start.1 = (bf16[96,2560]{1,0:T(8,128)(2,1)S(1)}, bf16[96,2560]{1,0:T(8,128)(2,1)S(1)}, u32[]{:S(2)}, u32[]{:S(2)}) collective-permute-start(bf16[96,2560]{1,0:T(8,128)(2,1)S(1)} %add_two.3), channel_id=1, source_target_pairs={{0,3},{1,0},{2,1},{3,2},{4,7},{5,4},{6,5},{7,6},{8,11},{9,8},{10,9... | collective-permute-start | bytes 1474568 | tf_op jit(solution)/shard_map/ppermute | solution.py:87
  19.7 1.8 %product.2.own = bf16[96,5120]{1,0:T(8,128)(2,1)S(1)} custom-call(bf16[96,1024]{1,0:T(8,128)(2,1)S(1)} %get-tuple-element.33.up_rows, bf16[1,1024,5120]{2,1,0:T(8,128)(2,1)S(1)} %get-tuple-element.34.act_ref), custom_call_target="tpu_custom_call" | custom-call | flops 1006632960 | bytes 11665408 | tf_op jit(solution)/shard_map/product/pallas_call | solution.py:196
  21.5 0.4 collective-permute-done.2.left_two
  21.9 0.0 collective-permute-done.3.right_one
  21.9 5.2 %collective-permute-done.5.right_two = bf16[96,2560]{1,0:T(8,128)(2,1)S(1)} collective-permute-done((bf16[96,2560]{1,0:T(8,128)(2,1)S(1)}, bf16[96,2560]{1,0:T(8,128)(2,1)S(1)}, u32[]{:S(2)}, u32[]{:S(2)}) %collective-permute-start.5) | collective-permute-done | bytes 491552 | tf_op jit(solution)/shard_map/ppermute | solution.py:87
  27.2 0.0 collective-permute-done.1.left_one
  27.2 0.4 add_first.1
  27.6 2.8 %collective-permute-start.6 = (bf16[24,5120]{1,0:T(8,128)(2,1)S(1)}, bf16[24,5120]{1,0:T(8,128)(2,1)S(1)}, u32[]{:S(2)}, u32[]{:S(2)}) collective-permute-start(bf16[24,5120]{1,0:T(8,128)(2,1)S(1)} %get-tuple-element.43), channel_id=1, source_target_pairs={{0,8},{1,9},{2,10},{3,11},{4,12},{5,13},{6,14},{7,15},{8,0},{9,1},... | collective-permute-start | bytes 737288 | tf_op jit(solution)/shard_map/ppermute | solution.py:87
  30.4 0.9 collective-permute-start.7
  31.3 0.6 collective-permute-start.8
  31.9 2.3 %collective-permute-done.6.one = bf16[24,5120]{1,0:T(8,128)(2,1)S(1)} collective-permute-done((bf16[24,5120]{1,0:T(8,128)(2,1)S(1)}, bf16[24,5120]{1,0:T(8,128)(2,1)S(1)}, u32[]{:S(2)}, u32[]{:S(2)}) %collective-permute-start.6) | collective-permute-done | bytes 245792 | tf_op jit(solution)/shard_map/ppermute | solution.py:87
  34.2 3.0 %collective-permute-done.7.two = bf16[24,5120]{1,0:T(8,128)(2,1)S(1)} collective-permute-done((bf16[24,5120]{1,0:T(8,128)(2,1)S(1)}, bf16[24,5120]{1,0:T(8,128)(2,1)S(1)}, u32[]{:S(2)}, u32[]{:S(2)}) %collective-permute-start.7) | collective-permute-done | bytes 245792 | tf_op jit(solution)/shard_map/ppermute | solution.py:87
  37.2 0.6 collective-permute-done.8.three
  37.8 0.1 add_second.1
  37.9 6.7 %collective-permute-start.9 = (bf16[24,2560]{1,0:T(8,128)(2,1)S(1)}, bf16[24,2560]{1,0:T(8,128)(2,1)S(1)}, u32[]{:S(2)}, u32[]{:S(2)}) collective-permute-start(bf16[24,2560]{1,0:T(8,128)(2,1)S(1)} %get-tuple-element.47), channel_id=1, source_target_pairs={{0,16},{1,17},{2,18},{3,19},{4,20},{5,21},{6,22},{7,23},{8,24},{9,... | collective-permute-start | bytes 368648 | tf_op jit(solution)/shard_map/ppermute | solution.py:87
  44.6 0.1 copy.22.drift
  44.7 0.1 copy.23.first
  44.8 0.1 copy.24.second
  44.8 2.2 %collective-permute-done.9.arrived = bf16[24,2560]{1,0:T(8,128)(2,1)S(1)} collective-permute-done((bf16[24,2560]{1,0:T(8,128)(2,1)S(1)}, bf16[24,2560]{1,0:T(8,128)(2,1)S(1)}, u32[]{:S(2)}, u32[]{:S(2)}) %collective-permute-start.9) | collective-permute-done | bytes 122912 | tf_op jit(solution)/shard_map/ppermute | solution.py:87
  47.0 0.6 inner_step.1
  47.6 5.4 %collective-permute-start.10 = (bf16[24,1280]{1,0:T(8,128)(2,1)S(1)}, bf16[24,1280]{1,0:T(8,128)(2,1)S(1)}, u32[]{:S(2)}, u32[]{:S(2)}) collective-permute-start(bf16[24,1280]{1,0:T(8,128)(2,1)S(1)} %get-tuple-element.51), channel_id=1, source_target_pairs={{0,32},{1,33},{2,34},{3,35},{4,36},{5,37},{6,38},{7,39},{8,40},{9,... | collective-permute-start | bytes 184328 | tf_op jit(solution)/shard_map/ppermute | solution.py:87
  53.0 0.9 collective-permute-done.10.arrived
  53.9 0.7 collective-permute-start.11
  54.7 1.9 %collective-permute-start.12 = (bf16[24,1280]{1,0:T(8,128)(2,1)S(1)}, bf16[24,1280]{1,0:T(8,128)(2,1)S(1)}, u32[]{:S(2)}, u32[]{:S(2)}) collective-permute-start(bf16[24,1280]{1,0:T(8,128)(2,1)S(1)} %add_two.5.own), channel_id=1, source_target_pairs={{0,128},{1,129},{2,130},{3,131},{4,132},{5,133},{6,134},{7,135},{8... | collective-permute-start | bytes 184328 | tf_op jit(solution)/shard_map/ppermute | solution.py:87
  56.6 1.0 %collective-permute-start.13 = (bf16[24,1280]{1,0:T(8,128)(2,1)S(1)}, bf16[24,1280]{1,0:T(8,128)(2,1)S(1)}, u32[]{:S(2)}, u32[]{:S(2)}) collective-permute-start(bf16[24,1280]{1,0:T(8,128)(2,1)S(1)} %add_two.5.own), channel_id=1, source_target_pairs={{0,192},{1,193},{2,194},{3,195},{4,196},{5,197},{6,198},{7,199},{8... | collective-permute-start | bytes 184328 | tf_op jit(solution)/shard_map/ppermute | solution.py:87
  57.6 0.7 reshape.26
  58.3 0.7 reshape.27
  59.0 0.0 collective-permute-done.12.two
  59.1 2.4 %collective-permute-done.13.three = bf16[24,1280]{1,0:T(8,128)(2,1)S(1)} collective-permute-done((bf16[24,1280]{1,0:T(8,128)(2,1)S(1)}, bf16[24,1280]{1,0:T(8,128)(2,1)S(1)}, u32[]{:S(2)}, u32[]{:S(2)}) %collective-permute-start.13) | collective-permute-done | bytes 61472 | tf_op jit(solution)/shard_map/ppermute | solution.py:87
  61.4 0.7 outer_step.1
  62.2 5.8 %collective-permute-start.14 = (bf16[24,1280]{1,0:T(8,128)(2,1)S(1)}, bf16[24,1280]{1,0:T(8,128)(2,1)S(1)}, u32[]{:S(2)}, u32[]{:S(2)}) collective-permute-start(bf16[24,1280]{1,0:T(8,128)(2,1)S(1)} %get-tuple-element.60.refs_0_), channel_id=1, source_target_pairs={{0,144},{1,145},{2,146},{3,147},{4,148},{5,149},{6,150},{7,151},{8... | collective-permute-start | bytes 184328 | tf_op jit(solution)/shard_map/ppermute | solution.py:87
  68.0 1.7 %collective-permute-done.14.refs_1_ = bf16[24,1280]{1,0:T(8,128)(2,1)S(1)} collective-permute-done((bf16[24,1280]{1,0:T(8,128)(2,1)S(1)}, bf16[24,1280]{1,0:T(8,128)(2,1)S(1)}, u32[]{:S(2)}, u32[]{:S(2)}) %collective-permute-start.14) | collective-permute-done | bytes 61472 | tf_op jit(solution)/shard_map/ppermute | solution.py:87
  69.6 1.3 %collective-permute-start.15 = (bf16[48,1280]{1,0:T(8,128)(2,1)S(1)}, bf16[48,1280]{1,0:T(8,128)(2,1)S(1)}, u32[]{:S(2)}, u32[]{:S(2)}) collective-permute-start(bf16[48,1280]{1,0:T(8,128)(2,1)S(1)} %join.2.refs_0_), channel_id=1, source_target_pairs={{0,4},{1,5},{2,6},{3,7},{4,8},{5,9},{6,10},{7,11},{8,12},{9,13},{1... | collective-permute-start | bytes 368648 | tf_op jit(solution)/shard_map/ppermute | solution.py:87
  70.9 3.4 %collective-permute-start.16 = (bf16[48,1280]{1,0:T(8,128)(2,1)S(1)}, bf16[48,1280]{1,0:T(8,128)(2,1)S(1)}, u32[]{:S(2)}, u32[]{:S(2)}) collective-permute-start(bf16[48,1280]{1,0:T(8,128)(2,1)S(1)} %join.2.refs_0_), channel_id=1, source_target_pairs={{0,8},{1,9},{2,10},{3,11},{4,12},{5,13},{6,14},{7,15},{8,0},{9,1},... | collective-permute-start | bytes 368648 | tf_op jit(solution)/shard_map/ppermute | solution.py:87
  74.3 1.1 %collective-permute-done.15.refs_1_ = bf16[48,1280]{1,0:T(8,128)(2,1)S(1)} collective-permute-done((bf16[48,1280]{1,0:T(8,128)(2,1)S(1)}, bf16[48,1280]{1,0:T(8,128)(2,1)S(1)}, u32[]{:S(2)}, u32[]{:S(2)}) %collective-permute-start.15) | collective-permute-done | bytes 122912 | tf_op jit(solution)/shard_map/ppermute | solution.py:87
  75.4 2.8 %collective-permute-done.16.refs_2_ = bf16[48,1280]{1,0:T(8,128)(2,1)S(1)} collective-permute-done((bf16[48,1280]{1,0:T(8,128)(2,1)S(1)}, bf16[48,1280]{1,0:T(8,128)(2,1)S(1)}, u32[]{:S(2)}, u32[]{:S(2)}) %collective-permute-start.16) | collective-permute-done | bytes 122912 | tf_op jit(solution)/shard_map/ppermute | solution.py:87
  78.1 0.1 collective-permute-done.17.refs_3_
  78.3 0.1 collective-permute-start.19
  78.4 2.1 %collective-permute-start.21 = (bf16[192,1280]{1,0:T(8,128)(2,1)S(1)}, bf16[192,1280]{1,0:T(8,128)(2,1)S(1)}, u32[]{:S(2)}, u32[]{:S(2)}) collective-permute-start(bf16[192,1280]{1,0:T(8,128)(2,1)S(1)} %join.3.refs_0_), channel_id=1, source_target_pairs={{0,2},{1,3},{2,0},{3,1},{4,6},{5,7},{6,4},{7,5},{8,10},{9,11},{10,... | collective-permute-start | bytes 1474568 | tf_op jit(solution)/shard_map/ppermute | solution.py:87
  80.6 0.8 collective-permute-start.23
  81.4 3.9 %collective-permute-start.18 = (bf16[192,1280]{1,0:T(8,128)(2,1)S(1)}, bf16[192,1280]{1,0:T(8,128)(2,1)S(1)}, u32[]{:S(2)}, u32[]{:S(2)}) collective-permute-start(bf16[192,1280]{1,0:T(8,128)(2,1)S(1)} %join.3.refs_0_), channel_id=1, source_target_pairs={{0,32},{1,33},{2,34},{3,35},{4,36},{5,37},{6,38},{7,39},{8,40},{9,... | collective-permute-start | bytes 1474568 | tf_op jit(solution)/shard_map/ppermute | solution.py:87
  85.3 7.6 %collective-permute-done.19.refs_1_ = bf16[192,1280]{1,0:T(8,128)(2,1)S(1)} collective-permute-done((bf16[192,1280]{1,0:T(8,128)(2,1)S(1)}, bf16[192,1280]{1,0:T(8,128)(2,1)S(1)}, u32[]{:S(2)}, u32[]{:S(2)}) %collective-permute-start.19) | collective-permute-done | bytes 491552 | tf_op jit(solution)/shard_map/ppermute | solution.py:87
  92.9 0.0 collective-permute-start.20
  92.9 4.4 %collective-permute-start.22 = (bf16[192,1280]{1,0:T(8,128)(2,1)S(1)}, bf16[192,1280]{1,0:T(8,128)(2,1)S(1)}, u32[]{:S(2)}, u32[]{:S(2)}) collective-permute-start(bf16[192,1280]{1,0:T(8,128)(2,1)S(1)} %collective-permute-done.21.refs_2_), channel_id=1, source_target_pairs={{0,32},{1,33},{2,34},{3,35},{4,36},{5,37},{6,38},{7,39},{8,40},{9,... | collective-permute-start | bytes 1474568 | tf_op jit(solution)/shard_map/ppermute | solution.py:87
  97.3 0.0 collective-permute-start.24
  97.3 1.6 %place.2.refs_4_ = bf16[384,5120]{1,0:T(8,128)(2,1)} custom-call(s32[1]{0:T(128)} %bitcast.pos, bf16[192,1280]{1,0:T(8,128)(2,1)S(1)} %join.3.refs_0_, bf16[192,1280]{1,0:T(8,128)(2,1)S(1)} %collective-permute-done.19.refs_1_, bf16[192,1280]{1,0:T(8,128)(2,1)S(1)} %collective-permute-done.21.refs_2_, bf16[192,1280]{1,0:T(8,128)(2,1)S(1)} %collective-permute-done.23.refs_3_), custom_call_target="tpu_custom_call" | custom-call | tf_op jit(solution)/shard_map/place/pallas_call | solution.py:450
  98.9 0.6 collective-permute-done.24.refs_3_
  99.5 1.6 %place.3 = bf16[384,5120]{1,0:T(8,128)(2,1)} custom-call(s32[1]{0:T(128)} %bitcast.pos, bf16[192,1280]{1,0:T(8,128)(2,1)S(1)} %collective-permute-done.18.refs_0_, bf16[192,1280]{1,0:T(8,128)(2,1)S(1)} %collective-permute-done.20.refs_1_, bf16[192,1280]{1,0:T(8,128)(2,1)S(1)} %collective-permute-done.22.refs_2_, ...), custom_call_target="tpu_custom_call", output_to_operand_aliasing={{}: (5, {})} | custom-call | tf_op jit(solution)/shard_map/place/pallas_call | solution.py:450
  (17 shorter events, 0.1 us)
Async XLA Ops:
  6.5 10.2 %collective-permute-start.4 = (bf16[96,2560]{1,0:T(8,128)(2,1)S(1)}, bf16[96,2560]{1,0:T(8,128)(2,1)S(1)}, u32[]{:S(2)}, u32[]{:S(2)}) collective-permute-start(bf16[96,2560]{1,0:T(8,128)(2,1)S(1)} %get-tuple-element.41), channel_id=1, source_target_pairs={{0,1},{1,2},{2,3},{3,0},{4,5},{5,6},{6,7},{7,4},{8,9},{9,10},{10,1... | collective-permute-start | bytes 1474568 | tf_op jit(solution)/shard_map/ppermute | solution.py:87
  8.7 8.2 %collective-permute-start = (bf16[96,2560]{1,0:T(8,128)(2,1)S(1)}, bf16[96,2560]{1,0:T(8,128)(2,1)S(1)}, u32[]{:S(2)}, u32[]{:S(2)}) collective-permute-start(bf16[96,2560]{1,0:T(8,128)(2,1)S(1)} %get-tuple-element.37), channel_id=1, source_target_pairs={{0,3},{1,0},{2,1},{3,2},{4,7},{5,4},{6,5},{7,6},{8,11},{9,8},{10,9... | collective-permute-start | bytes 1474568 | tf_op jit(solution)/shard_map/ppermute | solution.py:87
  12.4 32.2 %copy-start.3 = (f32[1,12,5120]{2,0,1:T(1,128)S(1)}, f32[1,12,5120]{2,0,1:T(1,128)}, u32[]{:S(2)}) copy-start(f32[1,12,5120]{2,0,1:T(1,128)} %param.10) | copy-start | bytes 737284
  12.5 32.2 %copy-start.4 = (f32[1,12,5120]{2,0,1:T(1,128)S(1)}, f32[1,12,5120]{2,0,1:T(1,128)}, u32[]{:S(2)}) copy-start(f32[1,12,5120]{2,0,1:T(1,128)} %param.11) | copy-start | bytes 737284
  12.5 32.3 %copy-start.5 = (f32[1,12,5120]{2,0,1:T(1,128)S(1)}, f32[1,12,5120]{2,0,1:T(1,128)}, u32[]{:S(2)}) copy-start(f32[1,12,5120]{2,0,1:T(1,128)} %param.12) | copy-start | bytes 737284
  12.5 34.5 %copy-start = (f32[12,5120]{1,0:T(8,128)S(1)}, f32[12,5120]{1,0:T(8,128)}, u32[]{:S(2)}) copy-start(f32[12,5120]{1,0:T(8,128)} %base.3) | copy-start | bytes 737284
  12.5 34.5 %copy-start.2 = (s32[12,40]{1,0:T(8,128)S(1)}, s32[12,40]{1,0:T(8,128)}, u32[]{:S(2)}) copy-start(s32[12,40]{1,0:T(8,128)} %exponents.1) | copy-start | bytes 5764
  12.5 9.4 %collective-permute-start.2 = (bf16[96,2560]{1,0:T(8,128)(2,1)S(1)}, bf16[96,2560]{1,0:T(8,128)(2,1)S(1)}, u32[]{:S(2)}, u32[]{:S(2)}) collective-permute-start(bf16[96,2560]{1,0:T(8,128)(2,1)S(1)} %get-tuple-element.38), channel_id=1, source_target_pairs={{0,1},{1,2},{2,3},{3,0},{4,5},{5,6},{6,7},{7,4},{8,9},{9,10},{10,1... | collective-permute-start | bytes 1474568 | tf_op jit(solution)/shard_map/ppermute | solution.py:87
  12.6 9.3 %collective-permute-start.3 = (bf16[96,2560]{1,0:T(8,128)(2,1)S(1)}, bf16[96,2560]{1,0:T(8,128)(2,1)S(1)}, u32[]{:S(2)}, u32[]{:S(2)}) collective-permute-start(bf16[96,2560]{1,0:T(8,128)(2,1)S(1)} %get-tuple-element.39), channel_id=1, source_target_pairs={{0,3},{1,0},{2,1},{3,2},{4,7},{5,4},{6,5},{7,6},{8,11},{9,8},{10,9... | collective-permute-start | bytes 1474568 | tf_op jit(solution)/shard_map/ppermute | solution.py:87
  16.8 10.4 %collective-permute-start.5 = (bf16[96,2560]{1,0:T(8,128)(2,1)S(1)}, bf16[96,2560]{1,0:T(8,128)(2,1)S(1)}, u32[]{:S(2)}, u32[]{:S(2)}) collective-permute-start(bf16[96,2560]{1,0:T(8,128)(2,1)S(1)} %add_two.4), channel_id=1, source_target_pairs={{0,1},{1,2},{2,3},{3,0},{4,5},{5,6},{6,7},{7,4},{8,9},{9,10},{10,1... | collective-permute-start | bytes 1474568 | tf_op jit(solution)/shard_map/ppermute | solution.py:87
  17.0 44.4 %copy-start.1 = (f32[12,5120]{1,0:T(8,128)S(1)}, f32[12,5120]{1,0:T(8,128)}, u32[]{:S(2)}) copy-start(f32[12,5120]{1,0:T(8,128)} %momentum.1) | copy-start | bytes 737284
  17.0 10.2 %collective-permute-start.1 = (bf16[96,2560]{1,0:T(8,128)(2,1)S(1)}, bf16[96,2560]{1,0:T(8,128)(2,1)S(1)}, u32[]{:S(2)}, u32[]{:S(2)}) collective-permute-start(bf16[96,2560]{1,0:T(8,128)(2,1)S(1)} %add_two.3), channel_id=1, source_target_pairs={{0,3},{1,0},{2,1},{3,2},{4,7},{5,4},{6,5},{7,6},{8,11},{9,8},{10,9... | collective-permute-start | bytes 1474568 | tf_op jit(solution)/shard_map/ppermute | solution.py:87
  27.6 6.6 %collective-permute-start.6 = (bf16[24,5120]{1,0:T(8,128)(2,1)S(1)}, bf16[24,5120]{1,0:T(8,128)(2,1)S(1)}, u32[]{:S(2)}, u32[]{:S(2)}) collective-permute-start(bf16[24,5120]{1,0:T(8,128)(2,1)S(1)} %get-tuple-element.43), channel_id=1, source_target_pairs={{0,8},{1,9},{2,10},{3,11},{4,12},{5,13},{6,14},{7,15},{8,0},{9,1},... | collective-permute-start | bytes 737288 | tf_op jit(solution)/shard_map/ppermute | solution.py:87
  30.4 6.9 %collective-permute-start.7 = (bf16[24,5120]{1,0:T(8,128)(2,1)S(1)}, bf16[24,5120]{1,0:T(8,128)(2,1)S(1)}, u32[]{:S(2)}, u32[]{:S(2)}) collective-permute-start(bf16[24,5120]{1,0:T(8,128)(2,1)S(1)} %get-tuple-element.44), channel_id=1, source_target_pairs={{0,12},{1,13},{2,14},{3,15},{4,0},{5,1},{6,2},{7,3},{8,4},{9,5},{1... | collective-permute-start | bytes 737288 | tf_op jit(solution)/shard_map/ppermute | solution.py:87
  31.3 6.6 %collective-permute-start.8 = (bf16[24,5120]{1,0:T(8,128)(2,1)S(1)}, bf16[24,5120]{1,0:T(8,128)(2,1)S(1)}, u32[]{:S(2)}, u32[]{:S(2)}) collective-permute-start(bf16[24,5120]{1,0:T(8,128)(2,1)S(1)} %get-tuple-element.45), channel_id=1, source_target_pairs={{0,4},{1,5},{2,6},{3,7},{4,8},{5,9},{6,10},{7,11},{8,12},{9,13},{1... | collective-permute-start | bytes 737288 | tf_op jit(solution)/shard_map/ppermute | solution.py:87
  37.9 9.1 %collective-permute-start.9 = (bf16[24,2560]{1,0:T(8,128)(2,1)S(1)}, bf16[24,2560]{1,0:T(8,128)(2,1)S(1)}, u32[]{:S(2)}, u32[]{:S(2)}) collective-permute-start(bf16[24,2560]{1,0:T(8,128)(2,1)S(1)} %get-tuple-element.47), channel_id=1, source_target_pairs={{0,16},{1,17},{2,18},{3,19},{4,20},{5,21},{6,22},{7,23},{8,24},{9,... | collective-permute-start | bytes 368648 | tf_op jit(solution)/shard_map/ppermute | solution.py:87
  47.6 6.3 %collective-permute-start.10 = (bf16[24,1280]{1,0:T(8,128)(2,1)S(1)}, bf16[24,1280]{1,0:T(8,128)(2,1)S(1)}, u32[]{:S(2)}, u32[]{:S(2)}) collective-permute-start(bf16[24,1280]{1,0:T(8,128)(2,1)S(1)} %get-tuple-element.51), channel_id=1, source_target_pairs={{0,32},{1,33},{2,34},{3,35},{4,36},{5,37},{6,38},{7,39},{8,40},{9,... | collective-permute-start | bytes 184328 | tf_op jit(solution)/shard_map/ppermute | solution.py:87
  53.9 5.1 %collective-permute-start.11 = (bf16[24,1280]{1,0:T(8,128)(2,1)S(1)}, bf16[24,1280]{1,0:T(8,128)(2,1)S(1)}, u32[]{:S(2)}, u32[]{:S(2)}) collective-permute-start(bf16[24,1280]{1,0:T(8,128)(2,1)S(1)} %add_two.5.own), channel_id=1, source_target_pairs={{0,64},{1,65},{2,66},{3,67},{4,68},{5,69},{6,70},{7,71},{8,72},{9,... | collective-permute-start | bytes 184328 | tf_op jit(solution)/shard_map/ppermute | solution.py:87
  54.7 4.4 %collective-permute-start.12 = (bf16[24,1280]{1,0:T(8,128)(2,1)S(1)}, bf16[24,1280]{1,0:T(8,128)(2,1)S(1)}, u32[]{:S(2)}, u32[]{:S(2)}) collective-permute-start(bf16[24,1280]{1,0:T(8,128)(2,1)S(1)} %add_two.5.own), channel_id=1, source_target_pairs={{0,128},{1,129},{2,130},{3,131},{4,132},{5,133},{6,134},{7,135},{8... | collective-permute-start | bytes 184328 | tf_op jit(solution)/shard_map/ppermute | solution.py:87
  56.6 4.9 %collective-permute-start.13 = (bf16[24,1280]{1,0:T(8,128)(2,1)S(1)}, bf16[24,1280]{1,0:T(8,128)(2,1)S(1)}, u32[]{:S(2)}, u32[]{:S(2)}) collective-permute-start(bf16[24,1280]{1,0:T(8,128)(2,1)S(1)} %add_two.5.own), channel_id=1, source_target_pairs={{0,192},{1,193},{2,194},{3,195},{4,196},{5,197},{6,198},{7,199},{8... | collective-permute-start | bytes 184328 | tf_op jit(solution)/shard_map/ppermute | solution.py:87
  62.2 7.5 %collective-permute-start.14 = (bf16[24,1280]{1,0:T(8,128)(2,1)S(1)}, bf16[24,1280]{1,0:T(8,128)(2,1)S(1)}, u32[]{:S(2)}, u32[]{:S(2)}) collective-permute-start(bf16[24,1280]{1,0:T(8,128)(2,1)S(1)} %get-tuple-element.60.refs_0_), channel_id=1, source_target_pairs={{0,144},{1,145},{2,146},{3,147},{4,148},{5,149},{6,150},{7,151},{8... | collective-permute-start | bytes 184328 | tf_op jit(solution)/shard_map/ppermute | solution.py:87
  69.6 5.7 %collective-permute-start.15 = (bf16[48,1280]{1,0:T(8,128)(2,1)S(1)}, bf16[48,1280]{1,0:T(8,128)(2,1)S(1)}, u32[]{:S(2)}, u32[]{:S(2)}) collective-permute-start(bf16[48,1280]{1,0:T(8,128)(2,1)S(1)} %join.2.refs_0_), channel_id=1, source_target_pairs={{0,4},{1,5},{2,6},{3,7},{4,8},{5,9},{6,10},{7,11},{8,12},{9,13},{1... | collective-permute-start | bytes 368648 | tf_op jit(solution)/shard_map/ppermute | solution.py:87
  70.9 7.2 %collective-permute-start.16 = (bf16[48,1280]{1,0:T(8,128)(2,1)S(1)}, bf16[48,1280]{1,0:T(8,128)(2,1)S(1)}, u32[]{:S(2)}, u32[]{:S(2)}) collective-permute-start(bf16[48,1280]{1,0:T(8,128)(2,1)S(1)} %join.2.refs_0_), channel_id=1, source_target_pairs={{0,8},{1,9},{2,10},{3,11},{4,12},{5,13},{6,14},{7,15},{8,0},{9,1},... | collective-permute-start | bytes 368648 | tf_op jit(solution)/shard_map/ppermute | solution.py:87
  74.3 4.0 %collective-permute-start.17 = (bf16[48,1280]{1,0:T(8,128)(2,1)S(1)}, bf16[48,1280]{1,0:T(8,128)(2,1)S(1)}, u32[]{:S(2)}, u32[]{:S(2)}) collective-permute-start(bf16[48,1280]{1,0:T(8,128)(2,1)S(1)} %join.2.refs_0_), channel_id=1, source_target_pairs={{0,12},{1,13},{2,14},{3,15},{4,0},{5,1},{6,2},{7,3},{8,4},{9,5},{1... | collective-permute-start | bytes 368648 | tf_op jit(solution)/shard_map/ppermute | solution.py:87
  78.3 14.5 %collective-permute-start.19 = (bf16[192,1280]{1,0:T(8,128)(2,1)S(1)}, bf16[192,1280]{1,0:T(8,128)(2,1)S(1)}, u32[]{:S(2)}, u32[]{:S(2)}) collective-permute-start(bf16[192,1280]{1,0:T(8,128)(2,1)S(1)} %join.3.refs_0_), channel_id=1, source_target_pairs={{0,1},{1,2},{2,3},{3,0},{4,5},{5,6},{6,7},{7,4},{8,9},{9,10},{10,1... | collective-permute-start | bytes 1474568 | tf_op jit(solution)/shard_map/ppermute | solution.py:87
  78.4 14.4 %collective-permute-start.21 = (bf16[192,1280]{1,0:T(8,128)(2,1)S(1)}, bf16[192,1280]{1,0:T(8,128)(2,1)S(1)}, u32[]{:S(2)}, u32[]{:S(2)}) collective-permute-start(bf16[192,1280]{1,0:T(8,128)(2,1)S(1)} %join.3.refs_0_), channel_id=1, source_target_pairs={{0,2},{1,3},{2,0},{3,1},{4,6},{5,7},{6,4},{7,5},{8,10},{9,11},{10,... | collective-permute-start | bytes 1474568 | tf_op jit(solution)/shard_map/ppermute | solution.py:87
  80.6 16.7 %collective-permute-start.23 = (bf16[192,1280]{1,0:T(8,128)(2,1)S(1)}, bf16[192,1280]{1,0:T(8,128)(2,1)S(1)}, u32[]{:S(2)}, u32[]{:S(2)}) collective-permute-start(bf16[192,1280]{1,0:T(8,128)(2,1)S(1)} %join.3.refs_0_), channel_id=1, source_target_pairs={{0,3},{1,0},{2,1},{3,2},{4,7},{5,4},{6,5},{7,6},{8,11},{9,8},{10,9... | collective-permute-start | bytes 1474568 | tf_op jit(solution)/shard_map/ppermute | solution.py:87
  81.4 17.5 %collective-permute-start.18 = (bf16[192,1280]{1,0:T(8,128)(2,1)S(1)}, bf16[192,1280]{1,0:T(8,128)(2,1)S(1)}, u32[]{:S(2)}, u32[]{:S(2)}) collective-permute-start(bf16[192,1280]{1,0:T(8,128)(2,1)S(1)} %join.3.refs_0_), channel_id=1, source_target_pairs={{0,32},{1,33},{2,34},{3,35},{4,36},{5,37},{6,38},{7,39},{8,40},{9,... | collective-permute-start | bytes 1474568 | tf_op jit(solution)/shard_map/ppermute | solution.py:87
  92.9 6.0 %collective-permute-start.20 = (bf16[192,1280]{1,0:T(8,128)(2,1)S(1)}, bf16[192,1280]{1,0:T(8,128)(2,1)S(1)}, u32[]{:S(2)}, u32[]{:S(2)}) collective-permute-start(bf16[192,1280]{1,0:T(8,128)(2,1)S(1)} %collective-permute-done.19.refs_1_), channel_id=1, source_target_pairs={{0,32},{1,33},{2,34},{3,35},{4,36},{5,37},{6,38},{7,39},{8,40},{9,... | collective-permute-start | bytes 1474568 | tf_op jit(solution)/shard_map/ppermute | solution.py:87
  92.9 6.0 %collective-permute-start.22 = (bf16[192,1280]{1,0:T(8,128)(2,1)S(1)}, bf16[192,1280]{1,0:T(8,128)(2,1)S(1)}, u32[]{:S(2)}, u32[]{:S(2)}) collective-permute-start(bf16[192,1280]{1,0:T(8,128)(2,1)S(1)} %collective-permute-done.21.refs_2_), channel_id=1, source_target_pairs={{0,32},{1,33},{2,34},{3,35},{4,36},{5,37},{6,38},{7,39},{8,40},{9,... | collective-permute-start | bytes 1474568 | tf_op jit(solution)/shard_map/ppermute | solution.py:87
  97.3 2.2 %collective-permute-start.24 = (bf16[192,1280]{1,0:T(8,128)(2,1)S(1)}, bf16[192,1280]{1,0:T(8,128)(2,1)S(1)}, u32[]{:S(2)}, u32[]{:S(2)}) collective-permute-start(bf16[192,1280]{1,0:T(8,128)(2,1)S(1)} %collective-permute-done.23.refs_3_), channel_id=1, source_target_pairs={{0,32},{1,33},{2,34},{3,35},{4,36},{5,37},{6,38},{7,39},{8,40},{9,... | collective-permute-start | bytes 1474568 | tf_op jit(solution)/shard_map/ppermute | solution.py:87

commit v4 on v3

--- a/solution.py
+++ b/solution.py
@@ -31,7 +31,7 @@
 BF16 = jnp.bfloat16
 F32 = jnp.float32
 TILE = 1280
-READ_TILE = 1280
+READ_TILE = 2560
 AHEAD = 2
 AXES = ("island", "fsdp")
 SCALARS = pl.BlockSpec(memory_space=pltpu.SMEM)
@@ -336,7 +336,7 @@
     )(own, arrived)
 
 
-def outer_kernel(pos, own, one, two, three, unscale, momentum, base, momentum_out, base_out, fragment):
+def outer_kernel(pos, own, three, two, one, unscale, momentum, base, momentum_out, base_out, fragment):
     zlo, core, _, _, _ = coordinates(pos)
     share = own.shape[1] // 2
 
@@ -395,7 +395,7 @@
 
 
 def place_kernel(w, pos, *refs):
-    parts = refs[:4]
+    parts = refs[0], refs[1], refs[3], refs[2]
     out, held, sent = refs[-3:]
     _, core, zhi, y, x = coordinates(pos)
     whose = core if w == 0 else 1 - core
@@ -479,7 +479,7 @@
         pos, keep, arrived, drift, first_moment, second_moment, outer_base, scale_exponents
     )
     coded = add_two(own, send(away, OTHER_CORE))
-    parts = [send(coded, other_zlo(k)) for k in (1, 2, 3)]
+    parts = [send(coded, other_zlo(k)) for k in (3, 2, 1)]
     flat = (first_new.size // BLOCK, BLOCK)
     first_flat, second_flat, *parts = lax.optimization_barrier(
         (first_new.reshape(flat), second_new.reshape(flat), *parts)
@@ -492,7 +492,9 @@
     plane = {j: send(piece, along_a(-j)) for j in (2, 1, 3)}
     mine = [piece, plane[1], plane[2], plane[3]]
     theirs = [send(m, OTHER_CORE) for m in mine]
-    fragment = place(1, pos, theirs, place(0, pos, mine))
+    order = (0, 1, 3, 2)
+    fragment = place(0, pos, [mine[j] for j in order])
+    fragment = place(1, pos, [theirs[j] for j in order], fragment)
     return (
         first_flat.reshape(first_new.shape),
         second_flat.reshape(second_new.shape),

time: 101 us -> 98.4 us (0.974)
  starting transfers between devices: 51.1 us -> 48.4 us
    ppermute x25, starting transfers between devices: 51.1 us -> 48.4 us  [send(): return lax.ppermute(value, AXES, pairs)]
  transfers between devices with their start and end apart: 25 -> 25, of which waited for: 15 -> 14; matrix products, arithmetic and copies ran while one was open for 2% -> 2% of each run, Pallas kernels for 6% -> 6%
where the time goes in v4:
time: 98.4 us; the launch traced here: 98.3 us
  starting transfers between devices  48.4 us (49%)
  waiting for transfers between devices  32.7 us (33%)
  Pallas kernels  14.6 us (15%)
  local copies, waits for them, and re-layouts  1.66 us (2%)
  between operations  1.02 us (1%)
    ppermute x25, starting transfers between devices, send(): return lax.ppermute(value, AXES, pairs)  48.4 us
    ppermute x25, waiting for transfers between devices, send(): return lax.ppermute(value, AXES, pairs)  32.7 us
    pallas_call x1, Pallas kernels, far_product(): pl.pallas_call(far_kernel, in_specs=[SCALARS, IN_HBM, IN_HBM], out_specs=...  5.28 us
    pallas_call x2, Pallas kernels, product(): pl.pallas_call(product_kernel, in_specs=[IN_VMEM, IN_VMEM], out_specs=[IN...  4 us
    pallas_call x2, Pallas kernels, place(): pl.pallas_call(functools.partial(place_kernel, w), in_specs=[SCALARS] + [...  3.2 us
  transfers between devices with their start and end apart: 25, of which 14 were waited for; matrix products, arithmetic and copies ran while one was open for 2% of the time, Pallas kernels for 6%

profile of v4, /device:TPU:1, one launch (start us, length us, event | category | flops | bytes accessed | tf_op | source)
XLA Modules:
  0.0 98.3 jit_solution(10687678851379495029)
XLA Ops:
  0.6 5.3 %far_product.1 = (bf16[96,2560]{1,0:T(8,128)(2,1)S(1)}, bf16[96,2560]{1,0:T(8,128)(2,1)S(1)}, bf16[192,1024]{1,0:T(8,128)(2,1)S(1)}, bf16[96,1024]{1,0:T(8,128)(2,1)S(1)}, bf16[1,1024,5120]{2,1,0:T(8,128)(2,1)S(1)}) custom-call(s32[1]{0:T(128)} %bitcast.pos, bf16[1,1024,384]{2,1,0:T(8,128)(2,1)} %up_ref.1, bf16[1,1024,5120]{2,1,0:T(8,128)(2,1)} %act_ref.1), custom_call_target="tpu_custom_call" | custom-call | tf_op jit(solution)/shard_map/far_product/pallas_call | solution.py:159
  5.9 2.2 %collective-permute-start.4 = (bf16[96,2560]{1,0:T(8,128)(2,1)S(1)}, bf16[96,2560]{1,0:T(8,128)(2,1)S(1)}, u32[]{:S(2)}, u32[]{:S(2)}) collective-permute-start(bf16[96,2560]{1,0:T(8,128)(2,1)S(1)} %get-tuple-element.41), channel_id=1, source_target_pairs={{0,1},{1,2},{2,3},{3,0},{4,5},{5,6},{6,7},{7,4},{8,9},{9,10},{10,1... | collective-permute-start | bytes 1474568 | tf_op jit(solution)/shard_map/ppermute | solution.py:87
  8.1 1.5 %collective-permute-start = (bf16[96,2560]{1,0:T(8,128)(2,1)S(1)}, bf16[96,2560]{1,0:T(8,128)(2,1)S(1)}, u32[]{:S(2)}, u32[]{:S(2)}) collective-permute-start(bf16[96,2560]{1,0:T(8,128)(2,1)S(1)} %get-tuple-element.37), channel_id=1, source_target_pairs={{0,3},{1,0},{2,1},{3,2},{4,7},{5,4},{6,5},{7,6},{8,11},{9,8},{10,9... | collective-permute-start | bytes 1474568 | tf_op jit(solution)/shard_map/ppermute | solution.py:87
  9.7 2.2 %product.3 = (bf16[96,2560]{1,0:T(8,128)(2,1)S(1)}, bf16[96,2560]{1,0:T(8,128)(2,1)S(1)}, bf16[96,2560]{1,0:T(8,128)(2,1)S(1)}, bf16[96,2560]{1,0:T(8,128)(2,1)S(1)}) custom-call(bf16[192,1024]{1,0:T(8,128)(2,1)S(1)} %get-tuple-element.35.up_rows, bf16[1,1024,5120]{2,1,0:T(8,128)(2,1)S(1)} %get-tuple-element.34.act_ref), custom_call_target="tpu_custom_call" | custom-call | flops 2013265920 | bytes 12845056 | tf_op jit(solution)/shard_map/product/pallas_call | solution.py:196
  11.9 0.0 copy-start.3
  11.9 0.0 copy-start.4
  11.9 0.0 copy-start.5
  11.9 0.0 copy-start
  11.9 0.0 copy-start.2
  11.9 0.1 collective-permute-start.2
  12.0 2.7 %collective-permute-start.3 = (bf16[96,2560]{1,0:T(8,128)(2,1)S(1)}, bf16[96,2560]{1,0:T(8,128)(2,1)S(1)}, u32[]{:S(2)}, u32[]{:S(2)}) collective-permute-start(bf16[96,2560]{1,0:T(8,128)(2,1)S(1)} %get-tuple-element.39), channel_id=1, source_target_pairs={{0,3},{1,0},{2,1},{3,2},{4,7},{5,4},{6,5},{7,6},{8,11},{9,8},{10,9... | collective-permute-start | bytes 1474568 | tf_op jit(solution)/shard_map/ppermute | solution.py:87
  14.7 1.4 %collective-permute-done.4.arrived = bf16[96,2560]{1,0:T(8,128)(2,1)S(1)} collective-permute-done((bf16[96,2560]{1,0:T(8,128)(2,1)S(1)}, bf16[96,2560]{1,0:T(8,128)(2,1)S(1)}, u32[]{:S(2)}, u32[]{:S(2)}) %collective-permute-start.4) | collective-permute-done | bytes 491552 | tf_op jit(solution)/shard_map/ppermute | solution.py:87
  16.1 0.1 add_two.4
  16.2 0.1 collective-permute-start.5
  16.3 0.0 collective-permute-done.arrived
  16.3 0.1 add_two.3
  16.4 0.0 copy-start.1
  16.4 2.7 %collective-permute-start.1 = (bf16[96,2560]{1,0:T(8,128)(2,1)S(1)}, bf16[96,2560]{1,0:T(8,128)(2,1)S(1)}, u32[]{:S(2)}, u32[]{:S(2)}) collective-permute-start(bf16[96,2560]{1,0:T(8,128)(2,1)S(1)} %add_two.3), channel_id=1, source_target_pairs={{0,3},{1,0},{2,1},{3,2},{4,7},{5,4},{6,5},{7,6},{8,11},{9,8},{10,9... | collective-permute-start | bytes 1474568 | tf_op jit(solution)/shard_map/ppermute | solution.py:87
  19.2 1.8 %product.2.own = bf16[96,5120]{1,0:T(8,128)(2,1)S(1)} custom-call(bf16[96,1024]{1,0:T(8,128)(2,1)S(1)} %get-tuple-element.33.up_rows, bf16[1,1024,5120]{2,1,0:T(8,128)(2,1)S(1)} %get-tuple-element.34.act_ref), custom_call_target="tpu_custom_call" | custom-call | flops 1006632960 | bytes 11665408 | tf_op jit(solution)/shard_map/product/pallas_call | solution.py:196
  21.0 0.4 collective-permute-done.2.left_two
  21.4 0.0 collective-permute-done.3.right_one
  21.4 5.2 %collective-permute-done.5.right_two = bf16[96,2560]{1,0:T(8,128)(2,1)S(1)} collective-permute-done((bf16[96,2560]{1,0:T(8,128)(2,1)S(1)}, bf16[96,2560]{1,0:T(8,128)(2,1)S(1)}, u32[]{:S(2)}, u32[]{:S(2)}) %collective-permute-start.5) | collective-permute-done | bytes 491552 | tf_op jit(solution)/shard_map/ppermute | solution.py:87
  26.6 0.0 collective-permute-done.1.left_one
  26.6 0.4 add_first.1
  27.0 2.8 %collective-permute-start.6 = (bf16[24,5120]{1,0:T(8,128)(2,1)S(1)}, bf16[24,5120]{1,0:T(8,128)(2,1)S(1)}, u32[]{:S(2)}, u32[]{:S(2)}) collective-permute-start(bf16[24,5120]{1,0:T(8,128)(2,1)S(1)} %get-tuple-element.43), channel_id=1, source_target_pairs={{0,8},{1,9},{2,10},{3,11},{4,12},{5,13},{6,14},{7,15},{8,0},{9,1},... | collective-permute-start | bytes 737288 | tf_op jit(solution)/shard_map/ppermute | solution.py:87
  29.8 0.9 collective-permute-start.7
  30.7 0.6 collective-permute-start.8
  31.3 2.3 %collective-permute-done.6.one = bf16[24,5120]{1,0:T(8,128)(2,1)S(1)} collective-permute-done((bf16[24,5120]{1,0:T(8,128)(2,1)S(1)}, bf16[24,5120]{1,0:T(8,128)(2,1)S(1)}, u32[]{:S(2)}, u32[]{:S(2)}) %collective-permute-start.6) | collective-permute-done | bytes 245792 | tf_op jit(solution)/shard_map/ppermute | solution.py:87
  33.6 3.0 %collective-permute-done.7.two = bf16[24,5120]{1,0:T(8,128)(2,1)S(1)} collective-permute-done((bf16[24,5120]{1,0:T(8,128)(2,1)S(1)}, bf16[24,5120]{1,0:T(8,128)(2,1)S(1)}, u32[]{:S(2)}, u32[]{:S(2)}) %collective-permute-start.7) | collective-permute-done | bytes 245792 | tf_op jit(solution)/shard_map/ppermute | solution.py:87
  36.7 0.6 collective-permute-done.8.three
  37.2 0.1 add_second.1
  37.4 6.7 %collective-permute-start.9 = (bf16[24,2560]{1,0:T(8,128)(2,1)S(1)}, bf16[24,2560]{1,0:T(8,128)(2,1)S(1)}, u32[]{:S(2)}, u32[]{:S(2)}) collective-permute-start(bf16[24,2560]{1,0:T(8,128)(2,1)S(1)} %get-tuple-element.47), channel_id=1, source_target_pairs={{0,16},{1,17},{2,18},{3,19},{4,20},{5,21},{6,22},{7,23},{8,24},{9,... | collective-permute-start | bytes 368648 | tf_op jit(solution)/shard_map/ppermute | solution.py:87
  44.1 0.1 copy.22.drift
  44.1 0.1 copy.23.first
  44.2 0.1 copy.24.second
  44.3 2.2 %collective-permute-done.9.arrived = bf16[24,2560]{1,0:T(8,128)(2,1)S(1)} collective-permute-done((bf16[24,2560]{1,0:T(8,128)(2,1)S(1)}, bf16[24,2560]{1,0:T(8,128)(2,1)S(1)}, u32[]{:S(2)}, u32[]{:S(2)}) %collective-permute-start.9) | collective-permute-done | bytes 122912 | tf_op jit(solution)/shard_map/ppermute | solution.py:87
  46.5 0.6 inner_step.1
  47.1 5.4 %collective-permute-start.10 = (bf16[24,1280]{1,0:T(8,128)(2,1)S(1)}, bf16[24,1280]{1,0:T(8,128)(2,1)S(1)}, u32[]{:S(2)}, u32[]{:S(2)}) collective-permute-start(bf16[24,1280]{1,0:T(8,128)(2,1)S(1)} %get-tuple-element.51), channel_id=1, source_target_pairs={{0,32},{1,33},{2,34},{3,35},{4,36},{5,37},{6,38},{7,39},{8,40},{9,... | collective-permute-start | bytes 184328 | tf_op jit(solution)/shard_map/ppermute | solution.py:87
  52.5 0.9 collective-permute-done.10.arrived
  53.4 2.3 %collective-permute-start.11 = (bf16[24,1280]{1,0:T(8,128)(2,1)S(1)}, bf16[24,1280]{1,0:T(8,128)(2,1)S(1)}, u32[]{:S(2)}, u32[]{:S(2)}) collective-permute-start(bf16[24,1280]{1,0:T(8,128)(2,1)S(1)} %add_two.5.own), channel_id=1, source_target_pairs={{0,192},{1,193},{2,194},{3,195},{4,196},{5,197},{6,198},{7,199},{8... | collective-permute-start | bytes 184328 | tf_op jit(solution)/shard_map/ppermute | solution.py:87
  55.7 1.3 %collective-permute-start.13 = (bf16[24,1280]{1,0:T(8,128)(2,1)S(1)}, bf16[24,1280]{1,0:T(8,128)(2,1)S(1)}, u32[]{:S(2)}, u32[]{:S(2)}) collective-permute-start(bf16[24,1280]{1,0:T(8,128)(2,1)S(1)} %add_two.5.own), channel_id=1, source_target_pairs={{0,64},{1,65},{2,66},{3,67},{4,68},{5,69},{6,70},{7,71},{8,72},{9,... | collective-permute-start | bytes 184328 | tf_op jit(solution)/shard_map/ppermute | solution.py:87
  57.0 0.7 reshape.26
  57.8 0.7 reshape.27
  58.5 0.0 collective-permute-done.11.three
  58.5 3.4 %collective-permute-done.12.two = bf16[24,1280]{1,0:T(8,128)(2,1)S(1)} collective-permute-done((bf16[24,1280]{1,0:T(8,128)(2,1)S(1)}, bf16[24,1280]{1,0:T(8,128)(2,1)S(1)}, u32[]{:S(2)}, u32[]{:S(2)}) %collective-permute-start.12) | collective-permute-done | bytes 61472 | tf_op jit(solution)/shard_map/ppermute | solution.py:87
  61.9 0.0 collective-permute-done.13.one
  61.9 0.7 outer_step.1
  62.6 3.0 %collective-permute-start.14 = (bf16[24,1280]{1,0:T(8,128)(2,1)S(1)}, bf16[24,1280]{1,0:T(8,128)(2,1)S(1)}, u32[]{:S(2)}, u32[]{:S(2)}) collective-permute-start(bf16[24,1280]{1,0:T(8,128)(2,1)S(1)} %get-tuple-element.60.refs_0_), channel_id=1, source_target_pairs={{0,144},{1,145},{2,146},{3,147},{4,148},{5,149},{6,150},{7,151},{8... | collective-permute-start | bytes 184328 | tf_op jit(solution)/shard_map/ppermute | solution.py:87
  65.7 2.2 %collective-permute-done.14.refs_1_ = bf16[24,1280]{1,0:T(8,128)(2,1)S(1)} collective-permute-done((bf16[24,1280]{1,0:T(8,128)(2,1)S(1)}, bf16[24,1280]{1,0:T(8,128)(2,1)S(1)}, u32[]{:S(2)}, u32[]{:S(2)}) %collective-permute-start.14) | collective-permute-done | bytes 61472 | tf_op jit(solution)/shard_map/ppermute | solution.py:87
  67.9 1.2 %collective-permute-start.15 = (bf16[48,1280]{1,0:T(8,128)(2,1)S(1)}, bf16[48,1280]{1,0:T(8,128)(2,1)S(1)}, u32[]{:S(2)}, u32[]{:S(2)}) collective-permute-start(bf16[48,1280]{1,0:T(8,128)(2,1)S(1)} %join.2.refs_0_), channel_id=1, source_target_pairs={{0,4},{1,5},{2,6},{3,7},{4,8},{5,9},{6,10},{7,11},{8,12},{9,13},{1... | collective-permute-start | bytes 368648 | tf_op jit(solution)/shard_map/ppermute | solution.py:87
  69.1 3.0 %collective-permute-start.16 = (bf16[48,1280]{1,0:T(8,128)(2,1)S(1)}, bf16[48,1280]{1,0:T(8,128)(2,1)S(1)}, u32[]{:S(2)}, u32[]{:S(2)}) collective-permute-start(bf16[48,1280]{1,0:T(8,128)(2,1)S(1)} %join.2.refs_0_), channel_id=1, source_target_pairs={{0,8},{1,9},{2,10},{3,11},{4,12},{5,13},{6,14},{7,15},{8,0},{9,1},... | collective-permute-start | bytes 368648 | tf_op jit(solution)/shard_map/ppermute | solution.py:87
  72.1 0.4 collective-permute-start.17
  72.4 0.7 collective-permute-done.15.refs_1_
  73.1 2.8 %collective-permute-done.16.refs_2_ = bf16[48,1280]{1,0:T(8,128)(2,1)S(1)} collective-permute-done((bf16[48,1280]{1,0:T(8,128)(2,1)S(1)}, bf16[48,1280]{1,0:T(8,128)(2,1)S(1)}, u32[]{:S(2)}, u32[]{:S(2)}) %collective-permute-start.16) | collective-permute-done | bytes 122912 | tf_op jit(solution)/shard_map/ppermute | solution.py:87
  75.9 0.1 collective-permute-done.17.refs_3_
  76.1 0.1 collective-permute-start.19
  76.2 2.7 %collective-permute-start.21 = (bf16[192,1280]{1,0:T(8,128)(2,1)S(1)}, bf16[192,1280]{1,0:T(8,128)(2,1)S(1)}, u32[]{:S(2)}, u32[]{:S(2)}) collective-permute-start(bf16[192,1280]{1,0:T(8,128)(2,1)S(1)} %join.3.refs_0_), channel_id=1, source_target_pairs={{0,3},{1,0},{2,1},{3,2},{4,7},{5,4},{6,5},{7,6},{8,11},{9,8},{10,9... | collective-permute-start | bytes 1474568 | tf_op jit(solution)/shard_map/ppermute | solution.py:87
  78.9 0.4 collective-permute-start.23
  79.3 4.1 %collective-permute-start.18 = (bf16[192,1280]{1,0:T(8,128)(2,1)S(1)}, bf16[192,1280]{1,0:T(8,128)(2,1)S(1)}, u32[]{:S(2)}, u32[]{:S(2)}) collective-permute-start(bf16[192,1280]{1,0:T(8,128)(2,1)S(1)} %join.3.refs_0_), channel_id=1, source_target_pairs={{0,32},{1,33},{2,34},{3,35},{4,36},{5,37},{6,38},{7,39},{8,40},{9,... | collective-permute-start | bytes 1474568 | tf_op jit(solution)/shard_map/ppermute | solution.py:87
  83.3 7.3 %collective-permute-done.19.refs_1_ = bf16[192,1280]{1,0:T(8,128)(2,1)S(1)} collective-permute-done((bf16[192,1280]{1,0:T(8,128)(2,1)S(1)}, bf16[192,1280]{1,0:T(8,128)(2,1)S(1)}, u32[]{:S(2)}, u32[]{:S(2)}) %collective-permute-start.19) | collective-permute-done | bytes 491552 | tf_op jit(solution)/shard_map/ppermute | solution.py:87
  90.7 2.9 %collective-permute-start.22 = (bf16[192,1280]{1,0:T(8,128)(2,1)S(1)}, bf16[192,1280]{1,0:T(8,128)(2,1)S(1)}, u32[]{:S(2)}, u32[]{:S(2)}) collective-permute-start(bf16[192,1280]{1,0:T(8,128)(2,1)S(1)} %collective-permute-done.21.refs_2_), channel_id=1, source_target_pairs={{0,32},{1,33},{2,34},{3,35},{4,36},{5,37},{6,38},{7,39},{8,40},{9,... | collective-permute-start | bytes 1474568 | tf_op jit(solution)/shard_map/ppermute | solution.py:87
  93.5 1.4 %collective-permute-start.24 = (bf16[192,1280]{1,0:T(8,128)(2,1)S(1)}, bf16[192,1280]{1,0:T(8,128)(2,1)S(1)}, u32[]{:S(2)}, u32[]{:S(2)}) collective-permute-start(bf16[192,1280]{1,0:T(8,128)(2,1)S(1)} %collective-permute-done.23.refs_3_), channel_id=1, source_target_pairs={{0,32},{1,33},{2,34},{3,35},{4,36},{5,37},{6,38},{7,39},{8,40},{9,... | collective-permute-start | bytes 1474568 | tf_op jit(solution)/shard_map/ppermute | solution.py:87
  94.9 1.6 %place.2.refs_4_ = bf16[384,5120]{1,0:T(8,128)(2,1)} custom-call(s32[1]{0:T(128)} %bitcast.pos, bf16[192,1280]{1,0:T(8,128)(2,1)S(1)} %join.3.refs_0_, bf16[192,1280]{1,0:T(8,128)(2,1)S(1)} %collective-permute-done.19.refs_1_, bf16[192,1280]{1,0:T(8,128)(2,1)S(1)} %collective-permute-done.21.refs_2_, bf16[192,1280]{1,0:T(8,128)(2,1)S(1)} %collective-permute-done.23.refs_3_), custom_call_target="tpu_custom_call" | custom-call | tf_op jit(solution)/shard_map/place/pallas_call | solution.py:450
  96.5 1.6 %place.3 = bf16[384,5120]{1,0:T(8,128)(2,1)} custom-call(s32[1]{0:T(128)} %bitcast.pos, bf16[192,1280]{1,0:T(8,128)(2,1)S(1)} %collective-permute-done.18.refs_0_, bf16[192,1280]{1,0:T(8,128)(2,1)S(1)} %collective-permute-done.20.refs_1_, bf16[192,1280]{1,0:T(8,128)(2,1)S(1)} %collective-permute-done.22.refs_2_, ...), custom_call_target="tpu_custom_call", output_to_operand_aliasing={{}: (5, {})} | custom-call | tf_op jit(solution)/shard_map/place/pallas_call | solution.py:450
  (17 shorter events, 0.1 us)
Async XLA Ops:
  5.9 10.2 %collective-permute-start.4 = (bf16[96,2560]{1,0:T(8,128)(2,1)S(1)}, bf16[96,2560]{1,0:T(8,128)(2,1)S(1)}, u32[]{:S(2)}, u32[]{:S(2)}) collective-permute-start(bf16[96,2560]{1,0:T(8,128)(2,1)S(1)} %get-tuple-element.41), channel_id=1, source_target_pairs={{0,1},{1,2},{2,3},{3,0},{4,5},{5,6},{6,7},{7,4},{8,9},{9,10},{10,1... | collective-permute-start | bytes 1474568 | tf_op jit(solution)/shard_map/ppermute | solution.py:87
  8.1 8.2 %collective-permute-start = (bf16[96,2560]{1,0:T(8,128)(2,1)S(1)}, bf16[96,2560]{1,0:T(8,128)(2,1)S(1)}, u32[]{:S(2)}, u32[]{:S(2)}) collective-permute-start(bf16[96,2560]{1,0:T(8,128)(2,1)S(1)} %get-tuple-element.37), channel_id=1, source_target_pairs={{0,3},{1,0},{2,1},{3,2},{4,7},{5,4},{6,5},{7,6},{8,11},{9,8},{10,9... | collective-permute-start | bytes 1474568 | tf_op jit(solution)/shard_map/ppermute | solution.py:87
  11.9 32.2 %copy-start.3 = (f32[1,12,5120]{2,0,1:T(1,128)S(1)}, f32[1,12,5120]{2,0,1:T(1,128)}, u32[]{:S(2)}) copy-start(f32[1,12,5120]{2,0,1:T(1,128)} %param.10) | copy-start | bytes 737284
  11.9 32.2 %copy-start.4 = (f32[1,12,5120]{2,0,1:T(1,128)S(1)}, f32[1,12,5120]{2,0,1:T(1,128)}, u32[]{:S(2)}) copy-start(f32[1,12,5120]{2,0,1:T(1,128)} %param.11) | copy-start | bytes 737284
  11.9 32.3 %copy-start.5 = (f32[1,12,5120]{2,0,1:T(1,128)S(1)}, f32[1,12,5120]{2,0,1:T(1,128)}, u32[]{:S(2)}) copy-start(f32[1,12,5120]{2,0,1:T(1,128)} %param.12) | copy-start | bytes 737284
  11.9 34.5 %copy-start = (f32[12,5120]{1,0:T(8,128)S(1)}, f32[12,5120]{1,0:T(8,128)}, u32[]{:S(2)}) copy-start(f32[12,5120]{1,0:T(8,128)} %base.3) | copy-start | bytes 737284
  11.9 34.5 %copy-start.2 = (s32[12,40]{1,0:T(8,128)S(1)}, s32[12,40]{1,0:T(8,128)}, u32[]{:S(2)}) copy-start(s32[12,40]{1,0:T(8,128)} %exponents.1) | copy-start | bytes 5764
  11.9 9.4 %collective-permute-start.2 = (bf16[96,2560]{1,0:T(8,128)(2,1)S(1)}, bf16[96,2560]{1,0:T(8,128)(2,1)S(1)}, u32[]{:S(2)}, u32[]{:S(2)}) collective-permute-start(bf16[96,2560]{1,0:T(8,128)(2,1)S(1)} %get-tuple-element.38), channel_id=1, source_target_pairs={{0,1},{1,2},{2,3},{3,0},{4,5},{5,6},{6,7},{7,4},{8,9},{9,10},{10,1... | collective-permute-start | bytes 1474568 | tf_op jit(solution)/shard_map/ppermute | solution.py:87
  12.0 9.3 %collective-permute-start.3 = (bf16[96,2560]{1,0:T(8,128)(2,1)S(1)}, bf16[96,2560]{1,0:T(8,128)(2,1)S(1)}, u32[]{:S(2)}, u32[]{:S(2)}) collective-permute-start(bf16[96,2560]{1,0:T(8,128)(2,1)S(1)} %get-tuple-element.39), channel_id=1, source_target_pairs={{0,3},{1,0},{2,1},{3,2},{4,7},{5,4},{6,5},{7,6},{8,11},{9,8},{10,9... | collective-permute-start | bytes 1474568 | tf_op jit(solution)/shard_map/ppermute | solution.py:87
  16.2 10.4 %collective-permute-start.5 = (bf16[96,2560]{1,0:T(8,128)(2,1)S(1)}, bf16[96,2560]{1,0:T(8,128)(2,1)S(1)}, u32[]{:S(2)}, u32[]{:S(2)}) collective-permute-start(bf16[96,2560]{1,0:T(8,128)(2,1)S(1)} %add_two.4), channel_id=1, source_target_pairs={{0,1},{1,2},{2,3},{3,0},{4,5},{5,6},{6,7},{7,4},{8,9},{9,10},{10,1... | collective-permute-start | bytes 1474568 | tf_op jit(solution)/shard_map/ppermute | solution.py:87
  16.4 45.5 %copy-start.1 = (f32[12,5120]{1,0:T(8,128)S(1)}, f32[12,5120]{1,0:T(8,128)}, u32[]{:S(2)}) copy-start(f32[12,5120]{1,0:T(8,128)} %momentum.1) | copy-start | bytes 737284
  16.4 10.2 %collective-permute-start.1 = (bf16[96,2560]{1,0:T(8,128)(2,1)S(1)}, bf16[96,2560]{1,0:T(8,128)(2,1)S(1)}, u32[]{:S(2)}, u32[]{:S(2)}) collective-permute-start(bf16[96,2560]{1,0:T(8,128)(2,1)S(1)} %add_two.3), channel_id=1, source_target_pairs={{0,3},{1,0},{2,1},{3,2},{4,7},{5,4},{6,5},{7,6},{8,11},{9,8},{10,9... | collective-permute-start | bytes 1474568 | tf_op jit(solution)/shard_map/ppermute | solution.py:87
  27.0 6.6 %collective-permute-start.6 = (bf16[24,5120]{1,0:T(8,128)(2,1)S(1)}, bf16[24,5120]{1,0:T(8,128)(2,1)S(1)}, u32[]{:S(2)}, u32[]{:S(2)}) collective-permute-start(bf16[24,5120]{1,0:T(8,128)(2,1)S(1)} %get-tuple-element.43), channel_id=1, source_target_pairs={{0,8},{1,9},{2,10},{3,11},{4,12},{5,13},{6,14},{7,15},{8,0},{9,1},... | collective-permute-start | bytes 737288 | tf_op jit(solution)/shard_map/ppermute | solution.py:87
  29.8 6.9 %collective-permute-start.7 = (bf16[24,5120]{1,0:T(8,128)(2,1)S(1)}, bf16[24,5120]{1,0:T(8,128)(2,1)S(1)}, u32[]{:S(2)}, u32[]{:S(2)}) collective-permute-start(bf16[24,5120]{1,0:T(8,128)(2,1)S(1)} %get-tuple-element.44), channel_id=1, source_target_pairs={{0,12},{1,13},{2,14},{3,15},{4,0},{5,1},{6,2},{7,3},{8,4},{9,5},{1... | collective-permute-start | bytes 737288 | tf_op jit(solution)/shard_map/ppermute | solution.py:87
  30.7 6.6 %collective-permute-start.8 = (bf16[24,5120]{1,0:T(8,128)(2,1)S(1)}, bf16[24,5120]{1,0:T(8,128)(2,1)S(1)}, u32[]{:S(2)}, u32[]{:S(2)}) collective-permute-start(bf16[24,5120]{1,0:T(8,128)(2,1)S(1)} %get-tuple-element.45), channel_id=1, source_target_pairs={{0,4},{1,5},{2,6},{3,7},{4,8},{5,9},{6,10},{7,11},{8,12},{9,13},{1... | collective-permute-start | bytes 737288 | tf_op jit(solution)/shard_map/ppermute | solution.py:87
  37.4 9.1 %collective-permute-start.9 = (bf16[24,2560]{1,0:T(8,128)(2,1)S(1)}, bf16[24,2560]{1,0:T(8,128)(2,1)S(1)}, u32[]{:S(2)}, u32[]{:S(2)}) collective-permute-start(bf16[24,2560]{1,0:T(8,128)(2,1)S(1)} %get-tuple-element.47), channel_id=1, source_target_pairs={{0,16},{1,17},{2,18},{3,19},{4,20},{5,21},{6,22},{7,23},{8,24},{9,... | collective-permute-start | bytes 368648 | tf_op jit(solution)/shard_map/ppermute | solution.py:87
  47.1 6.3 %collective-permute-start.10 = (bf16[24,1280]{1,0:T(8,128)(2,1)S(1)}, bf16[24,1280]{1,0:T(8,128)(2,1)S(1)}, u32[]{:S(2)}, u32[]{:S(2)}) collective-permute-start(bf16[24,1280]{1,0:T(8,128)(2,1)S(1)} %get-tuple-element.51), channel_id=1, source_target_pairs={{0,32},{1,33},{2,34},{3,35},{4,36},{5,37},{6,38},{7,39},{8,40},{9,... | collective-permute-start | bytes 184328 | tf_op jit(solution)/shard_map/ppermute | solution.py:87
  53.4 5.1 %collective-permute-start.11 = (bf16[24,1280]{1,0:T(8,128)(2,1)S(1)}, bf16[24,1280]{1,0:T(8,128)(2,1)S(1)}, u32[]{:S(2)}, u32[]{:S(2)}) collective-permute-start(bf16[24,1280]{1,0:T(8,128)(2,1)S(1)} %add_two.5.own), channel_id=1, source_target_pairs={{0,192},{1,193},{2,194},{3,195},{4,196},{5,197},{6,198},{7,199},{8... | collective-permute-start | bytes 184328 | tf_op jit(solution)/shard_map/ppermute | solution.py:87
  55.7 6.2 %collective-permute-start.12 = (bf16[24,1280]{1,0:T(8,128)(2,1)S(1)}, bf16[24,1280]{1,0:T(8,128)(2,1)S(1)}, u32[]{:S(2)}, u32[]{:S(2)}) collective-permute-start(bf16[24,1280]{1,0:T(8,128)(2,1)S(1)} %add_two.5.own), channel_id=1, source_target_pairs={{0,128},{1,129},{2,130},{3,131},{4,132},{5,133},{6,134},{7,135},{8... | collective-permute-start | bytes 184328 | tf_op jit(solution)/shard_map/ppermute | solution.py:87
  55.7 6.2 %collective-permute-start.13 = (bf16[24,1280]{1,0:T(8,128)(2,1)S(1)}, bf16[24,1280]{1,0:T(8,128)(2,1)S(1)}, u32[]{:S(2)}, u32[]{:S(2)}) collective-permute-start(bf16[24,1280]{1,0:T(8,128)(2,1)S(1)} %add_two.5.own), channel_id=1, source_target_pairs={{0,64},{1,65},{2,66},{3,67},{4,68},{5,69},{6,70},{7,71},{8,72},{9,... | collective-permute-start | bytes 184328 | tf_op jit(solution)/shard_map/ppermute | solution.py:87
  62.6 5.2 %collective-permute-start.14 = (bf16[24,1280]{1,0:T(8,128)(2,1)S(1)}, bf16[24,1280]{1,0:T(8,128)(2,1)S(1)}, u32[]{:S(2)}, u32[]{:S(2)}) collective-permute-start(bf16[24,1280]{1,0:T(8,128)(2,1)S(1)} %get-tuple-element.60.refs_0_), channel_id=1, source_target_pairs={{0,144},{1,145},{2,146},{3,147},{4,148},{5,149},{6,150},{7,151},{8... | collective-permute-start | bytes 184328 | tf_op jit(solution)/shard_map/ppermute | solution.py:87
  67.9 5.3 %collective-permute-start.15 = (bf16[48,1280]{1,0:T(8,128)(2,1)S(1)}, bf16[48,1280]{1,0:T(8,128)(2,1)S(1)}, u32[]{:S(2)}, u32[]{:S(2)}) collective-permute-start(bf16[48,1280]{1,0:T(8,128)(2,1)S(1)} %join.2.refs_0_), channel_id=1, source_target_pairs={{0,4},{1,5},{2,6},{3,7},{4,8},{5,9},{6,10},{7,11},{8,12},{9,13},{1... | collective-permute-start | bytes 368648 | tf_op jit(solution)/shard_map/ppermute | solution.py:87
  69.1 6.8 %collective-permute-start.16 = (bf16[48,1280]{1,0:T(8,128)(2,1)S(1)}, bf16[48,1280]{1,0:T(8,128)(2,1)S(1)}, u32[]{:S(2)}, u32[]{:S(2)}) collective-permute-start(bf16[48,1280]{1,0:T(8,128)(2,1)S(1)} %join.2.refs_0_), channel_id=1, source_target_pairs={{0,8},{1,9},{2,10},{3,11},{4,12},{5,13},{6,14},{7,15},{8,0},{9,1},... | collective-permute-start | bytes 368648 | tf_op jit(solution)/shard_map/ppermute | solution.py:87
  72.1 4.0 %collective-permute-start.17 = (bf16[48,1280]{1,0:T(8,128)(2,1)S(1)}, bf16[48,1280]{1,0:T(8,128)(2,1)S(1)}, u32[]{:S(2)}, u32[]{:S(2)}) collective-permute-start(bf16[48,1280]{1,0:T(8,128)(2,1)S(1)} %join.2.refs_0_), channel_id=1, source_target_pairs={{0,12},{1,13},{2,14},{3,15},{4,0},{5,1},{6,2},{7,3},{8,4},{9,5},{1... | collective-permute-start | bytes 368648 | tf_op jit(solution)/shard_map/ppermute | solution.py:87
  76.1 14.5 %collective-permute-start.19 = (bf16[192,1280]{1,0:T(8,128)(2,1)S(1)}, bf16[192,1280]{1,0:T(8,128)(2,1)S(1)}, u32[]{:S(2)}, u32[]{:S(2)}) collective-permute-start(bf16[192,1280]{1,0:T(8,128)(2,1)S(1)} %join.3.refs_0_), channel_id=1, source_target_pairs={{0,1},{1,2},{2,3},{3,0},{4,5},{5,6},{6,7},{7,4},{8,9},{9,10},{10,1... | collective-permute-start | bytes 1474568 | tf_op jit(solution)/shard_map/ppermute | solution.py:87
  76.2 14.4 %collective-permute-start.21 = (bf16[192,1280]{1,0:T(8,128)(2,1)S(1)}, bf16[192,1280]{1,0:T(8,128)(2,1)S(1)}, u32[]{:S(2)}, u32[]{:S(2)}) collective-permute-start(bf16[192,1280]{1,0:T(8,128)(2,1)S(1)} %join.3.refs_0_), channel_id=1, source_target_pairs={{0,3},{1,0},{2,1},{3,2},{4,7},{5,4},{6,5},{7,6},{8,11},{9,8},{10,9... | collective-permute-start | bytes 1474568 | tf_op jit(solution)/shard_map/ppermute | solution.py:87
  78.9 14.7 %collective-permute-start.23 = (bf16[192,1280]{1,0:T(8,128)(2,1)S(1)}, bf16[192,1280]{1,0:T(8,128)(2,1)S(1)}, u32[]{:S(2)}, u32[]{:S(2)}) collective-permute-start(bf16[192,1280]{1,0:T(8,128)(2,1)S(1)} %join.3.refs_0_), channel_id=1, source_target_pairs={{0,2},{1,3},{2,0},{3,1},{4,6},{5,7},{6,4},{7,5},{8,10},{9,11},{10,... | collective-permute-start | bytes 1474568 | tf_op jit(solution)/shard_map/ppermute | solution.py:87
  79.3 17.2 %collective-permute-start.18 = (bf16[192,1280]{1,0:T(8,128)(2,1)S(1)}, bf16[192,1280]{1,0:T(8,128)(2,1)S(1)}, u32[]{:S(2)}, u32[]{:S(2)}) collective-permute-start(bf16[192,1280]{1,0:T(8,128)(2,1)S(1)} %join.3.refs_0_), channel_id=1, source_target_pairs={{0,32},{1,33},{2,34},{3,35},{4,36},{5,37},{6,38},{7,39},{8,40},{9,... | collective-permute-start | bytes 1474568 | tf_op jit(solution)/shard_map/ppermute | solution.py:87
  90.7 5.9 %collective-permute-start.20 = (bf16[192,1280]{1,0:T(8,128)(2,1)S(1)}, bf16[192,1280]{1,0:T(8,128)(2,1)S(1)}, u32[]{:S(2)}, u32[]{:S(2)}) collective-permute-start(bf16[192,1280]{1,0:T(8,128)(2,1)S(1)} %collective-permute-done.19.refs_1_), channel_id=1, source_target_pairs={{0,32},{1,33},{2,34},{3,35},{4,36},{5,37},{6,38},{7,39},{8,40},{9,... | collective-permute-start | bytes 1474568 | tf_op jit(solution)/shard_map/ppermute | solution.py:87
  90.7 5.9 %collective-permute-start.22 = (bf16[192,1280]{1,0:T(8,128)(2,1)S(1)}, bf16[192,1280]{1,0:T(8,128)(2,1)S(1)}, u32[]{:S(2)}, u32[]{:S(2)}) collective-permute-start(bf16[192,1280]{1,0:T(8,128)(2,1)S(1)} %collective-permute-done.21.refs_2_), channel_id=1, source_target_pairs={{0,32},{1,33},{2,34},{3,35},{4,36},{5,37},{6,38},{7,39},{8,40},{9,... | collective-permute-start | bytes 1474568 | tf_op jit(solution)/shard_map/ppermute | solution.py:87
  93.5 3.0 %collective-permute-start.24 = (bf16[192,1280]{1,0:T(8,128)(2,1)S(1)}, bf16[192,1280]{1,0:T(8,128)(2,1)S(1)}, u32[]{:S(2)}, u32[]{:S(2)}) collective-permute-start(bf16[192,1280]{1,0:T(8,128)(2,1)S(1)} %collective-permute-done.23.refs_3_), channel_id=1, source_target_pairs={{0,32},{1,33},{2,34},{3,35},{4,36},{5,37},{6,38},{7,39},{8,40},{9,... | collective-permute-start | bytes 1474568 | tf_op jit(solution)/shard_map/ppermute | solution.py:87

commit v5 on v4

--- a/solution.py
+++ b/solution.py
@@ -30,7 +30,7 @@
 MIB = 1 << 20
 BF16 = jnp.bfloat16
 F32 = jnp.float32
-TILE = 1280
+TILE = 2560
 READ_TILE = 2560
 AHEAD = 2
 AXES = ("island", "fsdp")
@@ -336,7 +336,7 @@
     )(own, arrived)
 
 
-def outer_kernel(pos, own, three, two, one, unscale, momentum, base, momentum_out, base_out, fragment):
+def outer_kernel(pos, own, two, three, one, unscale, momentum, base, momentum_out, base_out, fragment):
     zlo, core, _, _, _ = coordinates(pos)
     share = own.shape[1] // 2
 
@@ -479,7 +479,7 @@
         pos, keep, arrived, drift, first_moment, second_moment, outer_base, scale_exponents
     )
     coded = add_two(own, send(away, OTHER_CORE))
-    parts = [send(coded, other_zlo(k)) for k in (3, 2, 1)]
+    parts = [send(coded, other_zlo(k)) for k in (2, 3, 1)]
     flat = (first_new.size // BLOCK, BLOCK)
     first_flat, second_flat, *parts = lax.optimization_barrier(
         (first_new.reshape(flat), second_new.reshape(flat), *parts)

time: 98.4 us -> 98.5 us (level)
  starting transfers between devices: 48.4 us -> 52.6 us
  waiting for transfers between devices: 32.7 us -> 28.6 us
    ppermute x25, starting transfers between devices: 48.4 us -> 52.6 us  [send(): return lax.ppermute(value, AXES, pairs)]
    ppermute x25, waiting for transfers between devices: 32.7 us -> 28.6 us  [send(): return lax.ppermute(value, AXES, pairs)]
  transfers between devices with their start and end apart: 25 -> 25, of which waited for: 14 -> 17; matrix products, arithmetic and copies ran while one was open for 2% -> 2% of each run, Pallas kernels for 6% -> 6%
where the time goes in v5:
time: 98.5 us; the launch traced here: 98.4 us
  starting transfers between devices  52.6 us (53%)
  waiting for transfers between devices  28.6 us (29%)
  Pallas kernels  14.6 us (15%)
  local copies, waits for them, and re-layouts  1.66 us (2%)
  between operations  1.01 us (1%)
    ppermute x25, starting transfers between devices, send(): return lax.ppermute(value, AXES, pairs)  52.6 us
    ppermute x25, waiting for transfers between devices, send(): return lax.ppermute(value, AXES, pairs)  28.6 us
    pallas_call x1, Pallas kernels, far_product(): pl.pallas_call(far_kernel, in_specs=[SCALARS, IN_HBM, IN_HBM], out_specs=...  5.28 us
    pallas_call x2, Pallas kernels, product(): pl.pallas_call(product_kernel, in_specs=[IN_VMEM, IN_VMEM], out_specs=[IN...  4 us
    pallas_call x2, Pallas kernels, place(): pl.pallas_call(functools.partial(place_kernel, w), in_specs=[SCALARS] + [...  3.2 us
  transfers between devices with their start and end apart: 25, of which 17 were waited for; matrix products, arithmetic and copies ran while one was open for 2% of the time, Pallas kernels for 6%

profile of v5, /device:TPU:1, one launch (start us, length us, event | category | flops | bytes accessed | tf_op | source)
XLA Modules:
  0.0 98.4 jit_solution(7918316614269567309)
XLA Ops:
  0.6 5.3 %far_product.1 = (bf16[96,2560]{1,0:T(8,128)(2,1)S(1)}, bf16[96,2560]{1,0:T(8,128)(2,1)S(1)}, bf16[192,1024]{1,0:T(8,128)(2,1)S(1)}, bf16[96,1024]{1,0:T(8,128)(2,1)S(1)}, bf16[1,1024,5120]{2,1,0:T(8,128)(2,1)S(1)}) custom-call(s32[1]{0:T(128)} %bitcast.pos, bf16[1,1024,384]{2,1,0:T(8,128)(2,1)} %up_ref.1, bf16[1,1024,5120]{2,1,0:T(8,128)(2,1)} %act_ref.1), custom_call_target="tpu_custom_call" | custom-call | tf_op jit(solution)/shard_map/far_product/pallas_call | solution.py:159
  5.9 2.2 %collective-permute-start.4 = (bf16[96,2560]{1,0:T(8,128)(2,1)S(1)}, bf16[96,2560]{1,0:T(8,128)(2,1)S(1)}, u32[]{:S(2)}, u32[]{:S(2)}) collective-permute-start(bf16[96,2560]{1,0:T(8,128)(2,1)S(1)} %get-tuple-element.41), channel_id=1, source_target_pairs={{0,1},{1,2},{2,3},{3,0},{4,5},{5,6},{6,7},{7,4},{8,9},{9,10},{10,1... | collective-permute-start | bytes 1474568 | tf_op jit(solution)/shard_map/ppermute | solution.py:87
  8.1 1.5 %collective-permute-start = (bf16[96,2560]{1,0:T(8,128)(2,1)S(1)}, bf16[96,2560]{1,0:T(8,128)(2,1)S(1)}, u32[]{:S(2)}, u32[]{:S(2)}) collective-permute-start(bf16[96,2560]{1,0:T(8,128)(2,1)S(1)} %get-tuple-element.37), channel_id=1, source_target_pairs={{0,3},{1,0},{2,1},{3,2},{4,7},{5,4},{6,5},{7,6},{8,11},{9,8},{10,9... | collective-permute-start | bytes 1474568 | tf_op jit(solution)/shard_map/ppermute | solution.py:87
  9.7 2.2 %product.3 = (bf16[96,2560]{1,0:T(8,128)(2,1)S(1)}, bf16[96,2560]{1,0:T(8,128)(2,1)S(1)}, bf16[96,2560]{1,0:T(8,128)(2,1)S(1)}, bf16[96,2560]{1,0:T(8,128)(2,1)S(1)}) custom-call(bf16[192,1024]{1,0:T(8,128)(2,1)S(1)} %get-tuple-element.35.up_rows, bf16[1,1024,5120]{2,1,0:T(8,128)(2,1)S(1)} %get-tuple-element.34.act_ref), custom_call_target="tpu_custom_call" | custom-call | flops 2013265920 | bytes 12845056 | tf_op jit(solution)/shard_map/product/pallas_call | solution.py:196
  11.9 0.0 copy-start.3
  11.9 0.0 copy-start.4
  11.9 0.0 copy-start.5
  11.9 0.0 copy-start
  11.9 0.1 collective-permute-start.2
  12.0 2.7 %collective-permute-start.3 = (bf16[96,2560]{1,0:T(8,128)(2,1)S(1)}, bf16[96,2560]{1,0:T(8,128)(2,1)S(1)}, u32[]{:S(2)}, u32[]{:S(2)}) collective-permute-start(bf16[96,2560]{1,0:T(8,128)(2,1)S(1)} %get-tuple-element.39), channel_id=1, source_target_pairs={{0,3},{1,0},{2,1},{3,2},{4,7},{5,4},{6,5},{7,6},{8,11},{9,8},{10,9... | collective-permute-start | bytes 1474568 | tf_op jit(solution)/shard_map/ppermute | solution.py:87
  14.7 1.4 %collective-permute-done.4.arrived = bf16[96,2560]{1,0:T(8,128)(2,1)S(1)} collective-permute-done((bf16[96,2560]{1,0:T(8,128)(2,1)S(1)}, bf16[96,2560]{1,0:T(8,128)(2,1)S(1)}, u32[]{:S(2)}, u32[]{:S(2)}) %collective-permute-start.4) | collective-permute-done | bytes 491552 | tf_op jit(solution)/shard_map/ppermute | solution.py:87
  16.1 0.1 add_two.4
  16.2 0.1 collective-permute-start.5
  16.3 0.1 add_two.3
  16.4 0.0 copy-start.1
  16.4 2.7 %collective-permute-start.1 = (bf16[96,2560]{1,0:T(8,128)(2,1)S(1)}, bf16[96,2560]{1,0:T(8,128)(2,1)S(1)}, u32[]{:S(2)}, u32[]{:S(2)}) collective-permute-start(bf16[96,2560]{1,0:T(8,128)(2,1)S(1)} %add_two.3), channel_id=1, source_target_pairs={{0,3},{1,0},{2,1},{3,2},{4,7},{5,4},{6,5},{7,6},{8,11},{9,8},{10,9... | collective-permute-start | bytes 1474568 | tf_op jit(solution)/shard_map/ppermute | solution.py:87
  19.2 1.8 %product.2.own = bf16[96,5120]{1,0:T(8,128)(2,1)S(1)} custom-call(bf16[96,1024]{1,0:T(8,128)(2,1)S(1)} %get-tuple-element.33.up_rows, bf16[1,1024,5120]{2,1,0:T(8,128)(2,1)S(1)} %get-tuple-element.34.act_ref), custom_call_target="tpu_custom_call" | custom-call | flops 1006632960 | bytes 11665408 | tf_op jit(solution)/shard_map/product/pallas_call | solution.py:196
  21.0 0.4 collective-permute-done.2.left_two
  21.4 0.0 collective-permute-done.3.right_one
  21.4 5.2 %collective-permute-done.5.right_two = bf16[96,2560]{1,0:T(8,128)(2,1)S(1)} collective-permute-done((bf16[96,2560]{1,0:T(8,128)(2,1)S(1)}, bf16[96,2560]{1,0:T(8,128)(2,1)S(1)}, u32[]{:S(2)}, u32[]{:S(2)}) %collective-permute-start.5) | collective-permute-done | bytes 491552 | tf_op jit(solution)/shard_map/ppermute | solution.py:87
  26.6 0.0 collective-permute-done.1.left_one
  26.6 0.4 add_first.1
  27.0 2.8 %collective-permute-start.6 = (bf16[24,5120]{1,0:T(8,128)(2,1)S(1)}, bf16[24,5120]{1,0:T(8,128)(2,1)S(1)}, u32[]{:S(2)}, u32[]{:S(2)}) collective-permute-start(bf16[24,5120]{1,0:T(8,128)(2,1)S(1)} %get-tuple-element.43), channel_id=1, source_target_pairs={{0,8},{1,9},{2,10},{3,11},{4,12},{5,13},{6,14},{7,15},{8,0},{9,1},... | collective-permute-start | bytes 737288 | tf_op jit(solution)/shard_map/ppermute | solution.py:87
  29.8 0.9 collective-permute-start.7
  30.7 0.6 collective-permute-start.8
  31.3 2.3 %collective-permute-done.6.one = bf16[24,5120]{1,0:T(8,128)(2,1)S(1)} collective-permute-done((bf16[24,5120]{1,0:T(8,128)(2,1)S(1)}, bf16[24,5120]{1,0:T(8,128)(2,1)S(1)}, u32[]{:S(2)}, u32[]{:S(2)}) %collective-permute-start.6) | collective-permute-done | bytes 245792 | tf_op jit(solution)/shard_map/ppermute | solution.py:87
  33.6 3.0 %collective-permute-done.7.two = bf16[24,5120]{1,0:T(8,128)(2,1)S(1)} collective-permute-done((bf16[24,5120]{1,0:T(8,128)(2,1)S(1)}, bf16[24,5120]{1,0:T(8,128)(2,1)S(1)}, u32[]{:S(2)}, u32[]{:S(2)}) %collective-permute-start.7) | collective-permute-done | bytes 245792 | tf_op jit(solution)/shard_map/ppermute | solution.py:87
  36.7 0.6 collective-permute-done.8.three
  37.2 0.1 add_second.1
  37.4 6.7 %collective-permute-start.9 = (bf16[24,2560]{1,0:T(8,128)(2,1)S(1)}, bf16[24,2560]{1,0:T(8,128)(2,1)S(1)}, u32[]{:S(2)}, u32[]{:S(2)}) collective-permute-start(bf16[24,2560]{1,0:T(8,128)(2,1)S(1)} %get-tuple-element.47), channel_id=1, source_target_pairs={{0,16},{1,17},{2,18},{3,19},{4,20},{5,21},{6,22},{7,23},{8,24},{9,... | collective-permute-start | bytes 368648 | tf_op jit(solution)/shard_map/ppermute | solution.py:87
  44.1 0.1 copy.22.drift
  44.1 0.1 copy.23.first
  44.2 0.1 copy.24.second
  44.3 2.2 %collective-permute-done.9.arrived = bf16[24,2560]{1,0:T(8,128)(2,1)S(1)} collective-permute-done((bf16[24,2560]{1,0:T(8,128)(2,1)S(1)}, bf16[24,2560]{1,0:T(8,128)(2,1)S(1)}, u32[]{:S(2)}, u32[]{:S(2)}) %collective-permute-start.9) | collective-permute-done | bytes 122912 | tf_op jit(solution)/shard_map/ppermute | solution.py:87
  46.5 0.6 inner_step.1
  47.1 5.4 %collective-permute-start.10 = (bf16[24,1280]{1,0:T(8,128)(2,1)S(1)}, bf16[24,1280]{1,0:T(8,128)(2,1)S(1)}, u32[]{:S(2)}, u32[]{:S(2)}) collective-permute-start(bf16[24,1280]{1,0:T(8,128)(2,1)S(1)} %get-tuple-element.51), channel_id=1, source_target_pairs={{0,32},{1,33},{2,34},{3,35},{4,36},{5,37},{6,38},{7,39},{8,40},{9,... | collective-permute-start | bytes 184328 | tf_op jit(solution)/shard_map/ppermute | solution.py:87
  52.5 0.9 collective-permute-done.10.arrived
  53.4 1.5 %collective-permute-start.11 = (bf16[24,1280]{1,0:T(8,128)(2,1)S(1)}, bf16[24,1280]{1,0:T(8,128)(2,1)S(1)}, u32[]{:S(2)}, u32[]{:S(2)}) collective-permute-start(bf16[24,1280]{1,0:T(8,128)(2,1)S(1)} %add_two.5.own), channel_id=1, source_target_pairs={{0,128},{1,129},{2,130},{3,131},{4,132},{5,133},{6,134},{7,135},{8... | collective-permute-start | bytes 184328 | tf_op jit(solution)/shard_map/ppermute | solution.py:87
  54.9 1.3 %collective-permute-start.12 = (bf16[24,1280]{1,0:T(8,128)(2,1)S(1)}, bf16[24,1280]{1,0:T(8,128)(2,1)S(1)}, u32[]{:S(2)}, u32[]{:S(2)}) collective-permute-start(bf16[24,1280]{1,0:T(8,128)(2,1)S(1)} %add_two.5.own), channel_id=1, source_target_pairs={{0,192},{1,193},{2,194},{3,195},{4,196},{5,197},{6,198},{7,199},{8... | collective-permute-start | bytes 184328 | tf_op jit(solution)/shard_map/ppermute | solution.py:87
  56.2 0.7 reshape.26
  56.9 0.7 reshape.27
  57.7 1.6 %collective-permute-done.11.two = bf16[24,1280]{1,0:T(8,128)(2,1)S(1)} collective-permute-done((bf16[24,1280]{1,0:T(8,128)(2,1)S(1)}, bf16[24,1280]{1,0:T(8,128)(2,1)S(1)}, u32[]{:S(2)}, u32[]{:S(2)}) %collective-permute-start.11) | collective-permute-done | bytes 61472 | tf_op jit(solution)/shard_map/ppermute | solution.py:87
  59.3 0.6 collective-permute-done.12.three
  59.9 2.3 %collective-permute-done.13.one = bf16[24,1280]{1,0:T(8,128)(2,1)S(1)} collective-permute-done((bf16[24,1280]{1,0:T(8,128)(2,1)S(1)}, bf16[24,1280]{1,0:T(8,128)(2,1)S(1)}, u32[]{:S(2)}, u32[]{:S(2)}) %collective-permute-start.13) | collective-permute-done | bytes 61472 | tf_op jit(solution)/shard_map/ppermute | solution.py:87
  62.2 0.7 outer_step.1
  62.9 2.8 %collective-permute-start.14 = (bf16[24,1280]{1,0:T(8,128)(2,1)S(1)}, bf16[24,1280]{1,0:T(8,128)(2,1)S(1)}, u32[]{:S(2)}, u32[]{:S(2)}) collective-permute-start(bf16[24,1280]{1,0:T(8,128)(2,1)S(1)} %get-tuple-element.60.refs_0_), channel_id=1, source_target_pairs={{0,144},{1,145},{2,146},{3,147},{4,148},{5,149},{6,150},{7,151},{8... | collective-permute-start | bytes 184328 | tf_op jit(solution)/shard_map/ppermute | solution.py:87
  65.7 2.4 %collective-permute-done.14.refs_1_ = bf16[24,1280]{1,0:T(8,128)(2,1)S(1)} collective-permute-done((bf16[24,1280]{1,0:T(8,128)(2,1)S(1)}, bf16[24,1280]{1,0:T(8,128)(2,1)S(1)}, u32[]{:S(2)}, u32[]{:S(2)}) %collective-permute-start.14) | collective-permute-done | bytes 61472 | tf_op jit(solution)/shard_map/ppermute | solution.py:87
  68.1 1.3 %collective-permute-start.15 = (bf16[48,1280]{1,0:T(8,128)(2,1)S(1)}, bf16[48,1280]{1,0:T(8,128)(2,1)S(1)}, u32[]{:S(2)}, u32[]{:S(2)}) collective-permute-start(bf16[48,1280]{1,0:T(8,128)(2,1)S(1)} %join.2.refs_0_), channel_id=1, source_target_pairs={{0,4},{1,5},{2,6},{3,7},{4,8},{5,9},{6,10},{7,11},{8,12},{9,13},{1... | collective-permute-start | bytes 368648 | tf_op jit(solution)/shard_map/ppermute | solution.py:87
  69.4 2.1 %collective-permute-start.16 = (bf16[48,1280]{1,0:T(8,128)(2,1)S(1)}, bf16[48,1280]{1,0:T(8,128)(2,1)S(1)}, u32[]{:S(2)}, u32[]{:S(2)}) collective-permute-start(bf16[48,1280]{1,0:T(8,128)(2,1)S(1)} %join.2.refs_0_), channel_id=1, source_target_pairs={{0,8},{1,9},{2,10},{3,11},{4,12},{5,13},{6,14},{7,15},{8,0},{9,1},... | collective-permute-start | bytes 368648 | tf_op jit(solution)/shard_map/ppermute | solution.py:87
  71.5 1.2 %collective-permute-start.17 = (bf16[48,1280]{1,0:T(8,128)(2,1)S(1)}, bf16[48,1280]{1,0:T(8,128)(2,1)S(1)}, u32[]{:S(2)}, u32[]{:S(2)}) collective-permute-start(bf16[48,1280]{1,0:T(8,128)(2,1)S(1)} %join.2.refs_0_), channel_id=1, source_target_pairs={{0,12},{1,13},{2,14},{3,15},{4,0},{5,1},{6,2},{7,3},{8,4},{9,5},{1... | collective-permute-start | bytes 368648 | tf_op jit(solution)/shard_map/ppermute | solution.py:87
  72.7 0.5 collective-permute-done.15.refs_1_
  73.1 1.9 %collective-permute-done.16.refs_2_ = bf16[48,1280]{1,0:T(8,128)(2,1)S(1)} collective-permute-done((bf16[48,1280]{1,0:T(8,128)(2,1)S(1)}, bf16[48,1280]{1,0:T(8,128)(2,1)S(1)}, u32[]{:S(2)}, u32[]{:S(2)}) %collective-permute-start.16) | collective-permute-done | bytes 122912 | tf_op jit(solution)/shard_map/ppermute | solution.py:87
  75.0 0.4 collective-permute-done.17.refs_3_
  75.5 1.0 collective-permute-start.19
  76.5 1.8 %collective-permute-start.21 = (bf16[192,1280]{1,0:T(8,128)(2,1)S(1)}, bf16[192,1280]{1,0:T(8,128)(2,1)S(1)}, u32[]{:S(2)}, u32[]{:S(2)}) collective-permute-start(bf16[192,1280]{1,0:T(8,128)(2,1)S(1)} %join.3.refs_0_), channel_id=1, source_target_pairs={{0,3},{1,0},{2,1},{3,2},{4,7},{5,4},{6,5},{7,6},{8,11},{9,8},{10,9... | collective-permute-start | bytes 1474568 | tf_op jit(solution)/shard_map/ppermute | solution.py:87
  78.3 1.3 %collective-permute-start.23 = (bf16[192,1280]{1,0:T(8,128)(2,1)S(1)}, bf16[192,1280]{1,0:T(8,128)(2,1)S(1)}, u32[]{:S(2)}, u32[]{:S(2)}) collective-permute-start(bf16[192,1280]{1,0:T(8,128)(2,1)S(1)} %join.3.refs_0_), channel_id=1, source_target_pairs={{0,2},{1,3},{2,0},{3,1},{4,6},{5,7},{6,4},{7,5},{8,10},{9,11},{10,... | collective-permute-start | bytes 1474568 | tf_op jit(solution)/shard_map/ppermute | solution.py:87
  79.5 3.5 %collective-permute-start.18 = (bf16[192,1280]{1,0:T(8,128)(2,1)S(1)}, bf16[192,1280]{1,0:T(8,128)(2,1)S(1)}, u32[]{:S(2)}, u32[]{:S(2)}) collective-permute-start(bf16[192,1280]{1,0:T(8,128)(2,1)S(1)} %join.3.refs_0_), channel_id=1, source_target_pairs={{0,32},{1,33},{2,34},{3,35},{4,36},{5,37},{6,38},{7,39},{8,40},{9,... | collective-permute-start | bytes 1474568 | tf_op jit(solution)/shard_map/ppermute | solution.py:87
  83.0 1.8 %collective-permute-done.19.refs_1_ = bf16[192,1280]{1,0:T(8,128)(2,1)S(1)} collective-permute-done((bf16[192,1280]{1,0:T(8,128)(2,1)S(1)}, bf16[192,1280]{1,0:T(8,128)(2,1)S(1)}, u32[]{:S(2)}, u32[]{:S(2)}) %collective-permute-start.19) | collective-permute-done | bytes 491552 | tf_op jit(solution)/shard_map/ppermute | solution.py:87
  84.8 3.6 %collective-permute-start.20 = (bf16[192,1280]{1,0:T(8,128)(2,1)S(1)}, bf16[192,1280]{1,0:T(8,128)(2,1)S(1)}, u32[]{:S(2)}, u32[]{:S(2)}) collective-permute-start(bf16[192,1280]{1,0:T(8,128)(2,1)S(1)} %collective-permute-done.19.refs_1_), channel_id=1, source_target_pairs={{0,32},{1,33},{2,34},{3,35},{4,36},{5,37},{6,38},{7,39},{8,40},{9,... | collective-permute-start | bytes 1474568 | tf_op jit(solution)/shard_map/ppermute | solution.py:87
  88.4 0.9 collective-permute-done.21.refs_2_
  89.3 3.9 %collective-permute-start.22 = (bf16[192,1280]{1,0:T(8,128)(2,1)S(1)}, bf16[192,1280]{1,0:T(8,128)(2,1)S(1)}, u32[]{:S(2)}, u32[]{:S(2)}) collective-permute-start(bf16[192,1280]{1,0:T(8,128)(2,1)S(1)} %collective-permute-done.21.refs_2_), channel_id=1, source_target_pairs={{0,32},{1,33},{2,34},{3,35},{4,36},{5,37},{6,38},{7,39},{8,40},{9,... | collective-permute-start | bytes 1474568 | tf_op jit(solution)/shard_map/ppermute | solution.py:87
  93.3 1.7 %collective-permute-start.24 = (bf16[192,1280]{1,0:T(8,128)(2,1)S(1)}, bf16[192,1280]{1,0:T(8,128)(2,1)S(1)}, u32[]{:S(2)}, u32[]{:S(2)}) collective-permute-start(bf16[192,1280]{1,0:T(8,128)(2,1)S(1)} %collective-permute-done.23.refs_3_), channel_id=1, source_target_pairs={{0,32},{1,33},{2,34},{3,35},{4,36},{5,37},{6,38},{7,39},{8,40},{9,... | collective-permute-start | bytes 1474568 | tf_op jit(solution)/shard_map/ppermute | solution.py:87
  95.0 1.6 %place.2.refs_4_ = bf16[384,5120]{1,0:T(8,128)(2,1)} custom-call(s32[1]{0:T(128)} %bitcast.pos, bf16[192,1280]{1,0:T(8,128)(2,1)S(1)} %join.3.refs_0_, bf16[192,1280]{1,0:T(8,128)(2,1)S(1)} %collective-permute-done.19.refs_1_, bf16[192,1280]{1,0:T(8,128)(2,1)S(1)} %collective-permute-done.21.refs_2_, bf16[192,1280]{1,0:T(8,128)(2,1)S(1)} %collective-permute-done.23.refs_3_), custom_call_target="tpu_custom_call" | custom-call | tf_op jit(solution)/shard_map/place/pallas_call | solution.py:450
  96.6 1.6 %place.3 = bf16[384,5120]{1,0:T(8,128)(2,1)} custom-call(s32[1]{0:T(128)} %bitcast.pos, bf16[192,1280]{1,0:T(8,128)(2,1)S(1)} %collective-permute-done.18.refs_0_, bf16[192,1280]{1,0:T(8,128)(2,1)S(1)} %collective-permute-done.20.refs_1_, bf16[192,1280]{1,0:T(8,128)(2,1)S(1)} %collective-permute-done.22.refs_2_, ...), custom_call_target="tpu_custom_call", output_to_operand_aliasing={{}: (5, {})} | custom-call | tf_op jit(solution)/shard_map/place/pallas_call | solution.py:450
  (17 shorter events, 0.1 us)
Async XLA Ops:
  5.9 10.2 %collective-permute-start.4 = (bf16[96,2560]{1,0:T(8,128)(2,1)S(1)}, bf16[96,2560]{1,0:T(8,128)(2,1)S(1)}, u32[]{:S(2)}, u32[]{:S(2)}) collective-permute-start(bf16[96,2560]{1,0:T(8,128)(2,1)S(1)} %get-tuple-element.41), channel_id=1, source_target_pairs={{0,1},{1,2},{2,3},{3,0},{4,5},{5,6},{6,7},{7,4},{8,9},{9,10},{10,1... | collective-permute-start | bytes 1474568 | tf_op jit(solution)/shard_map/ppermute | solution.py:87
  8.1 8.2 %collective-permute-start = (bf16[96,2560]{1,0:T(8,128)(2,1)S(1)}, bf16[96,2560]{1,0:T(8,128)(2,1)S(1)}, u32[]{:S(2)}, u32[]{:S(2)}) collective-permute-start(bf16[96,2560]{1,0:T(8,128)(2,1)S(1)} %get-tuple-element.37), channel_id=1, source_target_pairs={{0,3},{1,0},{2,1},{3,2},{4,7},{5,4},{6,5},{7,6},{8,11},{9,8},{10,9... | collective-permute-start | bytes 1474568 | tf_op jit(solution)/shard_map/ppermute | solution.py:87
  11.9 32.2 %copy-start.3 = (f32[1,12,5120]{2,0,1:T(1,128)S(1)}, f32[1,12,5120]{2,0,1:T(1,128)}, u32[]{:S(2)}) copy-start(f32[1,12,5120]{2,0,1:T(1,128)} %param.10) | copy-start | bytes 737284
  11.9 32.2 %copy-start.4 = (f32[1,12,5120]{2,0,1:T(1,128)S(1)}, f32[1,12,5120]{2,0,1:T(1,128)}, u32[]{:S(2)}) copy-start(f32[1,12,5120]{2,0,1:T(1,128)} %param.11) | copy-start | bytes 737284
  11.9 32.3 %copy-start.5 = (f32[1,12,5120]{2,0,1:T(1,128)S(1)}, f32[1,12,5120]{2,0,1:T(1,128)}, u32[]{:S(2)}) copy-start(f32[1,12,5120]{2,0,1:T(1,128)} %param.12) | copy-start | bytes 737284
  11.9 34.5 %copy-start = (f32[12,5120]{1,0:T(8,128)S(1)}, f32[12,5120]{1,0:T(8,128)}, u32[]{:S(2)}) copy-start(f32[12,5120]{1,0:T(8,128)} %base.3) | copy-start | bytes 737284
  11.9 34.5 %copy-start.2 = (s32[12,40]{1,0:T(8,128)S(1)}, s32[12,40]{1,0:T(8,128)}, u32[]{:S(2)}) copy-start(s32[12,40]{1,0:T(8,128)} %exponents.1) | copy-start | bytes 5764
  11.9 9.4 %collective-permute-start.2 = (bf16[96,2560]{1,0:T(8,128)(2,1)S(1)}, bf16[96,2560]{1,0:T(8,128)(2,1)S(1)}, u32[]{:S(2)}, u32[]{:S(2)}) collective-permute-start(bf16[96,2560]{1,0:T(8,128)(2,1)S(1)} %get-tuple-element.38), channel_id=1, source_target_pairs={{0,1},{1,2},{2,3},{3,0},{4,5},{5,6},{6,7},{7,4},{8,9},{9,10},{10,1... | collective-permute-start | bytes 1474568 | tf_op jit(solution)/shard_map/ppermute | solution.py:87
  12.0 9.3 %collective-permute-start.3 = (bf16[96,2560]{1,0:T(8,128)(2,1)S(1)}, bf16[96,2560]{1,0:T(8,128)(2,1)S(1)}, u32[]{:S(2)}, u32[]{:S(2)}) collective-permute-start(bf16[96,2560]{1,0:T(8,128)(2,1)S(1)} %get-tuple-element.39), channel_id=1, source_target_pairs={{0,3},{1,0},{2,1},{3,2},{4,7},{5,4},{6,5},{7,6},{8,11},{9,8},{10,9... | collective-permute-start | bytes 1474568 | tf_op jit(solution)/shard_map/ppermute | solution.py:87
  16.2 10.4 %collective-permute-start.5 = (bf16[96,2560]{1,0:T(8,128)(2,1)S(1)}, bf16[96,2560]{1,0:T(8,128)(2,1)S(1)}, u32[]{:S(2)}, u32[]{:S(2)}) collective-permute-start(bf16[96,2560]{1,0:T(8,128)(2,1)S(1)} %add_two.4), channel_id=1, source_target_pairs={{0,1},{1,2},{2,3},{3,0},{4,5},{5,6},{6,7},{7,4},{8,9},{9,10},{10,1... | collective-permute-start | bytes 1474568 | tf_op jit(solution)/shard_map/ppermute | solution.py:87
  16.4 45.7 %copy-start.1 = (f32[12,5120]{1,0:T(8,128)S(1)}, f32[12,5120]{1,0:T(8,128)}, u32[]{:S(2)}) copy-start(f32[12,5120]{1,0:T(8,128)} %momentum.1) | copy-start | bytes 737284
  16.4 10.2 %collective-permute-start.1 = (bf16[96,2560]{1,0:T(8,128)(2,1)S(1)}, bf16[96,2560]{1,0:T(8,128)(2,1)S(1)}, u32[]{:S(2)}, u32[]{:S(2)}) collective-permute-start(bf16[96,2560]{1,0:T(8,128)(2,1)S(1)} %add_two.3), channel_id=1, source_target_pairs={{0,3},{1,0},{2,1},{3,2},{4,7},{5,4},{6,5},{7,6},{8,11},{9,8},{10,9... | collective-permute-start | bytes 1474568 | tf_op jit(solution)/shard_map/ppermute | solution.py:87
  27.0 6.6 %collective-permute-start.6 = (bf16[24,5120]{1,0:T(8,128)(2,1)S(1)}, bf16[24,5120]{1,0:T(8,128)(2,1)S(1)}, u32[]{:S(2)}, u32[]{:S(2)}) collective-permute-start(bf16[24,5120]{1,0:T(8,128)(2,1)S(1)} %get-tuple-element.43), channel_id=1, source_target_pairs={{0,8},{1,9},{2,10},{3,11},{4,12},{5,13},{6,14},{7,15},{8,0},{9,1},... | collective-permute-start | bytes 737288 | tf_op jit(solution)/shard_map/ppermute | solution.py:87
  29.8 6.9 %collective-permute-start.7 = (bf16[24,5120]{1,0:T(8,128)(2,1)S(1)}, bf16[24,5120]{1,0:T(8,128)(2,1)S(1)}, u32[]{:S(2)}, u32[]{:S(2)}) collective-permute-start(bf16[24,5120]{1,0:T(8,128)(2,1)S(1)} %get-tuple-element.44), channel_id=1, source_target_pairs={{0,12},{1,13},{2,14},{3,15},{4,0},{5,1},{6,2},{7,3},{8,4},{9,5},{1... | collective-permute-start | bytes 737288 | tf_op jit(solution)/shard_map/ppermute | solution.py:87
  30.7 6.6 %collective-permute-start.8 = (bf16[24,5120]{1,0:T(8,128)(2,1)S(1)}, bf16[24,5120]{1,0:T(8,128)(2,1)S(1)}, u32[]{:S(2)}, u32[]{:S(2)}) collective-permute-start(bf16[24,5120]{1,0:T(8,128)(2,1)S(1)} %get-tuple-element.45), channel_id=1, source_target_pairs={{0,4},{1,5},{2,6},{3,7},{4,8},{5,9},{6,10},{7,11},{8,12},{9,13},{1... | collective-permute-start | bytes 737288 | tf_op jit(solution)/shard_map/ppermute | solution.py:87
  37.4 9.1 %collective-permute-start.9 = (bf16[24,2560]{1,0:T(8,128)(2,1)S(1)}, bf16[24,2560]{1,0:T(8,128)(2,1)S(1)}, u32[]{:S(2)}, u32[]{:S(2)}) collective-permute-start(bf16[24,2560]{1,0:T(8,128)(2,1)S(1)} %get-tuple-element.47), channel_id=1, source_target_pairs={{0,16},{1,17},{2,18},{3,19},{4,20},{5,21},{6,22},{7,23},{8,24},{9,... | collective-permute-start | bytes 368648 | tf_op jit(solution)/shard_map/ppermute | solution.py:87
  47.1 6.3 %collective-permute-start.10 = (bf16[24,1280]{1,0:T(8,128)(2,1)S(1)}, bf16[24,1280]{1,0:T(8,128)(2,1)S(1)}, u32[]{:S(2)}, u32[]{:S(2)}) collective-permute-start(bf16[24,1280]{1,0:T(8,128)(2,1)S(1)} %get-tuple-element.51), channel_id=1, source_target_pairs={{0,32},{1,33},{2,34},{3,35},{4,36},{5,37},{6,38},{7,39},{8,40},{9,... | collective-permute-start | bytes 184328 | tf_op jit(solution)/shard_map/ppermute | solution.py:87
  53.4 5.9 %collective-permute-start.11 = (bf16[24,1280]{1,0:T(8,128)(2,1)S(1)}, bf16[24,1280]{1,0:T(8,128)(2,1)S(1)}, u32[]{:S(2)}, u32[]{:S(2)}) collective-permute-start(bf16[24,1280]{1,0:T(8,128)(2,1)S(1)} %add_two.5.own), channel_id=1, source_target_pairs={{0,128},{1,129},{2,130},{3,131},{4,132},{5,133},{6,134},{7,135},{8... | collective-permute-start | bytes 184328 | tf_op jit(solution)/shard_map/ppermute | solution.py:87
  54.9 5.0 %collective-permute-start.12 = (bf16[24,1280]{1,0:T(8,128)(2,1)S(1)}, bf16[24,1280]{1,0:T(8,128)(2,1)S(1)}, u32[]{:S(2)}, u32[]{:S(2)}) collective-permute-start(bf16[24,1280]{1,0:T(8,128)(2,1)S(1)} %add_two.5.own), channel_id=1, source_target_pairs={{0,192},{1,193},{2,194},{3,195},{4,196},{5,197},{6,198},{7,199},{8... | collective-permute-start | bytes 184328 | tf_op jit(solution)/shard_map/ppermute | solution.py:87
  56.2 6.0 %collective-permute-start.13 = (bf16[24,1280]{1,0:T(8,128)(2,1)S(1)}, bf16[24,1280]{1,0:T(8,128)(2,1)S(1)}, u32[]{:S(2)}, u32[]{:S(2)}) collective-permute-start(bf16[24,1280]{1,0:T(8,128)(2,1)S(1)} %add_two.5.own), channel_id=1, source_target_pairs={{0,64},{1,65},{2,66},{3,67},{4,68},{5,69},{6,70},{7,71},{8,72},{9,... | collective-permute-start | bytes 184328 | tf_op jit(solution)/shard_map/ppermute | solution.py:87
  62.9 5.2 %collective-permute-start.14 = (bf16[24,1280]{1,0:T(8,128)(2,1)S(1)}, bf16[24,1280]{1,0:T(8,128)(2,1)S(1)}, u32[]{:S(2)}, u32[]{:S(2)}) collective-permute-start(bf16[24,1280]{1,0:T(8,128)(2,1)S(1)} %get-tuple-element.60.refs_0_), channel_id=1, source_target_pairs={{0,144},{1,145},{2,146},{3,147},{4,148},{5,149},{6,150},{7,151},{8... | collective-permute-start | bytes 184328 | tf_op jit(solution)/shard_map/ppermute | solution.py:87
  68.1 5.0 %collective-permute-start.15 = (bf16[48,1280]{1,0:T(8,128)(2,1)S(1)}, bf16[48,1280]{1,0:T(8,128)(2,1)S(1)}, u32[]{:S(2)}, u32[]{:S(2)}) collective-permute-start(bf16[48,1280]{1,0:T(8,128)(2,1)S(1)} %join.2.refs_0_), channel_id=1, source_target_pairs={{0,4},{1,5},{2,6},{3,7},{4,8},{5,9},{6,10},{7,11},{8,12},{9,13},{1... | collective-permute-start | bytes 368648 | tf_op jit(solution)/shard_map/ppermute | solution.py:87
  69.4 5.7 %collective-permute-start.16 = (bf16[48,1280]{1,0:T(8,128)(2,1)S(1)}, bf16[48,1280]{1,0:T(8,128)(2,1)S(1)}, u32[]{:S(2)}, u32[]{:S(2)}) collective-permute-start(bf16[48,1280]{1,0:T(8,128)(2,1)S(1)} %join.2.refs_0_), channel_id=1, source_target_pairs={{0,8},{1,9},{2,10},{3,11},{4,12},{5,13},{6,14},{7,15},{8,0},{9,1},... | collective-permute-start | bytes 368648 | tf_op jit(solution)/shard_map/ppermute | solution.py:87
  71.5 4.0 %collective-permute-start.17 = (bf16[48,1280]{1,0:T(8,128)(2,1)S(1)}, bf16[48,1280]{1,0:T(8,128)(2,1)S(1)}, u32[]{:S(2)}, u32[]{:S(2)}) collective-permute-start(bf16[48,1280]{1,0:T(8,128)(2,1)S(1)} %join.2.refs_0_), channel_id=1, source_target_pairs={{0,12},{1,13},{2,14},{3,15},{4,0},{5,1},{6,2},{7,3},{8,4},{9,5},{1... | collective-permute-start | bytes 368648 | tf_op jit(solution)/shard_map/ppermute | solution.py:87
  75.5 9.3 %collective-permute-start.19 = (bf16[192,1280]{1,0:T(8,128)(2,1)S(1)}, bf16[192,1280]{1,0:T(8,128)(2,1)S(1)}, u32[]{:S(2)}, u32[]{:S(2)}) collective-permute-start(bf16[192,1280]{1,0:T(8,128)(2,1)S(1)} %join.3.refs_0_), channel_id=1, source_target_pairs={{0,1},{1,2},{2,3},{3,0},{4,5},{5,6},{6,7},{7,4},{8,9},{9,10},{10,1... | collective-permute-start | bytes 1474568 | tf_op jit(solution)/shard_map/ppermute | solution.py:87
  76.5 12.8 %collective-permute-start.21 = (bf16[192,1280]{1,0:T(8,128)(2,1)S(1)}, bf16[192,1280]{1,0:T(8,128)(2,1)S(1)}, u32[]{:S(2)}, u32[]{:S(2)}) collective-permute-start(bf16[192,1280]{1,0:T(8,128)(2,1)S(1)} %join.3.refs_0_), channel_id=1, source_target_pairs={{0,3},{1,0},{2,1},{3,2},{4,7},{5,4},{6,5},{7,6},{8,11},{9,8},{10,9... | collective-permute-start | bytes 1474568 | tf_op jit(solution)/shard_map/ppermute | solution.py:87
  78.3 15.0 %collective-permute-start.23 = (bf16[192,1280]{1,0:T(8,128)(2,1)S(1)}, bf16[192,1280]{1,0:T(8,128)(2,1)S(1)}, u32[]{:S(2)}, u32[]{:S(2)}) collective-permute-start(bf16[192,1280]{1,0:T(8,128)(2,1)S(1)} %join.3.refs_0_), channel_id=1, source_target_pairs={{0,2},{1,3},{2,0},{3,1},{4,6},{5,7},{6,4},{7,5},{8,10},{9,11},{10,... | collective-permute-start | bytes 1474568 | tf_op jit(solution)/shard_map/ppermute | solution.py:87
  79.5 17.0 %collective-permute-start.18 = (bf16[192,1280]{1,0:T(8,128)(2,1)S(1)}, bf16[192,1280]{1,0:T(8,128)(2,1)S(1)}, u32[]{:S(2)}, u32[]{:S(2)}) collective-permute-start(bf16[192,1280]{1,0:T(8,128)(2,1)S(1)} %join.3.refs_0_), channel_id=1, source_target_pairs={{0,32},{1,33},{2,34},{3,35},{4,36},{5,37},{6,38},{7,39},{8,40},{9,... | collective-permute-start | bytes 1474568 | tf_op jit(solution)/shard_map/ppermute | solution.py:87
  84.8 11.8 %collective-permute-start.20 = (bf16[192,1280]{1,0:T(8,128)(2,1)S(1)}, bf16[192,1280]{1,0:T(8,128)(2,1)S(1)}, u32[]{:S(2)}, u32[]{:S(2)}) collective-permute-start(bf16[192,1280]{1,0:T(8,128)(2,1)S(1)} %collective-permute-done.19.refs_1_), channel_id=1, source_target_pairs={{0,32},{1,33},{2,34},{3,35},{4,36},{5,37},{6,38},{7,39},{8,40},{9,... | collective-permute-start | bytes 1474568 | tf_op jit(solution)/shard_map/ppermute | solution.py:87
  89.3 7.3 %collective-permute-start.22 = (bf16[192,1280]{1,0:T(8,128)(2,1)S(1)}, bf16[192,1280]{1,0:T(8,128)(2,1)S(1)}, u32[]{:S(2)}, u32[]{:S(2)}) collective-permute-start(bf16[192,1280]{1,0:T(8,128)(2,1)S(1)} %collective-permute-done.21.refs_2_), channel_id=1, source_target_pairs={{0,32},{1,33},{2,34},{3,35},{4,36},{5,37},{6,38},{7,39},{8,40},{9,... | collective-permute-start | bytes 1474568 | tf_op jit(solution)/shard_map/ppermute | solution.py:87
  93.3 3.3 %collective-permute-start.24 = (bf16[192,1280]{1,0:T(8,128)(2,1)S(1)}, bf16[192,1280]{1,0:T(8,128)(2,1)S(1)}, u32[]{:S(2)}, u32[]{:S(2)}) collective-permute-start(bf16[192,1280]{1,0:T(8,128)(2,1)S(1)} %collective-permute-done.23.refs_3_), channel_id=1, source_target_pairs={{0,32},{1,33},{2,34},{3,35},{4,36},{5,37},{6,38},{7,39},{8,40},{9,... | collective-permute-start | bytes 1474568 | tf_op jit(solution)/shard_map/ppermute | solution.py:87
